TPU v7x, 256 devices: a whole 4x4x8 slice. The times are simulated.
256 devices in a mesh: ma: 2 (over core), ta: 128 (over y, x, z).
Axes of the slice: x: 4, y: 4, z: 8, core: 2. Of those that a mesh axis runs over, the one named last changes fastest.
Arguments:
- thickness: float32 [512, 128, 128], P('ta'), may hold values from 0.5 to 2
- driving: float32 [2, 512, 128, 128], P(None, 'ta'), may hold values from -6 to 6
- friction: float32 [1024, 128, 128], P(('ma', 'ta')), parts along dimension 0, may hold values from 0.3 to 3
- velocity_start: float32 [2, 512, 128, 128], P(None, 'ta'), may hold values from -6 to 6
- row_lengths: int32 [22], replicated, may hold values from 1 to 48, 512 in all
Outputs:
- velocity: float32 [2, 1024, 128, 128], P(None, ('ma', 'ta')), parts along dimension 1
- thickness_next: float32 [1024, 128, 128], P(('ma', 'ta')), parts along dimension 0
There are 2 independent parts, one for each index of `ma`. A program takes and returns all parts, laid end to end along the dimension named above; an argument that names none is the same for every part. Nothing has to cross between parts.
Inputs may be any that keep to these rules, and one draw needn't show every extreme that they name: Tile row r is ice in its last row_lengths[r] of 48 tile columns; the lengths sum to 512, and at least one row is ice in all 48 columns.
All inputs are finite; a program needn't handle non-finite values.
Results may differ from a plain program's by a relative error of at most 0.0003.
Values sent between devices are 32-bit elements; how exact they have to be, the bound alone decides.
No kernel may reach another device: no remote copies, remote signals or barrier semaphores. Data moves between devices by JAX's collectives and lax.ppermute only.
A program may use at most 128 MiB of HBM per device.

v0:
```python
import functools

import jax
import jax.numpy as jnp
from jax import lax
from jax.experimental import pallas as pl
from jax.experimental.pallas import tpu as pltpu
from jax.sharding import PartitionSpec as P


GC = 48
SWEEPS = 4
STRAIN_EPSILON = 0.01
TIME_STEP = 0.1

TS = 128
LANES = 128
TPD = 4
SECTION = 8
STRIP = 6 * SECTION
TOP = 16
ROWS = TS + 2 * TOP
MARGIN = 16
STRIDE = 3
HOPS = 5
MAIN_BLOCKS = 2 * TPD
PACK = (MAIN_BLOCKS + 2) * STRIP
FULL_PACK = PACK + TS
VMEM_LIMIT = 40 * 1024 * 1024


def cyclic_shift(value, steps):
    count = lax.axis_size("ta")
    return lax.ppermute(value, "ta", [(i, (i + steps) % count) for i in range(count)])


def fill_row_ends(len_ref, ends_ref):
    total = jnp.int32(0)
    ends = []
    for r in range(len_ref.shape[0]):
        total = total + len_ref[r]
        ends_ref[r] = total
        ends.append(total)
    return ends


class Tile:
    def __init__(self, len_ref, ends_ref, ends, slot, slots):
        rows = len_ref.shape[0]
        row = jnp.int32(0)
        for end in ends:
            row = row + jnp.where(end <= slot, 1, 0)
        self.slot = slot
        self.real = (slot >= 0) & (slot < slots)
        row = jnp.minimum(row, rows - 1)
        self.length = len_ref[row]
        self.above = jnp.where(row >= 1, len_ref[jnp.maximum(row - 1, 0)], 0)
        self.below = jnp.where(row < rows - 1, len_ref[jnp.minimum(row + 1, rows - 1)], 0)
        self.column = GC + slot - ends_ref[row]

    def side(self, down, step):
        column = self.column + step
        length = self.below if down else self.above
        there = self.real & (column < GC) & (column >= GC - length)
        slot = self.slot + (self.below if down else -self.length) + step
        return there, slot

    def lower_x(self):
        return self.real & (self.column > GC - self.length)

    def upper_x(self):
        return self.real & (self.column < GC - 1)


def hop(device, slot, down):
    owner = slot >> 2
    q = jnp.maximum((owner - device) if down else (device - owner), 0)
    a = jnp.minimum(((q + 1) * 11) >> 5, HOPS - 1)
    b = q - STRIDE * a
    return a, (-b if down else b)


def strips_kernel(h_ref, d_ref, f_ref, v_ref, bottom_ref, top_ref, right_ref, left_ref):
    fields = [v_ref.at[0], v_ref.at[1], h_ref, d_ref.at[0], d_ref.at[1], f_ref]
    row = lax.broadcasted_iota(jnp.int32, (SECTION, LANES), 0)
    lane = lax.broadcasted_iota(jnp.int32, (TS, LANES), 1)
    for t in range(TPD):
        for k, field in enumerate(fields):
            last = field[t, TS - SECTION :, :]
            first = field[t, :SECTION, :]
            if k in (3, 4):
                extra = fields[k - 3]
                last = jnp.where(row == 0, extra[t, TS - SECTION - 1 : TS - SECTION, :], last)
                first = jnp.where(row == SECTION - 1, extra[t, SECTION : SECTION + 1, :], first)
            bottom_ref[t, k * SECTION : (k + 1) * SECTION, :] = last
            top_ref[t, k * SECTION : (k + 1) * SECTION, :] = first
    right = jnp.zeros((TS, LANES), jnp.float32)
    left = jnp.zeros((TS, LANES), jnp.float32)
    for k, field in enumerate(fields):
        here = (lane >> 4) == k
        right = jnp.where(here, pltpu.roll(field[TPD - 1], (MARGIN * k + MARGIN) % LANES, 1), right)
        left = jnp.where(here, pltpu.roll(field[0], MARGIN * k, 1) if k else field[0], left)
    right_ref[...] = right
    left_ref[...] = left


def route_kernel(slots, len_ref, *refs):
    given = refs[: 2 * HOPS]
    right_ref, left_ref = refs[2 * HOPS : 2 * HOPS + 2]
    outs = refs[2 * HOPS + 2 : 2 * HOPS + 5]
    strips, ends_ref, sems = refs[2 * HOPS + 5 :]
    copies = [
        pltpu.make_async_copy(given[i], strips.at[i // HOPS, i % HOPS], sems.at[i]) for i in range(2 * HOPS)
    ]
    for copy in copies:
        copy.start()
    ends = fill_row_ends(len_ref, ends_ref)
    outs[0][PACK:, :] = left_ref[...]
    outs[2][PACK:, :] = right_ref[...]
    for out in outs:
        out[MAIN_BLOCKS * STRIP : PACK, :] = jnp.zeros((2 * STRIP, LANES), jnp.float32)
    lane = lax.broadcasted_iota(jnp.int32, (STRIP, LANES), 1)
    me, count = lax.axis_index("ta"), slots // TPD
    for copy in copies:
        copy.wait()
    for step, out in zip((-1, 0, 1), outs):
        device = lax.rem(me + step + count, count)
        for j in range(TPD):
            tile = Tile(len_ref, ends_ref, ends, device * TPD + j, slots)
            for down in (0, 1):
                for across in (-1, 0, 1):
                    there, slot = tile.side(down, across)
                    a, shift = hop(device, slot, down)

                    @pl.when(there & (shift == step))
                    def _(out=out, j=j, down=down, across=across, a=a, slot=slot):
                        strip = strips[down, a, slot & 3]
                        if across == 0:
                            block = down * TPD + j
                            out[block * STRIP : (block + 1) * STRIP, :] = strip
                        else:
                            block = MAIN_BLOCKS + down
                            first = 2 * j + (across + 1) // 2
                            moved = pltpu.roll(strip, (2 * MARGIN * j + MARGIN) % LANES, 1)
                            rows = slice(block * STRIP, (block + 1) * STRIP)
                            out[rows, :] = jnp.where((lane >> 4) == first, moved, out[rows, :])


def group_mask(flags, shape):
    bits = jnp.int32(0)
    for k, flag in enumerate(flags):
        bits = bits + jnp.where(flag, 1 << k, 0)
    group = lax.broadcasted_iota(jnp.int32, shape, 1) >> 4
    return ((jnp.full(shape, bits) >> group) & 1) == 1


def sweeps_kernel(
    slots, len_ref, h_ref, d_ref, f_ref, v_ref, back_ref, local_ref, ahead_ref,
    vel_ref, next_ref, u, v, w, h, d0, d1, f, ice, packs, ends_ref, sems,
):
    own = (pl.ds(0, TPD), pl.ds(TOP, TS))
    copies = [
        (v_ref.at[0], u.at[(0,) + own]),
        (v_ref.at[1], v.at[(0,) + own]),
        (h_ref, h.at[own]),
        (d_ref.at[0], d0.at[own]),
        (d_ref.at[1], d1.at[own]),
        (f_ref, f.at[own]),
        (back_ref, packs.at[0]),
        (local_ref, packs.at[1, pl.ds(0, PACK)]),
        (ahead_ref, packs.at[2]),
    ]
    copies = [pltpu.make_async_copy(a, b, sems.at[i]) for i, (a, b) in enumerate(copies)]
    for copy in copies:
        copy.start()
    me = lax.axis_index("ta")
    ends = fill_row_ends(len_ref, ends_ref)
    tiles = [Tile(len_ref, ends_ref, ends, me * TPD + j, slots) for j in range(TPD)]
    zero = jnp.zeros((SECTION, LANES), jnp.float32)
    one = jnp.ones((SECTION, LANES), jnp.float32)
    for block in range(TPD + 1):
        for start in (0, ROWS - SECTION):
            rows = slice(start, start + SECTION)
            u[0, block, rows, :] = zero
            v[0, block, rows, :] = zero
            w[block, rows, :] = zero
    for copy in copies:
        copy.wait()

    targets = (u.at[0], v.at[0], h, d0, d1, f)
    for down in (0, 1):
        start = TOP + TS if down else TOP - SECTION
        rows = slice(start, start + SECTION)
        deep = SECTION - 1 if down else 0
        far = start + SECTION if down else start - 1
        for j in range(TPD + 1):
            if j < TPD:
                there, slot = tiles[j].side(down, 0)
                _, shift = hop(me, slot, down)
                which = jnp.where(there, shift + 1, 1)
                base = (down * TPD + j) * STRIP
                parts = [packs[which, base + k * SECTION : base + (k + 1) * SECTION, :] for k in range(6)]
                mask = jnp.full((SECTION, LANES), jnp.where(there, 1, 0)) == 1
            else:
                base = (MAIN_BLOCKS + down) * STRIP
                parts = [
                    packs[0, base + k * SECTION : base + (k + 1) * SECTION, :]
                    + packs[1, base + k * SECTION : base + (k + 1) * SECTION, :]
                    + packs[2, base + k * SECTION : base + (k + 1) * SECTION, :]
                    for k in range(6)
                ]
                flags = [tile.side(down, across)[0] for tile in tiles for across in (-1, 1)]
                mask = group_mask(flags, (SECTION, LANES))
            for k, target in enumerate(targets):
                target[j, rows, :] = jnp.where(mask, parts[k], one if k == 5 else zero)
            for k in (0, 1):
                line = jnp.where(mask, parts[3 + k], zero)
                targets[k][j, far : far + 1, :] = line[deep : deep + 1, :]
            ice[j, rows, :] = jnp.where(mask, one, zero)

    flags = [flag for tile in tiles for flag in (tile.lower_x(), tile.upper_x())]
    mask = group_mask(flags, (TS, LANES))
    group = lax.broadcasted_iota(jnp.int32, (TS, LANES), 1) >> 4
    ice[TPD, TOP : TOP + TS, :] = jnp.where(mask, 1.0, 0.0)
    for k, target in enumerate(targets):
        before = pltpu.roll(packs[2, PACK:, :], (LANES - MARGIN * k) % LANES, 1)
        after = pltpu.roll(packs[0, PACK:, :], (LANES - MARGIN - MARGIN * k) % LANES, 1)
        beside = jnp.where(group == 0, before, after)
        for j in range(TPD):
            tile = target[j, TOP : TOP + TS, :]
            if j + 1 < TPD:
                moved = pltpu.roll(tile, (2 * MARGIN * j + 3 * MARGIN) % LANES, 1)
                beside = jnp.where(group == 2 * (j + 1), moved, beside)
            if j:
                moved = pltpu.roll(tile, (2 * MARGIN * j - MARGIN) % LANES, 1)
                beside = jnp.where(group == 2 * (j - 1) + 1, moved, beside)
        target[TPD, TOP : TOP + TS, :] = jnp.where(mask, beside, 1.0 if k == 5 else 0.0)

    chunk = 24
    first_row, last_row = TOP - SECTION, TOP + TS + SECTION
    lane = lax.broadcasted_iota(jnp.int32, (chunk, LANES), 1)
    at_start, at_end = lane == 0, lane == LANES - 1
    in_group = lane & (2 * MARGIN - 1)
    group_pair = lane >> 5
    before_gap, after_gap = in_group == MARGIN - 1, in_group == MARGIN

    def beside_tile(ref, lead, j, rows):
        centre = ref[lead + (j, rows)]
        edge = pltpu.roll(ref[lead + (TPD, rows)], LANES - MARGIN - 2 * MARGIN * j, 1)
        lower = pltpu.roll(jnp.where(at_end, edge, centre), 1, 1)
        upper = pltpu.roll(jnp.where(at_start, edge, centre), LANES - 1, 1)
        return centre, lower, upper

    def beside_columns(ref, lead, j, rows):
        centre = ref[lead + (TPD, rows)]
        edge = pltpu.roll(ref[lead + (0, rows)], MARGIN, 1)
        for t in range(1, TPD):
            moved = pltpu.roll(ref[lead + (t, rows)], (2 * MARGIN * t + MARGIN) % LANES, 1)
            edge = jnp.where(group_pair == t, moved, edge)
        lower = pltpu.roll(jnp.where(before_gap, edge, centre), 1, 1)
        upper = pltpu.roll(jnp.where(after_gap, edge, centre), LANES - 1, 1)
        return centre, lower, upper

    def viscosity(now, j, beside):
        for start in range(first_row, last_row, chunk):
            rows, under, over = (slice(start + k, start + k + chunk) for k in (0, -1, 1))
            _, u_lx, u_ux = beside(u, (now,), j, rows)
            _, v_lx, v_ux = beside(v, (now,), j, rows)
            ux = u_ux - u_lx
            vy = v[now, j, over] - v[now, j, under]
            shear = (u[now, j, over] - u[now, j, under]) + (v_ux - v_lx)
            strain = 0.25 * (ux * ux + vy * vy + ux * vy + 0.25 * shear * shear) + STRAIN_EPSILON
            w[j, rows] = (0.25 * h[j, rows]) * jnp.exp(jnp.log(strain) * (-1.0 / 3.0))

    def quotient(top, bottom):
        guess = pl.reciprocal(bottom, approx=True)
        return top * (guess * (2.0 - bottom * guess))

    def relax(now, j, beside):
        for start in range(first_row, last_row, chunk):
            rows, under, over = (slice(start + k, start + k + chunk) for k in (0, -1, 1))
            here, w_lx, w_ux = beside(w, (), j, rows)
            c_lx, c_ux = here + w_lx, here + w_ux
            c_ly, c_uy = here + w[j, under], here + w[j, over]
            _, u_lx, u_ux = beside(u, (now,), j, rows)
            _, v_lx, v_ux = beside(v, (now,), j, rows)
            c_x, c_y = c_lx + c_ux, c_ly + c_uy
            drag = f[j, rows]
            u_top = 4.0 * (c_lx * u_lx + c_ux * u_ux) + c_ly * u[now, j, under] + c_uy * u[now, j, over] - d0[j, rows]
            v_top = c_lx * v_lx + c_ux * v_ux + 4.0 * (c_ly * v[now, j, under] + c_uy * v[now, j, over]) - d1[j, rows]
            u_new = quotient(u_top, 4.0 * c_x + c_y + drag)
            v_new = quotient(v_top, c_x + 4.0 * c_y + drag)
            if beside is beside_columns or start == first_row or start + chunk == last_row:
                is_ice = ice[j, rows] > 0.0
                u_new = jnp.where(is_ice, u_new, 0.0)
                v_new = jnp.where(is_ice, v_new, 0.0)
            u[1 - now, j, rows] = u_new
            v[1 - now, j, rows] = v_new

    for j in range(TPD):
        ice[j, TOP : TOP + 2 * SECTION, :] = jnp.ones((2 * SECTION, LANES), jnp.float32)
        ice[j, TOP + TS - 2 * SECTION : TOP + TS, :] = jnp.ones((2 * SECTION, LANES), jnp.float32)

    @pl.loop(0, SWEEPS)
    def _(sweep):
        now = sweep & 1

        @pl.loop(0, TPD)
        def _(j):
            viscosity(now, j, beside_tile)

        viscosity(now, TPD, beside_columns)

        @pl.loop(0, TPD)
        def _(j):
            relax(now, j, beside_tile)

        relax(now, TPD, beside_columns)

    last = SWEEPS & 1
    results = [
        pltpu.make_async_copy(u.at[(last,) + own], vel_ref.at[0], sems.at[0]),
        pltpu.make_async_copy(v.at[(last,) + own], vel_ref.at[1], sems.at[1]),
    ]
    for copy in results:
        copy.start()

    @pl.loop(0, TPD)
    def _(j):
        part = 32
        lane = lax.broadcasted_iota(jnp.int32, (part, LANES), 1)
        at_start, at_end = lane == 0, lane == LANES - 1

        def beside_tile(ref, lead, rows):
            centre = ref[lead + (j, rows)]
            edge = pltpu.roll(ref[lead + (TPD, rows)], LANES - MARGIN - 2 * MARGIN * j, 1)
            lower = pltpu.roll(jnp.where(at_end, edge, centre), 1, 1)
            upper = pltpu.roll(jnp.where(at_start, edge, centre), LANES - 1, 1)
            return centre, lower, upper

        for start in range(TOP, TOP + TS, part):
            rows, under, over = (slice(start + k, start + k + part) for k in (0, -1, 1))
            u_c, u_lx, u_ux = beside_tile(u, (last,), rows)
            h_c, h_lx, h_ux = beside_tile(h, (), rows)
            v_c = v[last, j, rows]
            s_lx, s_ux = 0.5 * (u_lx + u_c), 0.5 * (u_c + u_ux)
            s_ly, s_uy = 0.5 * (v[last, j, under] + v_c), 0.5 * (v_c + v[last, j, over])
            flux_lx = jnp.maximum(s_lx, 0.0) * h_lx + jnp.minimum(s_lx, 0.0) * h_c
            flux_ux = jnp.maximum(s_ux, 0.0) * h_c + jnp.minimum(s_ux, 0.0) * h_ux
            flux_ly = jnp.maximum(s_ly, 0.0) * h[j, under] + jnp.minimum(s_ly, 0.0) * h_c
            flux_uy = jnp.maximum(s_uy, 0.0) * h_c + jnp.minimum(s_uy, 0.0) * h[j, over]
            next_ref[j, start - TOP : start - TOP + part, :] = h_c - TIME_STEP * (
                flux_ux - flux_lx + flux_uy - flux_ly
            )

    for copy in results:
        copy.wait()


def shards(slots, thickness, driving, friction, velocity_start, row_lengths):
    f32 = jnp.float32
    vmem = pl.BlockSpec(memory_space=pltpu.VMEM)
    smem = pl.BlockSpec(memory_space=pltpu.SMEM)
    anywhere = pl.BlockSpec(memory_space=pl.ANY)
    params = pltpu.CompilerParams(vmem_limit_bytes=VMEM_LIMIT)
    strips_shape = jax.ShapeDtypeStruct((TPD, STRIP, LANES), f32)
    columns_shape = jax.ShapeDtypeStruct((TS, LANES), f32)
    rows = row_lengths.shape[0]

    with jax.named_scope("strips"):
        bottom, top, right, left = pl.pallas_call(
            strips_kernel,
            out_shape=(strips_shape, strips_shape, columns_shape, columns_shape),
            in_specs=[vmem] * 4,
            out_specs=(vmem,) * 4,
            compiler_params=params,
        )(thickness, driving, friction, velocity_start)

    with jax.named_scope("strides"):
        bottoms = [bottom] + [cyclic_shift(bottom, STRIDE * a) for a in range(1, HOPS)]
        tops = [top] + [cyclic_shift(top, -STRIDE * a) for a in range(1, HOPS)]

    with jax.named_scope("route"):
        back, local, ahead = pl.pallas_call(
            functools.partial(route_kernel, slots),
            out_shape=(
                jax.ShapeDtypeStruct((FULL_PACK, LANES), f32),
                jax.ShapeDtypeStruct((PACK, LANES), f32),
                jax.ShapeDtypeStruct((FULL_PACK, LANES), f32),
            ),
            in_specs=[smem] + [anywhere] * (2 * HOPS) + [vmem] * 2,
            out_specs=(vmem,) * 3,
            scratch_shapes=[
                pltpu.VMEM((2, HOPS, TPD, STRIP, LANES), f32),
                pltpu.SMEM((rows,), jnp.int32),
                pltpu.SemaphoreType.DMA((2 * HOPS,)),
            ],
            compiler_params=params,
        )(row_lengths, *bottoms, *tops, right, left)

    with jax.named_scope("last_step"):
        back = cyclic_shift(back, -1)
        ahead = cyclic_shift(ahead, 1)

    with jax.named_scope("sweeps"):
        field = pltpu.VMEM((TPD + 1, ROWS, LANES), f32)
        pair = pltpu.VMEM((2, TPD + 1, ROWS, LANES), f32)
        velocity, thickness_next = pl.pallas_call(
            functools.partial(sweeps_kernel, slots),
            out_shape=(
                jax.ShapeDtypeStruct(velocity_start.shape, f32),
                jax.ShapeDtypeStruct(thickness.shape, f32),
            ),
            in_specs=[smem] + [anywhere] * 7,
            out_specs=(anywhere, vmem),
            scratch_shapes=[
                pair, pair, field, field, field, field, field, field,
                pltpu.VMEM((3, FULL_PACK, LANES), f32),
                pltpu.SMEM((rows,), jnp.int32),
                pltpu.SemaphoreType.DMA((9,)),
            ],
            compiler_params=params,
        )(row_lengths, thickness, driving, friction, velocity_start, back, local, ahead)
    return velocity, thickness_next


def solution(mesh):
    in_specs = (
        P("ta", None, None),
        P(None, "ta", None, None),
        P(("ma", "ta"), None, None),
        P(None, "ta", None, None),
        P(),
    )
    out_specs = (P(None, ("ma", "ta"), None, None), P(("ma", "ta"), None, None))
    slots = TPD * mesh.shape["ta"]
    return jax.shard_map(
        functools.partial(shards, slots), mesh=mesh, in_specs=in_specs, out_specs=out_specs, check_vma=False
    )
```

profile of v0, /device:TPU:0, one launch (start us, length us, event | category | flops | bytes accessed | tf_op | source)
XLA Modules:
  0.0 91.8 jit_solution(2720001372799814847)
XLA Ops:
  0.6 0.0 copy-start
  0.6 1.0 %copy-done = f32[2,4,128,128]{3,2,1,0:T(8,128)S(1)} copy-done((f32[2,4,128,128]{3,2,1,0:T(8,128)S(1)}, f32[2,4,128,128]{3,2,1,0:T(8,128)}, u32[]{:S(2)}) %copy-start) | copy-done | bytes 524312
  1.7 0.0 copy-start.2
  1.7 1.0 %copy-done.2 = f32[2,4,128,128]{3,2,1,0:T(8,128)S(1)} copy-done((f32[2,4,128,128]{3,2,1,0:T(8,128)S(1)}, f32[2,4,128,128]{3,2,1,0:T(8,128)}, u32[]{:S(2)}) %copy-start.2) | copy-done | bytes 524312
  2.7 0.0 copy-start.4
  2.7 0.9 %copy-done.4 = f32[4,128,128]{2,1,0:T(8,128)S(1)} copy-done((f32[4,128,128]{2,1,0:T(8,128)S(1)}, f32[4,128,128]{2,1,0:T(8,128)}, u32[]{:S(2)}) %copy-start.4) | copy-done | bytes 262168
  3.7 0.0 copy-start.6
  3.7 0.9 %copy-done.6 = f32[4,128,128]{2,1,0:T(8,128)S(1)} copy-done((f32[4,128,128]{2,1,0:T(8,128)S(1)}, f32[4,128,128]{2,1,0:T(8,128)}, u32[]{:S(2)}) %copy-start.6) | copy-done | bytes 262168
  4.6 0.0 copy-start.5
  4.6 0.0 copy-start.7
  4.6 0.3 strips.1
  4.9 6.5 %collective-permute-start.3 = (f32[4,48,128]{2,1,0:T(8,128)S(1)}, f32[4,48,128]{2,1,0:T(8,128)S(1)}, u32[]{:S(2)}, u32[]{:S(2)}) collective-permute-start(f32[4,48,128]{2,1,0:T(8,128)S(1)} %get-tuple-element.9.refs_0_), channel_id=1, source_target_pairs={{0,12},{1,13},{2,14},{3,15},{4,16},{5,17},{6,18},{7,19},{8,20},{9,... | collective-permute-start | bytes 294920 | tf_op jit(solution)/shard_map/strides/ppermute | solution.py:34
  11.3 1.9 %collective-permute-start.2 = (f32[4,48,128]{2,1,0:T(8,128)S(1)}, f32[4,48,128]{2,1,0:T(8,128)S(1)}, u32[]{:S(2)}, u32[]{:S(2)}) collective-permute-start(f32[4,48,128]{2,1,0:T(8,128)S(1)} %get-tuple-element.9.refs_0_), channel_id=1, source_target_pairs={{0,9},{1,10},{2,11},{3,12},{4,13},{5,14},{6,15},{7,16},{8,17},{9,1... | collective-permute-start | bytes 294920 | tf_op jit(solution)/shard_map/strides/ppermute | solution.py:34
  13.3 1.2 %collective-permute-start.1 = (f32[4,48,128]{2,1,0:T(8,128)S(1)}, f32[4,48,128]{2,1,0:T(8,128)S(1)}, u32[]{:S(2)}, u32[]{:S(2)}) collective-permute-start(f32[4,48,128]{2,1,0:T(8,128)S(1)} %get-tuple-element.9.refs_0_), channel_id=1, source_target_pairs={{0,6},{1,7},{2,8},{3,9},{4,10},{5,11},{6,12},{7,13},{8,14},{9,15},... | collective-permute-start | bytes 294920 | tf_op jit(solution)/shard_map/strides/ppermute | solution.py:34
  14.5 2.8 %collective-permute-start = (f32[4,48,128]{2,1,0:T(8,128)S(1)}, f32[4,48,128]{2,1,0:T(8,128)S(1)}, u32[]{:S(2)}, u32[]{:S(2)}) collective-permute-start(f32[4,48,128]{2,1,0:T(8,128)S(1)} %get-tuple-element.9.refs_0_), channel_id=1, source_target_pairs={{0,3},{1,4},{2,5},{3,6},{4,7},{5,8},{6,9},{7,10},{8,11},{9,12},{10... | collective-permute-start | bytes 294920 | tf_op jit(solution)/shard_map/strides/ppermute | solution.py:34
  17.3 5.6 %collective-permute-start.7 = (f32[4,48,128]{2,1,0:T(8,128)S(1)}, f32[4,48,128]{2,1,0:T(8,128)S(1)}, u32[]{:S(2)}, u32[]{:S(2)}) collective-permute-start(f32[4,48,128]{2,1,0:T(8,128)S(1)} %get-tuple-element.10.refs_5_), channel_id=1, source_target_pairs={{0,116},{1,117},{2,118},{3,119},{4,120},{5,121},{6,122},{7,123},{8... | collective-permute-start | bytes 294920 | tf_op jit(solution)/shard_map/strides/ppermute | solution.py:34
  22.9 0.0 collective-permute-done.3.refs_4_
  22.9 2.1 %collective-permute-start.6 = (f32[4,48,128]{2,1,0:T(8,128)S(1)}, f32[4,48,128]{2,1,0:T(8,128)S(1)}, u32[]{:S(2)}, u32[]{:S(2)}) collective-permute-start(f32[4,48,128]{2,1,0:T(8,128)S(1)} %get-tuple-element.10.refs_5_), channel_id=1, source_target_pairs={{0,119},{1,120},{2,121},{3,122},{4,123},{5,124},{6,125},{7,126},{8... | collective-permute-start | bytes 294920 | tf_op jit(solution)/shard_map/strides/ppermute | solution.py:34
  25.0 0.0 collective-permute-done.2.refs_3_
  25.0 3.1 %collective-permute-start.5 = (f32[4,48,128]{2,1,0:T(8,128)S(1)}, f32[4,48,128]{2,1,0:T(8,128)S(1)}, u32[]{:S(2)}, u32[]{:S(2)}) collective-permute-start(f32[4,48,128]{2,1,0:T(8,128)S(1)} %get-tuple-element.10.refs_5_), channel_id=1, source_target_pairs={{0,122},{1,123},{2,124},{3,125},{4,126},{5,127},{6,0},{7,1},{8,2},... | collective-permute-start | bytes 294920 | tf_op jit(solution)/shard_map/strides/ppermute | solution.py:34
  28.1 0.0 collective-permute-done.1.refs_2_
  28.1 1.6 %collective-permute-start.4 = (f32[4,48,128]{2,1,0:T(8,128)S(1)}, f32[4,48,128]{2,1,0:T(8,128)S(1)}, u32[]{:S(2)}, u32[]{:S(2)}) collective-permute-start(f32[4,48,128]{2,1,0:T(8,128)S(1)} %get-tuple-element.10.refs_5_), channel_id=1, source_target_pairs={{0,125},{1,126},{2,127},{3,0},{4,1},{5,2},{6,3},{7,4},{8,5},{9,6},... | collective-permute-start | bytes 294920 | tf_op jit(solution)/shard_map/strides/ppermute | solution.py:34
  29.7 6.6 %collective-permute-done.refs_1_ = f32[4,48,128]{2,1,0:T(8,128)S(1)} collective-permute-done((f32[4,48,128]{2,1,0:T(8,128)S(1)}, f32[4,48,128]{2,1,0:T(8,128)S(1)}, u32[]{:S(2)}, u32[]{:S(2)}) %collective-permute-start) | collective-permute-done | bytes 98336 | tf_op jit(solution)/shard_map/strides/ppermute | solution.py:34
  36.3 0.0 collective-permute-done.7.refs_9_
  36.3 0.0 collective-permute-done.6.refs_8_
  36.3 0.0 collective-permute-done.5.refs_7_
  36.3 2.5 %collective-permute-done.4.refs_6_ = f32[4,48,128]{2,1,0:T(8,128)S(1)} collective-permute-done((f32[4,48,128]{2,1,0:T(8,128)S(1)}, f32[4,48,128]{2,1,0:T(8,128)S(1)}, u32[]{:S(2)}, u32[]{:S(2)}) %collective-permute-start.4) | collective-permute-done | bytes 98336 | tf_op jit(solution)/shard_map/strides/ppermute | solution.py:34
  38.7 0.0 copy-start.8
  38.7 0.7 copy-done.8
  39.4 0.0 copy-start.1
  39.4 0.0 copy-start.3
  39.4 3.6 %route.1 = (f32[608,128]{1,0:T(8,128)S(1)}, f32[480,128]{1,0:T(8,128)S(1)}, f32[608,128]{1,0:T(8,128)S(1)}) custom-call(s32[22]{0:T(128)S(1)} %copy-done.8, f32[4,48,128]{2,1,0:T(8,128)S(1)} %get-tuple-element.9.refs_0_, f32[4,48,128]{2,1,0:T(8,128)S(1)} %collective-permute-done.refs_1_, f32[4,48,128]{2,1,0:T(8,128)S(1)} %collective-permute-done.1.refs_2_, ...), custom_call_target="tpu_custom_call" | custom-call | tf_op jit(solution)/shard_map/route/pallas_call | solution.py:384
  43.0 6.9 %collective-permute-start.8 = (f32[608,128]{1,0:T(8,128)S(1)}, f32[608,128]{1,0:T(8,128)S(1)}, u32[]{:S(2)}, u32[]{:S(2)}) collective-permute-start(f32[608,128]{1,0:T(8,128)S(1)} %get-tuple-element.13), channel_id=1, source_target_pairs={{0,127},{1,0},{2,1},{3,2},{4,3},{5,4},{6,5},{7,6},{8,7},{9,8},{10,... | collective-permute-start | bytes 933896 | tf_op jit(solution)/shard_map/last_step/ppermute | solution.py:34
  49.9 0.0 collective-permute-start.9
  49.9 4.8 %collective-permute-done.8.back_ref = f32[608,128]{1,0:T(8,128)S(1)} collective-permute-done((f32[608,128]{1,0:T(8,128)S(1)}, f32[608,128]{1,0:T(8,128)S(1)}, u32[]{:S(2)}, u32[]{:S(2)}) %collective-permute-start.8) | collective-permute-done | bytes 311328 | tf_op jit(solution)/shard_map/last_step/ppermute | solution.py:34
  54.8 7.6 %collective-permute-done.9.ahead_ref = f32[608,128]{1,0:T(8,128)S(1)} collective-permute-done((f32[608,128]{1,0:T(8,128)S(1)}, f32[608,128]{1,0:T(8,128)S(1)}, u32[]{:S(2)}, u32[]{:S(2)}) %collective-permute-start.9) | collective-permute-done | bytes 311328 | tf_op jit(solution)/shard_map/last_step/ppermute | solution.py:34
  62.4 0.0 copy-done.5
  62.4 0.0 copy-done.7
  62.4 0.0 copy-done.1
  62.4 0.0 copy-done.3
  62.4 29.2 %sweeps.1 = (f32[2,4,128,128]{3,2,1,0:T(8,128)}, f32[4,128,128]{2,1,0:T(8,128)}) custom-call(s32[22]{0:T(128)S(1)} %copy-done.8, f32[4,128,128]{2,1,0:T(8,128)S(1)} %copy-done.5, f32[2,4,128,128]{3,2,1,0:T(8,128)S(1)} %copy-done.1, f32[4,128,128]{2,1,0:T(8,128)S(1)} %copy-done.7, f32[2,4,128,128]{3,2,1,0:T(8,128)S(1)} %copy-done.3, ...), custom_call_target="tpu_custom_call" | custom-call | tf_op jit(solution)/shard_map/sweeps/pallas_call | solution.py:408
Async XLA Ops:
  0.6 1.0 %copy-start = (f32[2,4,128,128]{3,2,1,0:T(8,128)S(1)}, f32[2,4,128,128]{3,2,1,0:T(8,128)}, u32[]{:S(2)}) copy-start(f32[2,4,128,128]{3,2,1,0:T(8,128)} %d_ref.3) | copy-start | bytes 1572868
  1.7 1.0 %copy-start.2 = (f32[2,4,128,128]{3,2,1,0:T(8,128)S(1)}, f32[2,4,128,128]{3,2,1,0:T(8,128)}, u32[]{:S(2)}) copy-start(f32[2,4,128,128]{3,2,1,0:T(8,128)} %v_ref.3) | copy-start | bytes 1572868
  2.7 0.9 %copy-start.4 = (f32[4,128,128]{2,1,0:T(8,128)S(1)}, f32[4,128,128]{2,1,0:T(8,128)}, u32[]{:S(2)}) copy-start(f32[4,128,128]{2,1,0:T(8,128)} %h_ref.3) | copy-start | bytes 786436
  3.7 0.9 %copy-start.6 = (f32[4,128,128]{2,1,0:T(8,128)S(1)}, f32[4,128,128]{2,1,0:T(8,128)}, u32[]{:S(2)}) copy-start(f32[4,128,128]{2,1,0:T(8,128)} %f_ref.3) | copy-start | bytes 786436
  4.6 57.8 %copy-start.5 = (f32[4,128,128]{2,1,0:T(8,128)S(1)}, f32[4,128,128]{2,1,0:T(8,128)}, u32[]{:S(2)}) copy-start(f32[4,128,128]{2,1,0:T(8,128)} %h_ref.3) | copy-start | bytes 786436
  4.6 57.8 %copy-start.7 = (f32[4,128,128]{2,1,0:T(8,128)S(1)}, f32[4,128,128]{2,1,0:T(8,128)}, u32[]{:S(2)}) copy-start(f32[4,128,128]{2,1,0:T(8,128)} %f_ref.3) | copy-start | bytes 786436
  4.9 18.1 %collective-permute-start.3 = (f32[4,48,128]{2,1,0:T(8,128)S(1)}, f32[4,48,128]{2,1,0:T(8,128)S(1)}, u32[]{:S(2)}, u32[]{:S(2)}) collective-permute-start(f32[4,48,128]{2,1,0:T(8,128)S(1)} %get-tuple-element.9.refs_0_), channel_id=1, source_target_pairs={{0,12},{1,13},{2,14},{3,15},{4,16},{5,17},{6,18},{7,19},{8,20},{9,... | collective-permute-start | bytes 294920 | tf_op jit(solution)/shard_map/strides/ppermute | solution.py:34
  11.3 13.7 %collective-permute-start.2 = (f32[4,48,128]{2,1,0:T(8,128)S(1)}, f32[4,48,128]{2,1,0:T(8,128)S(1)}, u32[]{:S(2)}, u32[]{:S(2)}) collective-permute-start(f32[4,48,128]{2,1,0:T(8,128)S(1)} %get-tuple-element.9.refs_0_), channel_id=1, source_target_pairs={{0,9},{1,10},{2,11},{3,12},{4,13},{5,14},{6,15},{7,16},{8,17},{9,1... | collective-permute-start | bytes 294920 | tf_op jit(solution)/shard_map/strides/ppermute | solution.py:34
  13.3 14.8 %collective-permute-start.1 = (f32[4,48,128]{2,1,0:T(8,128)S(1)}, f32[4,48,128]{2,1,0:T(8,128)S(1)}, u32[]{:S(2)}, u32[]{:S(2)}) collective-permute-start(f32[4,48,128]{2,1,0:T(8,128)S(1)} %get-tuple-element.9.refs_0_), channel_id=1, source_target_pairs={{0,6},{1,7},{2,8},{3,9},{4,10},{5,11},{6,12},{7,13},{8,14},{9,15},... | collective-permute-start | bytes 294920 | tf_op jit(solution)/shard_map/strides/ppermute | solution.py:34
  14.5 21.8 %collective-permute-start = (f32[4,48,128]{2,1,0:T(8,128)S(1)}, f32[4,48,128]{2,1,0:T(8,128)S(1)}, u32[]{:S(2)}, u32[]{:S(2)}) collective-permute-start(f32[4,48,128]{2,1,0:T(8,128)S(1)} %get-tuple-element.9.refs_0_), channel_id=1, source_target_pairs={{0,3},{1,4},{2,5},{3,6},{4,7},{5,8},{6,9},{7,10},{8,11},{9,12},{10... | collective-permute-start | bytes 294920 | tf_op jit(solution)/shard_map/strides/ppermute | solution.py:34
  17.3 19.0 %collective-permute-start.7 = (f32[4,48,128]{2,1,0:T(8,128)S(1)}, f32[4,48,128]{2,1,0:T(8,128)S(1)}, u32[]{:S(2)}, u32[]{:S(2)}) collective-permute-start(f32[4,48,128]{2,1,0:T(8,128)S(1)} %get-tuple-element.10.refs_5_), channel_id=1, source_target_pairs={{0,116},{1,117},{2,118},{3,119},{4,120},{5,121},{6,122},{7,123},{8... | collective-permute-start | bytes 294920 | tf_op jit(solution)/shard_map/strides/ppermute | solution.py:34
  22.9 13.3 %collective-permute-start.6 = (f32[4,48,128]{2,1,0:T(8,128)S(1)}, f32[4,48,128]{2,1,0:T(8,128)S(1)}, u32[]{:S(2)}, u32[]{:S(2)}) collective-permute-start(f32[4,48,128]{2,1,0:T(8,128)S(1)} %get-tuple-element.10.refs_5_), channel_id=1, source_target_pairs={{0,119},{1,120},{2,121},{3,122},{4,123},{5,124},{6,125},{7,126},{8... | collective-permute-start | bytes 294920 | tf_op jit(solution)/shard_map/strides/ppermute | solution.py:34
  25.0 11.3 %collective-permute-start.5 = (f32[4,48,128]{2,1,0:T(8,128)S(1)}, f32[4,48,128]{2,1,0:T(8,128)S(1)}, u32[]{:S(2)}, u32[]{:S(2)}) collective-permute-start(f32[4,48,128]{2,1,0:T(8,128)S(1)} %get-tuple-element.10.refs_5_), channel_id=1, source_target_pairs={{0,122},{1,123},{2,124},{3,125},{4,126},{5,127},{6,0},{7,1},{8,2},... | collective-permute-start | bytes 294920 | tf_op jit(solution)/shard_map/strides/ppermute | solution.py:34
  28.1 10.7 %collective-permute-start.4 = (f32[4,48,128]{2,1,0:T(8,128)S(1)}, f32[4,48,128]{2,1,0:T(8,128)S(1)}, u32[]{:S(2)}, u32[]{:S(2)}) collective-permute-start(f32[4,48,128]{2,1,0:T(8,128)S(1)} %get-tuple-element.10.refs_5_), channel_id=1, source_target_pairs={{0,125},{1,126},{2,127},{3,0},{4,1},{5,2},{6,3},{7,4},{8,5},{9,6},... | collective-permute-start | bytes 294920 | tf_op jit(solution)/shard_map/strides/ppermute | solution.py:34
  38.7 0.7 copy-start.8
  39.4 23.0 %copy-start.1 = (f32[2,4,128,128]{3,2,1,0:T(8,128)S(1)}, f32[2,4,128,128]{3,2,1,0:T(8,128)}, u32[]{:S(2)}) copy-start(f32[2,4,128,128]{3,2,1,0:T(8,128)} %d_ref.3) | copy-start | bytes 1572868
  39.4 23.0 %copy-start.3 = (f32[2,4,128,128]{3,2,1,0:T(8,128)S(1)}, f32[2,4,128,128]{3,2,1,0:T(8,128)}, u32[]{:S(2)}) copy-start(f32[2,4,128,128]{3,2,1,0:T(8,128)} %v_ref.3) | copy-start | bytes 1572868
  43.0 11.7 %collective-permute-start.8 = (f32[608,128]{1,0:T(8,128)S(1)}, f32[608,128]{1,0:T(8,128)S(1)}, u32[]{:S(2)}, u32[]{:S(2)}) collective-permute-start(f32[608,128]{1,0:T(8,128)S(1)} %get-tuple-element.13), channel_id=1, source_target_pairs={{0,127},{1,0},{2,1},{3,2},{4,3},{5,4},{6,5},{7,6},{8,7},{9,8},{10,... | collective-permute-start | bytes 933896 | tf_op jit(solution)/shard_map/last_step/ppermute | solution.py:34
  49.9 12.4 %collective-permute-start.9 = (f32[608,128]{1,0:T(8,128)S(1)}, f32[608,128]{1,0:T(8,128)S(1)}, u32[]{:S(2)}, u32[]{:S(2)}) collective-permute-start(f32[608,128]{1,0:T(8,128)S(1)} %get-tuple-element.15), channel_id=1, source_target_pairs={{0,1},{1,2},{2,3},{3,4},{4,5},{5,6},{6,7},{7,8},{8,9},{9,10},{10,1... | collective-permute-start | bytes 933896 | tf_op jit(solution)/shard_map/last_step/ppermute | solution.py:34
where the time goes:
time: 92 us; the launch traced here: 91.8 us
  Pallas kernels  33.1 us (36%)
  starting transfers between devices  31.7 us (34%)
  waiting for transfers between devices  21.5 us (23%)
  local copies, waits for them, and re-layouts  4.65 us (5%)
    ppermute x10, starting transfers between devices, cyclic_shift(): lax.ppermute(value, 'ta', [(i, (i + steps) % count) for i in range(count)])  31.7 us
    pallas_call x1, Pallas kernels, shards(): pl.pallas_call(functools.partial(sweeps_kernel, slots), out_shape=(jax.Sh...  29.2 us
    ppermute x10, waiting for transfers between devices, cyclic_shift(): lax.ppermute(value, 'ta', [(i, (i + steps) % count) for i in range(count)])  21.5 us
    unnamed x18, local copies, waits for them, and re-layouts  4.65 us
    pallas_call x1, Pallas kernels, shards(): pl.pallas_call(functools.partial(route_kernel, slots), out_shape=(jax.Sha...  3.59 us
  transfers between devices with their start and end apart: 10, of which 4 were waited for; matrix products, arithmetic and copies ran while one was open for 0% of the time, Pallas kernels for 0%

commit v1 on v0

--- a/solution.py
+++ b/solution.py
@@ -134,14 +134,13 @@
 
                     @pl.when(there & (shift == step))
                     def _(out=out, j=j, down=down, across=across, a=a, slot=slot):
-                        strip = strips[down, a, slot & 3]
+                        moved = pltpu.roll(strips[down, a, slot & 3], 2 * MARGIN * j + MARGIN, 1)
                         if across == 0:
                             block = down * TPD + j
-                            out[block * STRIP : (block + 1) * STRIP, :] = strip
+                            out[block * STRIP : (block + 1) * STRIP, :] = moved
                         else:
                             block = MAIN_BLOCKS + down
                             first = 2 * j + (across + 1) // 2
-                            moved = pltpu.roll(strip, (2 * MARGIN * j + MARGIN) % LANES, 1)
                             rows = slice(block * STRIP, (block + 1) * STRIP)
                             out[rows, :] = jnp.where((lane >> 4) == first, moved, out[rows, :])
 
@@ -156,12 +155,13 @@
 
 def sweeps_kernel(
     slots, len_ref, h_ref, d_ref, f_ref, v_ref, back_ref, local_ref, ahead_ref,
-    vel_ref, next_ref, u, v, w, h, d0, d1, f, ice, packs, ends_ref, sems,
+    vel_ref, next_ref, u, v, u_other, v_other, w, h, d0, d1, f, ice,
+    u_low, u_high, v_low, v_high, results, packs, ends_ref, sems, out_sems,
 ):
     own = (pl.ds(0, TPD), pl.ds(TOP, TS))
     copies = [
-        (v_ref.at[0], u.at[(0,) + own]),
-        (v_ref.at[1], v.at[(0,) + own]),
+        (v_ref.at[0], u.at[own]),
+        (v_ref.at[1], v.at[own]),
         (h_ref, h.at[own]),
         (d_ref.at[0], d0.at[own]),
         (d_ref.at[1], d1.at[own]),
@@ -181,13 +181,13 @@
     for block in range(TPD + 1):
         for start in (0, ROWS - SECTION):
             rows = slice(start, start + SECTION)
-            u[0, block, rows, :] = zero
-            v[0, block, rows, :] = zero
+            u[block, rows, :] = zero
+            v[block, rows, :] = zero
             w[block, rows, :] = zero
     for copy in copies:
         copy.wait()
 
-    targets = (u.at[0], v.at[0], h, d0, d1, f)
+    targets = (u, v, h, d0, d1, f)
     for down in (0, 1):
         start = TOP + TS if down else TOP - SECTION
         rows = slice(start, start + SECTION)
@@ -220,55 +220,54 @@
 
     flags = [flag for tile in tiles for flag in (tile.lower_x(), tile.upper_x())]
     mask = group_mask(flags, (TS, LANES))
-    group = lax.broadcasted_iota(jnp.int32, (TS, LANES), 1) >> 4
-    ice[TPD, TOP : TOP + TS, :] = jnp.where(mask, 1.0, 0.0)
+    lane = lax.broadcasted_iota(jnp.int32, (TS, LANES), 1)
+    group, group_pair = lane >> 4, lane >> 5
+    middle = slice(TOP, TOP + TS)
+    ice[TPD, middle, :] = jnp.where(mask, 1.0, 0.0)
     for k, target in enumerate(targets):
+        edges = None
+        for j in range(TPD):
+            tile = pltpu.roll(target[j, middle, :], 2 * MARGIN * j + MARGIN, 1)
+            target[j, middle, :] = tile
+            edges = tile if j == 0 else jnp.where(group_pair == j, tile, edges)
         before = pltpu.roll(packs[2, PACK:, :], (LANES - MARGIN * k) % LANES, 1)
         after = pltpu.roll(packs[0, PACK:, :], (LANES - MARGIN - MARGIN * k) % LANES, 1)
-        beside = jnp.where(group == 0, before, after)
-        for j in range(TPD):
-            tile = target[j, TOP : TOP + TS, :]
-            if j + 1 < TPD:
-                moved = pltpu.roll(tile, (2 * MARGIN * j + 3 * MARGIN) % LANES, 1)
-                beside = jnp.where(group == 2 * (j + 1), moved, beside)
-            if j:
-                moved = pltpu.roll(tile, (2 * MARGIN * j - MARGIN) % LANES, 1)
-                beside = jnp.where(group == 2 * (j - 1) + 1, moved, beside)
-        target[TPD, TOP : TOP + TS, :] = jnp.where(mask, beside, 1.0 if k == 5 else 0.0)
-
-    chunk = 24
+        lower = jnp.where(group == 0, before, pltpu.roll(edges, 2 * MARGIN, 1))
+        upper = jnp.where(group == 2 * TPD - 1, after, pltpu.roll(edges, LANES - 2 * MARGIN, 1))
+        beside = jnp.where((group & 1) == 0, lower, upper)
+        target[TPD, middle, :] = jnp.where(mask, beside, 1.0 if k == 5 else 0.0)
+
+    chunk = 72
     first_row, last_row = TOP - SECTION, TOP + TS + SECTION
-    lane = lax.broadcasted_iota(jnp.int32, (chunk, LANES), 1)
-    at_start, at_end = lane == 0, lane == LANES - 1
-    in_group = lane & (2 * MARGIN - 1)
-    group_pair = lane >> 5
-    before_gap, after_gap = in_group == MARGIN - 1, in_group == MARGIN
-
-    def beside_tile(ref, lead, j, rows):
-        centre = ref[lead + (j, rows)]
-        edge = pltpu.roll(ref[lead + (TPD, rows)], LANES - MARGIN - 2 * MARGIN * j, 1)
-        lower = pltpu.roll(jnp.where(at_end, edge, centre), 1, 1)
-        upper = pltpu.roll(jnp.where(at_start, edge, centre), LANES - 1, 1)
+
+    def in_tile(ref, j, rows):
+        centre, edge = ref[j, rows], ref[TPD, rows]
+        lane = lax.broadcasted_iota(jnp.int32, centre.shape, 1)
+        high_side = 2 * MARGIN * j + MARGIN
+        lower = pltpu.roll(jnp.where(lane == high_side - 1, edge, centre), 1, 1)
+        upper = pltpu.roll(jnp.where(lane == high_side, edge, centre), LANES - 1, 1)
         return centre, lower, upper
 
-    def beside_columns(ref, lead, j, rows):
-        centre = ref[lead + (TPD, rows)]
-        edge = pltpu.roll(ref[lead + (0, rows)], MARGIN, 1)
+    def in_columns(ref, j, rows):
+        centre, edge = ref[TPD, rows], ref[0, rows]
+        lane = lax.broadcasted_iota(jnp.int32, centre.shape, 1)
         for t in range(1, TPD):
-            moved = pltpu.roll(ref[lead + (t, rows)], (2 * MARGIN * t + MARGIN) % LANES, 1)
-            edge = jnp.where(group_pair == t, moved, edge)
-        lower = pltpu.roll(jnp.where(before_gap, edge, centre), 1, 1)
-        upper = pltpu.roll(jnp.where(after_gap, edge, centre), LANES - 1, 1)
+            edge = jnp.where((lane >> 5) == t, ref[t, rows], edge)
+        within = lane & (2 * MARGIN - 1)
+        lower = pltpu.roll(jnp.where(within == MARGIN - 1, edge, centre), 1, 1)
+        upper = pltpu.roll(jnp.where(within == MARGIN, edge, centre), LANES - 1, 1)
         return centre, lower, upper
 
-    def viscosity(now, j, beside):
+    def viscosity(u, v, j, beside):
         for start in range(first_row, last_row, chunk):
             rows, under, over = (slice(start + k, start + k + chunk) for k in (0, -1, 1))
-            _, u_lx, u_ux = beside(u, (now,), j, rows)
-            _, v_lx, v_ux = beside(v, (now,), j, rows)
+            _, u_lx, u_ux = beside(u, j, rows)
+            _, v_lx, v_ux = beside(v, j, rows)
+            u_low[j, rows], u_high[j, rows] = u_lx, u_ux
+            v_low[j, rows], v_high[j, rows] = v_lx, v_ux
             ux = u_ux - u_lx
-            vy = v[now, j, over] - v[now, j, under]
-            shear = (u[now, j, over] - u[now, j, under]) + (v_ux - v_lx)
+            vy = v[j, over] - v[j, under]
+            shear = (u[j, over] - u[j, under]) + (v_ux - v_lx)
             strain = 0.25 * (ux * ux + vy * vy + ux * vy + 0.25 * shear * shear) + STRAIN_EPSILON
             w[j, rows] = (0.25 * h[j, rows]) * jnp.exp(jnp.log(strain) * (-1.0 / 3.0))
 
@@ -276,85 +275,77 @@
         guess = pl.reciprocal(bottom, approx=True)
         return top * (guess * (2.0 - bottom * guess))
 
-    def relax(now, j, beside):
+    def relax(u, v, u_next, v_next, j, beside):
         for start in range(first_row, last_row, chunk):
             rows, under, over = (slice(start + k, start + k + chunk) for k in (0, -1, 1))
-            here, w_lx, w_ux = beside(w, (), j, rows)
+            here, w_lx, w_ux = beside(w, j, rows)
             c_lx, c_ux = here + w_lx, here + w_ux
             c_ly, c_uy = here + w[j, under], here + w[j, over]
-            _, u_lx, u_ux = beside(u, (now,), j, rows)
-            _, v_lx, v_ux = beside(v, (now,), j, rows)
+            u_lx, u_ux = u_low[j, rows], u_high[j, rows]
+            v_lx, v_ux = v_low[j, rows], v_high[j, rows]
             c_x, c_y = c_lx + c_ux, c_ly + c_uy
             drag = f[j, rows]
-            u_top = 4.0 * (c_lx * u_lx + c_ux * u_ux) + c_ly * u[now, j, under] + c_uy * u[now, j, over] - d0[j, rows]
-            v_top = c_lx * v_lx + c_ux * v_ux + 4.0 * (c_ly * v[now, j, under] + c_uy * v[now, j, over]) - d1[j, rows]
+            u_top = 4.0 * (c_lx * u_lx + c_ux * u_ux) + c_ly * u[j, under] + c_uy * u[j, over] - d0[j, rows]
+            v_top = c_lx * v_lx + c_ux * v_ux + 4.0 * (c_ly * v[j, under] + c_uy * v[j, over]) - d1[j, rows]
             u_new = quotient(u_top, 4.0 * c_x + c_y + drag)
             v_new = quotient(v_top, c_x + 4.0 * c_y + drag)
-            if beside is beside_columns or start == first_row or start + chunk == last_row:
+            if beside is in_columns or start == first_row or start + chunk == last_row:
                 is_ice = ice[j, rows] > 0.0
                 u_new = jnp.where(is_ice, u_new, 0.0)
                 v_new = jnp.where(is_ice, v_new, 0.0)
-            u[1 - now, j, rows] = u_new
-            v[1 - now, j, rows] = v_new
+            u_next[j, rows] = u_new
+            v_next[j, rows] = v_new
 
     for j in range(TPD):
-        ice[j, TOP : TOP + 2 * SECTION, :] = jnp.ones((2 * SECTION, LANES), jnp.float32)
-        ice[j, TOP + TS - 2 * SECTION : TOP + TS, :] = jnp.ones((2 * SECTION, LANES), jnp.float32)
-
-    @pl.loop(0, SWEEPS)
-    def _(sweep):
-        now = sweep & 1
-
+        ice[j, middle, :] = jnp.ones((TS, LANES), jnp.float32)
+
+    def sweep(*state):
         @pl.loop(0, TPD)
         def _(j):
-            viscosity(now, j, beside_tile)
-
-        viscosity(now, TPD, beside_columns)
+            viscosity(*state[:2], j, in_tile)
+
+        viscosity(*state[:2], TPD, in_columns)
 
         @pl.loop(0, TPD)
         def _(j):
-            relax(now, j, beside_tile)
-
-        relax(now, TPD, beside_columns)
-
-    last = SWEEPS & 1
-    results = [
-        pltpu.make_async_copy(u.at[(last,) + own], vel_ref.at[0], sems.at[0]),
-        pltpu.make_async_copy(v.at[(last,) + own], vel_ref.at[1], sems.at[1]),
-    ]
-    for copy in results:
-        copy.start()
+            relax(*state, j, in_tile)
+
+        relax(*state, TPD, in_columns)
+
+    @pl.loop(0, SWEEPS // 2)
+    def _(_):
+        sweep(u, v, u_other, v_other)
+        sweep(u_other, v_other, u, v)
+
+    def given(j):
+        refs = (vel_ref.at[0, j], vel_ref.at[1, j], next_ref.at[j])
+        return [pltpu.make_async_copy(results.at[k, j], ref, out_sems.at[k, j]) for k, ref in enumerate(refs)]
 
     @pl.loop(0, TPD)
     def _(j):
-        part = 32
-        lane = lax.broadcasted_iota(jnp.int32, (part, LANES), 1)
-        at_start, at_end = lane == 0, lane == LANES - 1
-
-        def beside_tile(ref, lead, rows):
-            centre = ref[lead + (j, rows)]
-            edge = pltpu.roll(ref[lead + (TPD, rows)], LANES - MARGIN - 2 * MARGIN * j, 1)
-            lower = pltpu.roll(jnp.where(at_end, edge, centre), 1, 1)
-            upper = pltpu.roll(jnp.where(at_start, edge, centre), LANES - 1, 1)
-            return centre, lower, upper
+        part = 64
+        back = LANES - MARGIN - 2 * MARGIN * j
 
         for start in range(TOP, TOP + TS, part):
             rows, under, over = (slice(start + k, start + k + part) for k in (0, -1, 1))
-            u_c, u_lx, u_ux = beside_tile(u, (last,), rows)
-            h_c, h_lx, h_ux = beside_tile(h, (), rows)
-            v_c = v[last, j, rows]
+            u_c, u_lx, u_ux = in_tile(u, j, rows)
+            h_c, h_lx, h_ux = in_tile(h, j, rows)
+            v_c = v[j, rows]
             s_lx, s_ux = 0.5 * (u_lx + u_c), 0.5 * (u_c + u_ux)
-            s_ly, s_uy = 0.5 * (v[last, j, under] + v_c), 0.5 * (v_c + v[last, j, over])
+            s_ly, s_uy = 0.5 * (v[j, under] + v_c), 0.5 * (v_c + v[j, over])
             flux_lx = jnp.maximum(s_lx, 0.0) * h_lx + jnp.minimum(s_lx, 0.0) * h_c
             flux_ux = jnp.maximum(s_ux, 0.0) * h_c + jnp.minimum(s_ux, 0.0) * h_ux
             flux_ly = jnp.maximum(s_ly, 0.0) * h[j, under] + jnp.minimum(s_ly, 0.0) * h_c
             flux_uy = jnp.maximum(s_uy, 0.0) * h_c + jnp.minimum(s_uy, 0.0) * h[j, over]
-            next_ref[j, start - TOP : start - TOP + part, :] = h_c - TIME_STEP * (
-                flux_ux - flux_lx + flux_uy - flux_ly
-            )
-
-    for copy in results:
-        copy.wait()
+            h_next = h_c - TIME_STEP * (flux_ux - flux_lx + flux_uy - flux_ly)
+            for k, value in enumerate((u_c, v_c, h_next)):
+                results[k, j, start - TOP : start - TOP + part, :] = pltpu.roll(value, back, 1)
+        for copy in given(j):
+            copy.start()
+
+    for j in range(TPD):
+        for copy in given(j):
+            copy.wait()
 
 
 def shards(slots, thickness, driving, friction, velocity_start, row_lengths):
@@ -404,7 +395,6 @@
 
     with jax.named_scope("sweeps"):
         field = pltpu.VMEM((TPD + 1, ROWS, LANES), f32)
-        pair = pltpu.VMEM((2, TPD + 1, ROWS, LANES), f32)
         velocity, thickness_next = pl.pallas_call(
             functools.partial(sweeps_kernel, slots),
             out_shape=(
@@ -412,12 +402,14 @@
                 jax.ShapeDtypeStruct(thickness.shape, f32),
             ),
             in_specs=[smem] + [anywhere] * 7,
-            out_specs=(anywhere, vmem),
+            out_specs=(anywhere, anywhere),
             scratch_shapes=[
-                pair, pair, field, field, field, field, field, field,
+                *[field] * 14,
+                pltpu.VMEM((3, TPD, TS, LANES), f32),
                 pltpu.VMEM((3, FULL_PACK, LANES), f32),
                 pltpu.SMEM((rows,), jnp.int32),
                 pltpu.SemaphoreType.DMA((9,)),
+                pltpu.SemaphoreType.DMA((3, TPD)),
             ],
             compiler_params=params,
         )(row_lengths, thickness, driving, friction, velocity_start, back, local, ahead)

time: 92 us -> 73.9 us (0.80)
  Pallas kernels: 33.1 us -> 15.1 us
    pallas_call x1, Pallas kernels: 29.2 us -> 10.8 us  [shards(): pl.pallas_call(functools.partial(sweeps_kernel, slots), out_shape=(jax.Sh...]
where the time goes in v1:
time: 73.9 us; the launch traced here: 73.7 us
  starting transfers between devices  31.6 us (43%)
  waiting for transfers between devices  21.5 us (29%)
  Pallas kernels  15.1 us (20%)
  local copies, waits for them, and re-layouts  4.65 us (6%)
  between operations  0.84 us (1%)
    ppermute x10, starting transfers between devices, cyclic_shift(): lax.ppermute(value, 'ta', [(i, (i + steps) % count) for i in range(count)])  31.6 us
    ppermute x10, waiting for transfers between devices, cyclic_shift(): lax.ppermute(value, 'ta', [(i, (i + steps) % count) for i in range(count)])  21.5 us
    pallas_call x1, Pallas kernels, shards(): pl.pallas_call(functools.partial(sweeps_kernel, slots), out_shape=(jax.Sh...  10.8 us
    unnamed x18, local copies, waits for them, and re-layouts  4.65 us
    pallas_call x1, Pallas kernels, shards(): pl.pallas_call(functools.partial(route_kernel, slots), out_shape=(jax.Sha...  4.02 us
  transfers between devices with their start and end apart: 10, of which 4 were waited for; matrix products, arithmetic and copies ran while one was open for 0% of the time, Pallas kernels for 0%

profile of v1, /device:TPU:0, one launch (start us, length us, event | category | flops | bytes accessed | tf_op | source)
XLA Modules:
  0.0 73.7 jit_solution(10995335624973204907)
XLA Ops:
  0.6 0.0 copy-start
  0.6 1.0 %copy-done = f32[2,4,128,128]{3,2,1,0:T(8,128)S(1)} copy-done((f32[2,4,128,128]{3,2,1,0:T(8,128)S(1)}, f32[2,4,128,128]{3,2,1,0:T(8,128)}, u32[]{:S(2)}) %copy-start) | copy-done | bytes 524312
  1.7 0.0 copy-start.2
  1.7 1.0 %copy-done.2 = f32[2,4,128,128]{3,2,1,0:T(8,128)S(1)} copy-done((f32[2,4,128,128]{3,2,1,0:T(8,128)S(1)}, f32[2,4,128,128]{3,2,1,0:T(8,128)}, u32[]{:S(2)}) %copy-start.2) | copy-done | bytes 524312
  2.7 0.0 copy-start.4
  2.7 0.9 %copy-done.4 = f32[4,128,128]{2,1,0:T(8,128)S(1)} copy-done((f32[4,128,128]{2,1,0:T(8,128)S(1)}, f32[4,128,128]{2,1,0:T(8,128)}, u32[]{:S(2)}) %copy-start.4) | copy-done | bytes 262168
  3.7 0.0 copy-start.6
  3.7 0.9 %copy-done.6 = f32[4,128,128]{2,1,0:T(8,128)S(1)} copy-done((f32[4,128,128]{2,1,0:T(8,128)S(1)}, f32[4,128,128]{2,1,0:T(8,128)}, u32[]{:S(2)}) %copy-start.6) | copy-done | bytes 262168
  4.6 0.0 copy-start.5
  4.6 0.0 copy-start.7
  4.6 0.3 strips.1
  4.9 6.5 %collective-permute-start.3 = (f32[4,48,128]{2,1,0:T(8,128)S(1)}, f32[4,48,128]{2,1,0:T(8,128)S(1)}, u32[]{:S(2)}, u32[]{:S(2)}) collective-permute-start(f32[4,48,128]{2,1,0:T(8,128)S(1)} %get-tuple-element.9.refs_0_), channel_id=1, source_target_pairs={{0,12},{1,13},{2,14},{3,15},{4,16},{5,17},{6,18},{7,19},{8,20},{9,... | collective-permute-start | bytes 294920 | tf_op jit(solution)/shard_map/strides/ppermute | solution.py:34
  11.3 1.9 %collective-permute-start.2 = (f32[4,48,128]{2,1,0:T(8,128)S(1)}, f32[4,48,128]{2,1,0:T(8,128)S(1)}, u32[]{:S(2)}, u32[]{:S(2)}) collective-permute-start(f32[4,48,128]{2,1,0:T(8,128)S(1)} %get-tuple-element.9.refs_0_), channel_id=1, source_target_pairs={{0,9},{1,10},{2,11},{3,12},{4,13},{5,14},{6,15},{7,16},{8,17},{9,1... | collective-permute-start | bytes 294920 | tf_op jit(solution)/shard_map/strides/ppermute | solution.py:34
  13.3 1.2 %collective-permute-start.1 = (f32[4,48,128]{2,1,0:T(8,128)S(1)}, f32[4,48,128]{2,1,0:T(8,128)S(1)}, u32[]{:S(2)}, u32[]{:S(2)}) collective-permute-start(f32[4,48,128]{2,1,0:T(8,128)S(1)} %get-tuple-element.9.refs_0_), channel_id=1, source_target_pairs={{0,6},{1,7},{2,8},{3,9},{4,10},{5,11},{6,12},{7,13},{8,14},{9,15},... | collective-permute-start | bytes 294920 | tf_op jit(solution)/shard_map/strides/ppermute | solution.py:34
  14.5 2.8 %collective-permute-start = (f32[4,48,128]{2,1,0:T(8,128)S(1)}, f32[4,48,128]{2,1,0:T(8,128)S(1)}, u32[]{:S(2)}, u32[]{:S(2)}) collective-permute-start(f32[4,48,128]{2,1,0:T(8,128)S(1)} %get-tuple-element.9.refs_0_), channel_id=1, source_target_pairs={{0,3},{1,4},{2,5},{3,6},{4,7},{5,8},{6,9},{7,10},{8,11},{9,12},{10... | collective-permute-start | bytes 294920 | tf_op jit(solution)/shard_map/strides/ppermute | solution.py:34
  17.3 5.6 %collective-permute-start.7 = (f32[4,48,128]{2,1,0:T(8,128)S(1)}, f32[4,48,128]{2,1,0:T(8,128)S(1)}, u32[]{:S(2)}, u32[]{:S(2)}) collective-permute-start(f32[4,48,128]{2,1,0:T(8,128)S(1)} %get-tuple-element.10.refs_5_), channel_id=1, source_target_pairs={{0,116},{1,117},{2,118},{3,119},{4,120},{5,121},{6,122},{7,123},{8... | collective-permute-start | bytes 294920 | tf_op jit(solution)/shard_map/strides/ppermute | solution.py:34
  22.9 0.0 collective-permute-done.3.refs_4_
  22.9 2.1 %collective-permute-start.6 = (f32[4,48,128]{2,1,0:T(8,128)S(1)}, f32[4,48,128]{2,1,0:T(8,128)S(1)}, u32[]{:S(2)}, u32[]{:S(2)}) collective-permute-start(f32[4,48,128]{2,1,0:T(8,128)S(1)} %get-tuple-element.10.refs_5_), channel_id=1, source_target_pairs={{0,119},{1,120},{2,121},{3,122},{4,123},{5,124},{6,125},{7,126},{8... | collective-permute-start | bytes 294920 | tf_op jit(solution)/shard_map/strides/ppermute | solution.py:34
  25.0 0.0 collective-permute-done.2.refs_3_
  25.0 3.1 %collective-permute-start.5 = (f32[4,48,128]{2,1,0:T(8,128)S(1)}, f32[4,48,128]{2,1,0:T(8,128)S(1)}, u32[]{:S(2)}, u32[]{:S(2)}) collective-permute-start(f32[4,48,128]{2,1,0:T(8,128)S(1)} %get-tuple-element.10.refs_5_), channel_id=1, source_target_pairs={{0,122},{1,123},{2,124},{3,125},{4,126},{5,127},{6,0},{7,1},{8,2},... | collective-permute-start | bytes 294920 | tf_op jit(solution)/shard_map/strides/ppermute | solution.py:34
  28.1 0.0 collective-permute-done.1.refs_2_
  28.1 1.6 %collective-permute-start.4 = (f32[4,48,128]{2,1,0:T(8,128)S(1)}, f32[4,48,128]{2,1,0:T(8,128)S(1)}, u32[]{:S(2)}, u32[]{:S(2)}) collective-permute-start(f32[4,48,128]{2,1,0:T(8,128)S(1)} %get-tuple-element.10.refs_5_), channel_id=1, source_target_pairs={{0,125},{1,126},{2,127},{3,0},{4,1},{5,2},{6,3},{7,4},{8,5},{9,6},... | collective-permute-start | bytes 294920 | tf_op jit(solution)/shard_map/strides/ppermute | solution.py:34
  29.7 6.6 %collective-permute-done.refs_1_ = f32[4,48,128]{2,1,0:T(8,128)S(1)} collective-permute-done((f32[4,48,128]{2,1,0:T(8,128)S(1)}, f32[4,48,128]{2,1,0:T(8,128)S(1)}, u32[]{:S(2)}, u32[]{:S(2)}) %collective-permute-start) | collective-permute-done | bytes 98336 | tf_op jit(solution)/shard_map/strides/ppermute | solution.py:34
  36.3 0.0 collective-permute-done.7.refs_9_
  36.3 0.0 collective-permute-done.6.refs_8_
  36.3 0.0 collective-permute-done.5.refs_7_
  36.3 2.5 %collective-permute-done.4.refs_6_ = f32[4,48,128]{2,1,0:T(8,128)S(1)} collective-permute-done((f32[4,48,128]{2,1,0:T(8,128)S(1)}, f32[4,48,128]{2,1,0:T(8,128)S(1)}, u32[]{:S(2)}, u32[]{:S(2)}) %collective-permute-start.4) | collective-permute-done | bytes 98336 | tf_op jit(solution)/shard_map/strides/ppermute | solution.py:34
  38.7 0.0 copy-start.8
  38.7 0.7 copy-done.8
  39.4 0.0 copy-start.1
  39.4 0.0 copy-start.3
  39.4 4.0 %route.1 = (f32[608,128]{1,0:T(8,128)S(1)}, f32[480,128]{1,0:T(8,128)S(1)}, f32[608,128]{1,0:T(8,128)S(1)}) custom-call(s32[22]{0:T(128)S(1)} %copy-done.8, f32[4,48,128]{2,1,0:T(8,128)S(1)} %get-tuple-element.9.refs_0_, f32[4,48,128]{2,1,0:T(8,128)S(1)} %collective-permute-done.refs_1_, f32[4,48,128]{2,1,0:T(8,128)S(1)} %collective-permute-done.1.refs_2_, ...), custom_call_target="tpu_custom_call" | custom-call | tf_op jit(solution)/shard_map/route/pallas_call | solution.py:375
  43.4 6.8 %collective-permute-start.8 = (f32[608,128]{1,0:T(8,128)S(1)}, f32[608,128]{1,0:T(8,128)S(1)}, u32[]{:S(2)}, u32[]{:S(2)}) collective-permute-start(f32[608,128]{1,0:T(8,128)S(1)} %get-tuple-element.13), channel_id=1, source_target_pairs={{0,127},{1,0},{2,1},{3,2},{4,3},{5,4},{6,5},{7,6},{8,7},{9,8},{10,... | collective-permute-start | bytes 933896 | tf_op jit(solution)/shard_map/last_step/ppermute | solution.py:34
  50.2 0.0 collective-permute-start.9
  50.2 4.8 %collective-permute-done.8.back_ref = f32[608,128]{1,0:T(8,128)S(1)} collective-permute-done((f32[608,128]{1,0:T(8,128)S(1)}, f32[608,128]{1,0:T(8,128)S(1)}, u32[]{:S(2)}, u32[]{:S(2)}) %collective-permute-start.8) | collective-permute-done | bytes 311328 | tf_op jit(solution)/shard_map/last_step/ppermute | solution.py:34
  55.1 7.6 %collective-permute-done.9.ahead_ref = f32[608,128]{1,0:T(8,128)S(1)} collective-permute-done((f32[608,128]{1,0:T(8,128)S(1)}, f32[608,128]{1,0:T(8,128)S(1)}, u32[]{:S(2)}, u32[]{:S(2)}) %collective-permute-start.9) | collective-permute-done | bytes 311328 | tf_op jit(solution)/shard_map/last_step/ppermute | solution.py:34
  62.7 0.0 copy-done.5
  62.7 0.0 copy-done.7
  62.7 0.0 copy-done.1
  62.7 0.0 copy-done.3
  62.7 10.8 %sweeps.1 = (f32[2,4,128,128]{3,2,1,0:T(8,128)}, f32[4,128,128]{2,1,0:T(8,128)}) custom-call(s32[22]{0:T(128)S(1)} %copy-done.8, f32[4,128,128]{2,1,0:T(8,128)S(1)} %copy-done.5, f32[2,4,128,128]{3,2,1,0:T(8,128)S(1)} %copy-done.1, f32[4,128,128]{2,1,0:T(8,128)S(1)} %copy-done.7, f32[2,4,128,128]{3,2,1,0:T(8,128)S(1)} %copy-done.3, ...), custom_call_target="tpu_custom_call" | custom-call | tf_op jit(solution)/shard_map/sweeps/pallas_call | solution.py:398
Async XLA Ops:
  0.6 1.0 %copy-start = (f32[2,4,128,128]{3,2,1,0:T(8,128)S(1)}, f32[2,4,128,128]{3,2,1,0:T(8,128)}, u32[]{:S(2)}) copy-start(f32[2,4,128,128]{3,2,1,0:T(8,128)} %d_ref.3) | copy-start | bytes 1572868
  1.7 1.0 %copy-start.2 = (f32[2,4,128,128]{3,2,1,0:T(8,128)S(1)}, f32[2,4,128,128]{3,2,1,0:T(8,128)}, u32[]{:S(2)}) copy-start(f32[2,4,128,128]{3,2,1,0:T(8,128)} %v_ref.3) | copy-start | bytes 1572868
  2.7 0.9 %copy-start.4 = (f32[4,128,128]{2,1,0:T(8,128)S(1)}, f32[4,128,128]{2,1,0:T(8,128)}, u32[]{:S(2)}) copy-start(f32[4,128,128]{2,1,0:T(8,128)} %h_ref.3) | copy-start | bytes 786436
  3.7 0.9 %copy-start.6 = (f32[4,128,128]{2,1,0:T(8,128)S(1)}, f32[4,128,128]{2,1,0:T(8,128)}, u32[]{:S(2)}) copy-start(f32[4,128,128]{2,1,0:T(8,128)} %f_ref.3) | copy-start | bytes 786436
  4.6 58.1 %copy-start.5 = (f32[4,128,128]{2,1,0:T(8,128)S(1)}, f32[4,128,128]{2,1,0:T(8,128)}, u32[]{:S(2)}) copy-start(f32[4,128,128]{2,1,0:T(8,128)} %h_ref.3) | copy-start | bytes 786436
  4.6 58.1 %copy-start.7 = (f32[4,128,128]{2,1,0:T(8,128)S(1)}, f32[4,128,128]{2,1,0:T(8,128)}, u32[]{:S(2)}) copy-start(f32[4,128,128]{2,1,0:T(8,128)} %f_ref.3) | copy-start | bytes 786436
  4.9 18.1 %collective-permute-start.3 = (f32[4,48,128]{2,1,0:T(8,128)S(1)}, f32[4,48,128]{2,1,0:T(8,128)S(1)}, u32[]{:S(2)}, u32[]{:S(2)}) collective-permute-start(f32[4,48,128]{2,1,0:T(8,128)S(1)} %get-tuple-element.9.refs_0_), channel_id=1, source_target_pairs={{0,12},{1,13},{2,14},{3,15},{4,16},{5,17},{6,18},{7,19},{8,20},{9,... | collective-permute-start | bytes 294920 | tf_op jit(solution)/shard_map/strides/ppermute | solution.py:34
  11.3 13.7 %collective-permute-start.2 = (f32[4,48,128]{2,1,0:T(8,128)S(1)}, f32[4,48,128]{2,1,0:T(8,128)S(1)}, u32[]{:S(2)}, u32[]{:S(2)}) collective-permute-start(f32[4,48,128]{2,1,0:T(8,128)S(1)} %get-tuple-element.9.refs_0_), channel_id=1, source_target_pairs={{0,9},{1,10},{2,11},{3,12},{4,13},{5,14},{6,15},{7,16},{8,17},{9,1... | collective-permute-start | bytes 294920 | tf_op jit(solution)/shard_map/strides/ppermute | solution.py:34
  13.3 14.8 %collective-permute-start.1 = (f32[4,48,128]{2,1,0:T(8,128)S(1)}, f32[4,48,128]{2,1,0:T(8,128)S(1)}, u32[]{:S(2)}, u32[]{:S(2)}) collective-permute-start(f32[4,48,128]{2,1,0:T(8,128)S(1)} %get-tuple-element.9.refs_0_), channel_id=1, source_target_pairs={{0,6},{1,7},{2,8},{3,9},{4,10},{5,11},{6,12},{7,13},{8,14},{9,15},... | collective-permute-start | bytes 294920 | tf_op jit(solution)/shard_map/strides/ppermute | solution.py:34
  14.5 21.8 %collective-permute-start = (f32[4,48,128]{2,1,0:T(8,128)S(1)}, f32[4,48,128]{2,1,0:T(8,128)S(1)}, u32[]{:S(2)}, u32[]{:S(2)}) collective-permute-start(f32[4,48,128]{2,1,0:T(8,128)S(1)} %get-tuple-element.9.refs_0_), channel_id=1, source_target_pairs={{0,3},{1,4},{2,5},{3,6},{4,7},{5,8},{6,9},{7,10},{8,11},{9,12},{10... | collective-permute-start | bytes 294920 | tf_op jit(solution)/shard_map/strides/ppermute | solution.py:34
  17.3 19.0 %collective-permute-start.7 = (f32[4,48,128]{2,1,0:T(8,128)S(1)}, f32[4,48,128]{2,1,0:T(8,128)S(1)}, u32[]{:S(2)}, u32[]{:S(2)}) collective-permute-start(f32[4,48,128]{2,1,0:T(8,128)S(1)} %get-tuple-element.10.refs_5_), channel_id=1, source_target_pairs={{0,116},{1,117},{2,118},{3,119},{4,120},{5,121},{6,122},{7,123},{8... | collective-permute-start | bytes 294920 | tf_op jit(solution)/shard_map/strides/ppermute | solution.py:34
  22.9 13.3 %collective-permute-start.6 = (f32[4,48,128]{2,1,0:T(8,128)S(1)}, f32[4,48,128]{2,1,0:T(8,128)S(1)}, u32[]{:S(2)}, u32[]{:S(2)}) collective-permute-start(f32[4,48,128]{2,1,0:T(8,128)S(1)} %get-tuple-element.10.refs_5_), channel_id=1, source_target_pairs={{0,119},{1,120},{2,121},{3,122},{4,123},{5,124},{6,125},{7,126},{8... | collective-permute-start | bytes 294920 | tf_op jit(solution)/shard_map/strides/ppermute | solution.py:34
  25.0 11.3 %collective-permute-start.5 = (f32[4,48,128]{2,1,0:T(8,128)S(1)}, f32[4,48,128]{2,1,0:T(8,128)S(1)}, u32[]{:S(2)}, u32[]{:S(2)}) collective-permute-start(f32[4,48,128]{2,1,0:T(8,128)S(1)} %get-tuple-element.10.refs_5_), channel_id=1, source_target_pairs={{0,122},{1,123},{2,124},{3,125},{4,126},{5,127},{6,0},{7,1},{8,2},... | collective-permute-start | bytes 294920 | tf_op jit(solution)/shard_map/strides/ppermute | solution.py:34
  28.1 10.7 %collective-permute-start.4 = (f32[4,48,128]{2,1,0:T(8,128)S(1)}, f32[4,48,128]{2,1,0:T(8,128)S(1)}, u32[]{:S(2)}, u32[]{:S(2)}) collective-permute-start(f32[4,48,128]{2,1,0:T(8,128)S(1)} %get-tuple-element.10.refs_5_), channel_id=1, source_target_pairs={{0,125},{1,126},{2,127},{3,0},{4,1},{5,2},{6,3},{7,4},{8,5},{9,6},... | collective-permute-start | bytes 294920 | tf_op jit(solution)/shard_map/strides/ppermute | solution.py:34
  38.7 0.7 copy-start.8
  39.4 23.3 %copy-start.1 = (f32[2,4,128,128]{3,2,1,0:T(8,128)S(1)}, f32[2,4,128,128]{3,2,1,0:T(8,128)}, u32[]{:S(2)}) copy-start(f32[2,4,128,128]{3,2,1,0:T(8,128)} %d_ref.3) | copy-start | bytes 1572868
  39.4 23.3 %copy-start.3 = (f32[2,4,128,128]{3,2,1,0:T(8,128)S(1)}, f32[2,4,128,128]{3,2,1,0:T(8,128)}, u32[]{:S(2)}) copy-start(f32[2,4,128,128]{3,2,1,0:T(8,128)} %v_ref.3) | copy-start | bytes 1572868
  43.4 11.6 %collective-permute-start.8 = (f32[608,128]{1,0:T(8,128)S(1)}, f32[608,128]{1,0:T(8,128)S(1)}, u32[]{:S(2)}, u32[]{:S(2)}) collective-permute-start(f32[608,128]{1,0:T(8,128)S(1)} %get-tuple-element.13), channel_id=1, source_target_pairs={{0,127},{1,0},{2,1},{3,2},{4,3},{5,4},{6,5},{7,6},{8,7},{9,8},{10,... | collective-permute-start | bytes 933896 | tf_op jit(solution)/shard_map/last_step/ppermute | solution.py:34
  50.2 12.4 %collective-permute-start.9 = (f32[608,128]{1,0:T(8,128)S(1)}, f32[608,128]{1,0:T(8,128)S(1)}, u32[]{:S(2)}, u32[]{:S(2)}) collective-permute-start(f32[608,128]{1,0:T(8,128)S(1)} %get-tuple-element.15), channel_id=1, source_target_pairs={{0,1},{1,2},{2,3},{3,4},{4,5},{5,6},{6,7},{7,8},{8,9},{9,10},{10,1... | collective-permute-start | bytes 933896 | tf_op jit(solution)/shard_map/last_step/ppermute | solution.py:34

commit v2 on v1

--- a/solution.py
+++ b/solution.py
@@ -27,6 +27,11 @@
 PACK = (MAIN_BLOCKS + 2) * STRIP
 FULL_PACK = PACK + TS
 VMEM_LIMIT = 40 * 1024 * 1024
+FIRST_VMEM_LIMIT = 60 * 1024 * 1024
+ROUTE = 3 * TPD * 2 * 3
+WHICH = ROUTE
+BITS = WHICH + 2 * TPD
+PLAN = 128
 
 
 def cyclic_shift(value, steps):
@@ -80,20 +85,47 @@
     return a, (-b if down else b)
 
 
-def strips_kernel(h_ref, d_ref, f_ref, v_ref, bottom_ref, top_ref, right_ref, left_ref):
-    fields = [v_ref.at[0], v_ref.at[1], h_ref, d_ref.at[0], d_ref.at[1], f_ref]
+def field_refs(h_ref, d_ref, f_ref, v_ref):
+    return [v_ref.at[0], v_ref.at[1], h_ref, d_ref.at[0], d_ref.at[1], f_ref]
+
+
+def put_strips(ends, bottom_ref, top_ref):
     row = lax.broadcasted_iota(jnp.int32, (SECTION, LANES), 0)
-    lane = lax.broadcasted_iota(jnp.int32, (TS, LANES), 1)
     for t in range(TPD):
-        for k, field in enumerate(fields):
-            last = field[t, TS - SECTION :, :]
-            first = field[t, :SECTION, :]
+        for k in range(6):
+            last = ends(k, t, slice(TS - SECTION, TS))
+            first = ends(k, t, slice(0, SECTION))
             if k in (3, 4):
-                extra = fields[k - 3]
-                last = jnp.where(row == 0, extra[t, TS - SECTION - 1 : TS - SECTION, :], last)
-                first = jnp.where(row == SECTION - 1, extra[t, SECTION : SECTION + 1, :], first)
+                last = jnp.where(row == 0, ends(k - 3, t, slice(TS - SECTION - 1, TS - SECTION)), last)
+                first = jnp.where(row == SECTION - 1, ends(k - 3, t, slice(SECTION, SECTION + 1)), first)
             bottom_ref[t, k * SECTION : (k + 1) * SECTION, :] = last
             top_ref[t, k * SECTION : (k + 1) * SECTION, :] = first
+
+
+def sent_strips_kernel(h_ref, d_ref, f_ref, v_ref, bottom_ref, top_ref, held, sems):
+    copies = []
+    for k, ref in enumerate(field_refs(h_ref, d_ref, f_ref, v_ref)):
+        copies += [
+            pltpu.make_async_copy(ref.at[:, pl.ds(0, 2 * SECTION)], held.at[0, k], sems.at[0, k]),
+            pltpu.make_async_copy(ref.at[:, pl.ds(TS - 2 * SECTION, 2 * SECTION)], held.at[1, k], sems.at[1, k]),
+        ]
+    for copy in copies:
+        copy.start()
+    for copy in copies:
+        copy.wait()
+
+    def ends(k, t, rows):
+        if rows.start < 2 * SECTION:
+            return held[0, k, t, rows, :]
+        return held[1, k, t, rows.start - TS + 2 * SECTION : rows.stop - TS + 2 * SECTION, :]
+
+    put_strips(ends, bottom_ref, top_ref)
+
+
+def own_strips_kernel(h_ref, d_ref, f_ref, v_ref, bottom_ref, top_ref, right_ref, left_ref):
+    fields = field_refs(h_ref, d_ref, f_ref, v_ref)
+    put_strips(lambda k, t, rows: fields[k][t, rows, :], bottom_ref, top_ref)
+    lane = lax.broadcasted_iota(jnp.int32, (TS, LANES), 1)
     right = jnp.zeros((TS, LANES), jnp.float32)
     left = jnp.zeros((TS, LANES), jnp.float32)
     for k, field in enumerate(fields):
@@ -104,68 +136,98 @@
     left_ref[...] = left
 
 
-def route_kernel(slots, len_ref, *refs):
+def plan_kernel(slots, len_ref, out_ref, plan_ref, ends_ref, sem):
+    ends = fill_row_ends(len_ref, ends_ref)
+    me, count = lax.axis_index("ta"), slots // TPD
+    for step in (-1, 0, 1):
+        device = lax.rem(me + step + count, count)
+        tiles = [Tile(len_ref, ends_ref, ends, device * TPD + j, slots) for j in range(TPD)]
+        for j, tile in enumerate(tiles):
+            for down in (0, 1):
+                for across in (-1, 0, 1):
+                    there, slot = tile.side(down, across)
+                    a, shift = hop(device, slot, down)
+                    entry = (((step + 1) * TPD + j) * 2 + down) * 3 + across + 1
+                    plan_ref[entry] = jnp.where(there & (shift == step), TPD * a + (slot & 3), -1)
+                    if step == 0 and across == 0:
+                        plan_ref[WHICH + down * TPD + j] = jnp.where(there, shift + 1, -1)
+        if step == 0:
+            for down in (0, 1):
+                plan_ref[BITS + down] = flag_bits([t.side(down, k)[0] for t in tiles for k in (-1, 1)])
+            plan_ref[BITS + 2] = flag_bits([flag for t in tiles for flag in (t.lower_x(), t.upper_x())])
+    for unused in range(BITS + 3, PLAN):
+        plan_ref[unused] = 0
+    copy = pltpu.make_async_copy(plan_ref, out_ref, sem)
+    copy.start()
+    copy.wait()
+
+
+def flag_bits(flags):
+    bits = jnp.int32(0)
+    for k, flag in enumerate(flags):
+        bits = bits + jnp.where(flag, 1 << k, 0)
+    return bits
+
+
+def own_fields_kernel(h_ref, d_ref, f_ref, v_ref, *outs):
+    group = lax.broadcasted_iota(jnp.int32, (TS, LANES), 1) >> 4
+    middle = slice(TOP, TOP + TS)
+    for ref, out in zip(field_refs(h_ref, d_ref, f_ref, v_ref), outs):
+        edges = None
+        for j in range(TPD):
+            tile = pltpu.roll(ref[j], 2 * MARGIN * j + MARGIN, 1)
+            out[j, middle, :] = tile
+            edges = tile if j == 0 else jnp.where((group >> 1) == j, tile, edges)
+        lower, upper = pltpu.roll(edges, 2 * MARGIN, 1), pltpu.roll(edges, LANES - 2 * MARGIN, 1)
+        out[TPD, middle, :] = jnp.where((group & 1) == 0, lower, upper)
+
+
+def route_kernel(plan_hbm, *refs):
     given = refs[: 2 * HOPS]
     right_ref, left_ref = refs[2 * HOPS : 2 * HOPS + 2]
     outs = refs[2 * HOPS + 2 : 2 * HOPS + 5]
-    strips, ends_ref, sems = refs[2 * HOPS + 5 :]
-    copies = [
-        pltpu.make_async_copy(given[i], strips.at[i // HOPS, i % HOPS], sems.at[i]) for i in range(2 * HOPS)
-    ]
-    for copy in copies:
-        copy.start()
-    ends = fill_row_ends(len_ref, ends_ref)
+    plan_ref, sem = refs[2 * HOPS + 5 :]
+    copy = pltpu.make_async_copy(plan_hbm, plan_ref, sem)
+    copy.start()
     outs[0][PACK:, :] = left_ref[...]
     outs[2][PACK:, :] = right_ref[...]
     for out in outs:
         out[MAIN_BLOCKS * STRIP : PACK, :] = jnp.zeros((2 * STRIP, LANES), jnp.float32)
     lane = lax.broadcasted_iota(jnp.int32, (STRIP, LANES), 1)
-    me, count = lax.axis_index("ta"), slots // TPD
-    for copy in copies:
-        copy.wait()
-    for step, out in zip((-1, 0, 1), outs):
-        device = lax.rem(me + step + count, count)
-        for j in range(TPD):
-            tile = Tile(len_ref, ends_ref, ends, device * TPD + j, slots)
-            for down in (0, 1):
-                for across in (-1, 0, 1):
-                    there, slot = tile.side(down, across)
-                    a, shift = hop(device, slot, down)
-
-                    @pl.when(there & (shift == step))
-                    def _(out=out, j=j, down=down, across=across, a=a, slot=slot):
-                        moved = pltpu.roll(strips[down, a, slot & 3], 2 * MARGIN * j + MARGIN, 1)
-                        if across == 0:
-                            block = down * TPD + j
-                            out[block * STRIP : (block + 1) * STRIP, :] = moved
-                        else:
-                            block = MAIN_BLOCKS + down
-                            first = 2 * j + (across + 1) // 2
-                            rows = slice(block * STRIP, (block + 1) * STRIP)
-                            out[rows, :] = jnp.where((lane >> 4) == first, moved, out[rows, :])
-
-
-def group_mask(flags, shape):
-    bits = jnp.int32(0)
-    for k, flag in enumerate(flags):
-        bits = bits + jnp.where(flag, 1 << k, 0)
+    copy.wait()
+    for step, out in enumerate(outs):
+        for down in (0, 1):
+            for across in (-1, 0, 1):
+
+                @pl.loop(0, TPD)
+                def _(j, step=step, out=out, down=down, across=across):
+                    source = plan_ref[((step * TPD + j) * 2 + down) * 3 + across + 1]
+
+                    @pl.when(source >= 0)
+                    def _():
+                        for a in range(HOPS):
+
+                            @pl.when((source >> 2) == a)
+                            def _():
+                                strip = given[down * HOPS + a][source & 3]
+                                moved = pltpu.roll(strip, 2 * MARGIN * j + MARGIN, 1)
+                                if across == 0:
+                                    out[pl.ds(pl.multiple_of((down * TPD + j) * STRIP, 8), STRIP), :] = moved
+                                else:
+                                    rows = slice((MAIN_BLOCKS + down) * STRIP, (MAIN_BLOCKS + down + 1) * STRIP)
+                                    here = (lane >> 4) == 2 * j + (across + 1) // 2
+                                    out[rows, :] = jnp.where(here, moved, out[rows, :])
+
+
+def group_mask(bits, shape):
     group = lax.broadcasted_iota(jnp.int32, shape, 1) >> 4
     return ((jnp.full(shape, bits) >> group) & 1) == 1
 
 
-def sweeps_kernel(
-    slots, len_ref, h_ref, d_ref, f_ref, v_ref, back_ref, local_ref, ahead_ref,
-    vel_ref, next_ref, u, v, u_other, v_other, w, h, d0, d1, f, ice,
-    u_low, u_high, v_low, v_high, results, packs, ends_ref, sems, out_sems,
-):
-    own = (pl.ds(0, TPD), pl.ds(TOP, TS))
+def sweeps_kernel(plan_ref, ahead_ref, local_ref, back_ref, *refs):
+    vel_ref, next_ref, u, v, h, d0, d1, f = refs[6:14]
+    u_other, v_other, w, ice, u_low, u_high, v_low, v_high, results, packs, sems, out_sems = refs[14:]
     copies = [
-        (v_ref.at[0], u.at[own]),
-        (v_ref.at[1], v.at[own]),
-        (h_ref, h.at[own]),
-        (d_ref.at[0], d0.at[own]),
-        (d_ref.at[1], d1.at[own]),
-        (f_ref, f.at[own]),
         (back_ref, packs.at[0]),
         (local_ref, packs.at[1, pl.ds(0, PACK)]),
         (ahead_ref, packs.at[2]),
@@ -173,9 +235,6 @@
     copies = [pltpu.make_async_copy(a, b, sems.at[i]) for i, (a, b) in enumerate(copies)]
     for copy in copies:
         copy.start()
-    me = lax.axis_index("ta")
-    ends = fill_row_ends(len_ref, ends_ref)
-    tiles = [Tile(len_ref, ends_ref, ends, me * TPD + j, slots) for j in range(TPD)]
     zero = jnp.zeros((SECTION, LANES), jnp.float32)
     one = jnp.ones((SECTION, LANES), jnp.float32)
     for block in range(TPD + 1):
@@ -195,9 +254,9 @@
         far = start + SECTION if down else start - 1
         for j in range(TPD + 1):
             if j < TPD:
-                there, slot = tiles[j].side(down, 0)
-                _, shift = hop(me, slot, down)
-                which = jnp.where(there, shift + 1, 1)
+                which = plan_ref[WHICH + down * TPD + j]
+                there = which >= 0
+                which = jnp.maximum(which, 0)
                 base = (down * TPD + j) * STRIP
                 parts = [packs[which, base + k * SECTION : base + (k + 1) * SECTION, :] for k in range(6)]
                 mask = jnp.full((SECTION, LANES), jnp.where(there, 1, 0)) == 1
@@ -209,8 +268,7 @@
                     + packs[2, base + k * SECTION : base + (k + 1) * SECTION, :]
                     for k in range(6)
                 ]
-                flags = [tile.side(down, across)[0] for tile in tiles for across in (-1, 1)]
-                mask = group_mask(flags, (SECTION, LANES))
+                mask = group_mask(plan_ref[BITS + down], (SECTION, LANES))
             for k, target in enumerate(targets):
                 target[j, rows, :] = jnp.where(mask, parts[k], one if k == 5 else zero)
             for k in (0, 1):
@@ -218,23 +276,15 @@
                 targets[k][j, far : far + 1, :] = line[deep : deep + 1, :]
             ice[j, rows, :] = jnp.where(mask, one, zero)
 
-    flags = [flag for tile in tiles for flag in (tile.lower_x(), tile.upper_x())]
-    mask = group_mask(flags, (TS, LANES))
-    lane = lax.broadcasted_iota(jnp.int32, (TS, LANES), 1)
-    group, group_pair = lane >> 4, lane >> 5
+    mask = group_mask(plan_ref[BITS + 2], (TS, LANES))
+    group = lax.broadcasted_iota(jnp.int32, (TS, LANES), 1) >> 4
     middle = slice(TOP, TOP + TS)
     ice[TPD, middle, :] = jnp.where(mask, 1.0, 0.0)
     for k, target in enumerate(targets):
-        edges = None
-        for j in range(TPD):
-            tile = pltpu.roll(target[j, middle, :], 2 * MARGIN * j + MARGIN, 1)
-            target[j, middle, :] = tile
-            edges = tile if j == 0 else jnp.where(group_pair == j, tile, edges)
         before = pltpu.roll(packs[2, PACK:, :], (LANES - MARGIN * k) % LANES, 1)
         after = pltpu.roll(packs[0, PACK:, :], (LANES - MARGIN - MARGIN * k) % LANES, 1)
-        lower = jnp.where(group == 0, before, pltpu.roll(edges, 2 * MARGIN, 1))
-        upper = jnp.where(group == 2 * TPD - 1, after, pltpu.roll(edges, LANES - 2 * MARGIN, 1))
-        beside = jnp.where((group & 1) == 0, lower, upper)
+        beside = jnp.where(group == 0, before, target[TPD, middle, :])
+        beside = jnp.where(group == 2 * TPD - 1, after, beside)
         target[TPD, middle, :] = jnp.where(mask, beside, 1.0 if k == 5 else 0.0)
 
     chunk = 72
@@ -356,63 +406,93 @@
     params = pltpu.CompilerParams(vmem_limit_bytes=VMEM_LIMIT)
     strips_shape = jax.ShapeDtypeStruct((TPD, STRIP, LANES), f32)
     columns_shape = jax.ShapeDtypeStruct((TS, LANES), f32)
+    field_shape = jax.ShapeDtypeStruct((TPD + 1, ROWS, LANES), f32)
+    pack_shape = jax.ShapeDtypeStruct((FULL_PACK, LANES), f32)
     rows = row_lengths.shape[0]
-
-    with jax.named_scope("strips"):
+    cost = pl.CostEstimate(flops=4_000_000, bytes_accessed=4_000_000, transcendentals=0)
+    given = (thickness, driving, friction, velocity_start)
+
+    with jax.named_scope("sent_strips"):
+        sent_bottom, sent_top = pl.pallas_call(
+            sent_strips_kernel,
+            out_shape=(strips_shape, strips_shape),
+            in_specs=[anywhere] * 4,
+            out_specs=(vmem,) * 2,
+            scratch_shapes=[
+                pltpu.VMEM((2, 6, TPD, 2 * SECTION, LANES), f32),
+                pltpu.SemaphoreType.DMA((2, 6)),
+            ],
+            compiler_params=pltpu.CompilerParams(vmem_limit_bytes=FIRST_VMEM_LIMIT),
+        )(*given)
+
+    with jax.named_scope("own_strips"):
         bottom, top, right, left = pl.pallas_call(
-            strips_kernel,
+            own_strips_kernel,
             out_shape=(strips_shape, strips_shape, columns_shape, columns_shape),
             in_specs=[vmem] * 4,
             out_specs=(vmem,) * 4,
+            cost_estimate=cost,
             compiler_params=params,
-        )(thickness, driving, friction, velocity_start)
+        )(*given)
+
+    with jax.named_scope("plan"):
+        plan = pl.pallas_call(
+            functools.partial(plan_kernel, slots),
+            out_shape=jax.ShapeDtypeStruct((PLAN,), jnp.int32),
+            in_specs=[smem],
+            out_specs=anywhere,
+            scratch_shapes=[pltpu.SMEM((PLAN,), jnp.int32), pltpu.SMEM((rows,), jnp.int32), pltpu.SemaphoreType.DMA],
+            cost_estimate=cost,
+        )(row_lengths)
+
+    with jax.named_scope("own_fields"):
+        fields = pl.pallas_call(
+            own_fields_kernel,
+            out_shape=(field_shape,) * 6,
+            in_specs=[vmem] * 4,
+            out_specs=(vmem,) * 6,
+            cost_estimate=cost,
+            compiler_params=params,
+        )(*given)
 
     with jax.named_scope("strides"):
-        bottoms = [bottom] + [cyclic_shift(bottom, STRIDE * a) for a in range(1, HOPS)]
-        tops = [top] + [cyclic_shift(top, -STRIDE * a) for a in range(1, HOPS)]
+        bottoms = [bottom] + [cyclic_shift(sent_bottom, STRIDE * a) for a in range(1, HOPS)]
+        tops = [top] + [cyclic_shift(sent_top, -STRIDE * a) for a in range(1, HOPS)]
 
     with jax.named_scope("route"):
         back, local, ahead = pl.pallas_call(
-            functools.partial(route_kernel, slots),
-            out_shape=(
-                jax.ShapeDtypeStruct((FULL_PACK, LANES), f32),
-                jax.ShapeDtypeStruct((PACK, LANES), f32),
-                jax.ShapeDtypeStruct((FULL_PACK, LANES), f32),
-            ),
-            in_specs=[smem] + [anywhere] * (2 * HOPS) + [vmem] * 2,
+            route_kernel,
+            out_shape=(pack_shape, jax.ShapeDtypeStruct((PACK, LANES), f32), pack_shape),
+            in_specs=[anywhere] + [vmem] * (2 * HOPS + 2),
             out_specs=(vmem,) * 3,
-            scratch_shapes=[
-                pltpu.VMEM((2, HOPS, TPD, STRIP, LANES), f32),
-                pltpu.SMEM((rows,), jnp.int32),
-                pltpu.SemaphoreType.DMA((2 * HOPS,)),
-            ],
+            scratch_shapes=[pltpu.SMEM((PLAN,), jnp.int32), pltpu.SemaphoreType.DMA],
             compiler_params=params,
-        )(row_lengths, *bottoms, *tops, right, left)
+        )(plan, *bottoms, *tops, right, left)
 
     with jax.named_scope("last_step"):
         back = cyclic_shift(back, -1)
         ahead = cyclic_shift(ahead, 1)
 
     with jax.named_scope("sweeps"):
-        field = pltpu.VMEM((TPD + 1, ROWS, LANES), f32)
-        velocity, thickness_next = pl.pallas_call(
-            functools.partial(sweeps_kernel, slots),
+        field = pltpu.VMEM(field_shape.shape, f32)
+        velocity, thickness_next, *_ = pl.pallas_call(
+            sweeps_kernel,
             out_shape=(
                 jax.ShapeDtypeStruct(velocity_start.shape, f32),
                 jax.ShapeDtypeStruct(thickness.shape, f32),
-            ),
-            in_specs=[smem] + [anywhere] * 7,
-            out_specs=(anywhere, anywhere),
+            ) + (field_shape,) * 6,
+            in_specs=[smem] + [anywhere] * 3 + [vmem] * 6,
+            out_specs=(anywhere, anywhere) + (vmem,) * 6,
+            input_output_aliases={4 + k: 2 + k for k in range(6)},
             scratch_shapes=[
-                *[field] * 14,
+                *[field] * 8,
                 pltpu.VMEM((3, TPD, TS, LANES), f32),
                 pltpu.VMEM((3, FULL_PACK, LANES), f32),
-                pltpu.SMEM((rows,), jnp.int32),
-                pltpu.SemaphoreType.DMA((9,)),
+                pltpu.SemaphoreType.DMA((3,)),
                 pltpu.SemaphoreType.DMA((3, TPD)),
             ],
             compiler_params=params,
-        )(row_lengths, thickness, driving, friction, velocity_start, back, local, ahead)
+        )(plan, ahead, local, back, *fields)
     return velocity, thickness_next
 
 

time: 73.9 us -> 63.3 us (0.86)
  waiting for transfers between devices: 21.5 us -> 11.7 us
  local copies, waits for them, and re-layouts: 4.65 us -> 0.69 us
  Pallas kernels: 15.1 us -> 17.8 us
    ppermute x10, waiting for transfers between devices: 21.5 us -> 11.7 us  [cyclic_shift(): lax.ppermute(value, 'ta', [(i, (i + steps) % count) for i in range(count)])]
    unnamed x18 -> x10, local copies, waits for them, and re-layouts: 4.65 us -> 0.69 us
    pallas_call x3 -> x6, Pallas kernels: 15.1 us -> 17.8 us  [the longest x1 9.85 us: shards(): pl.pallas_call(sweeps_kernel, out_shape=(jax.ShapeDtypeStruct(velocity_st...]
  transfers between devices with their start and end apart: 10 -> 10, of which waited for: 4 -> 3; matrix products, arithmetic and copies ran while one was open for 0% -> 0% of each run, Pallas kernels for 0% -> 5%
where the time goes in v2:
time: 63.3 us; the launch traced here: 63.2 us
  starting transfers between devices  32.3 us (51%)
  Pallas kernels  17.8 us (28%)
  waiting for transfers between devices  11.7 us (18%)
  between operations  0.72 us (1%)
  local copies, waits for them, and re-layouts  0.69 us (1%)
    ppermute x10, starting transfers between devices, cyclic_shift(): lax.ppermute(value, 'ta', [(i, (i + steps) % count) for i in range(count)])  32.3 us
    ppermute x10, waiting for transfers between devices, cyclic_shift(): lax.ppermute(value, 'ta', [(i, (i + steps) % count) for i in range(count)])  11.7 us
    pallas_call x1, Pallas kernels, shards(): pl.pallas_call(sweeps_kernel, out_shape=(jax.ShapeDtypeStruct(velocity_st...  9.85 us
    pallas_call x1, Pallas kernels, shards(): pl.pallas_call(route_kernel, out_shape=(pack_shape, jax.ShapeDtypeStruct(...  2.68 us
    pallas_call x1, Pallas kernels, shards(): pl.pallas_call(functools.partial(plan_kernel, slots), out_shape=jax.Shape...  2.18 us
    pallas_call x1, Pallas kernels, shards(): pl.pallas_call(sent_strips_kernel, out_shape=(strips_shape, strips_shape)...  1.84 us
  transfers between devices with their start and end apart: 10, of which 3 were waited for; matrix products, arithmetic and copies ran while one was open for 0% of the time, Pallas kernels for 5%

profile of v2, /device:TPU:0, one launch (start us, length us, event | category | flops | bytes accessed | tf_op | source)
XLA Modules:
  0.0 63.2 jit_solution(1534246172998444323)
XLA Ops:
  0.6 0.0 copy-start.1
  0.6 0.0 copy-start.3
  0.7 0.0 copy-start
  0.7 0.0 copy-start.2
  0.7 1.8 %sent_strips.1 = (f32[4,48,128]{2,1,0:T(8,128)}, f32[4,48,128]{2,1,0:T(8,128)}) custom-call(f32[4,128,128]{2,1,0:T(8,128)} %h_ref.5, f32[2,4,128,128]{3,2,1,0:T(8,128)} %d_ref.5, f32[4,128,128]{2,1,0:T(8,128)} %f_ref.5, f32[2,4,128,128]{3,2,1,0:T(8,128)} %v_ref.5), custom_call_target="tpu_custom_call" | custom-call | tf_op jit(solution)/shard_map/sent_strips/pallas_call | solution.py:416
  2.5 6.5 %collective-permute-start.3 = (f32[4,48,128]{2,1,0:T(8,128)}, f32[4,48,128]{2,1,0:T(8,128)S(1)}, u32[]{:S(2)}, u32[]{:S(2)}) collective-permute-start(f32[4,48,128]{2,1,0:T(8,128)} %get-tuple-element.20), channel_id=1, source_target_pairs={{0,12},{1,13},{2,14},{3,15},{4,16},{5,17},{6,18},{7,19},{8,20},{9,... | collective-permute-start | bytes 294920 | tf_op jit(solution)/shard_map/strides/ppermute | solution.py:39
  9.0 1.9 %collective-permute-start.2 = (f32[4,48,128]{2,1,0:T(8,128)}, f32[4,48,128]{2,1,0:T(8,128)S(1)}, u32[]{:S(2)}, u32[]{:S(2)}) collective-permute-start(f32[4,48,128]{2,1,0:T(8,128)} %get-tuple-element.20), channel_id=1, source_target_pairs={{0,9},{1,10},{2,11},{3,12},{4,13},{5,14},{6,15},{7,16},{8,17},{9,1... | collective-permute-start | bytes 294920 | tf_op jit(solution)/shard_map/strides/ppermute | solution.py:39
  10.9 1.2 %collective-permute-start.1 = (f32[4,48,128]{2,1,0:T(8,128)}, f32[4,48,128]{2,1,0:T(8,128)S(1)}, u32[]{:S(2)}, u32[]{:S(2)}) collective-permute-start(f32[4,48,128]{2,1,0:T(8,128)} %get-tuple-element.20), channel_id=1, source_target_pairs={{0,6},{1,7},{2,8},{3,9},{4,10},{5,11},{6,12},{7,13},{8,14},{9,15},... | collective-permute-start | bytes 294920 | tf_op jit(solution)/shard_map/strides/ppermute | solution.py:39
  12.1 2.8 %collective-permute-start = (f32[4,48,128]{2,1,0:T(8,128)}, f32[4,48,128]{2,1,0:T(8,128)S(1)}, u32[]{:S(2)}, u32[]{:S(2)}) collective-permute-start(f32[4,48,128]{2,1,0:T(8,128)} %get-tuple-element.20), channel_id=1, source_target_pairs={{0,3},{1,4},{2,5},{3,6},{4,7},{5,8},{6,9},{7,10},{8,11},{9,12},{10... | collective-permute-start | bytes 294920 | tf_op jit(solution)/shard_map/strides/ppermute | solution.py:39
  14.9 5.6 %collective-permute-start.7 = (f32[4,48,128]{2,1,0:T(8,128)}, f32[4,48,128]{2,1,0:T(8,128)S(1)}, u32[]{:S(2)}, u32[]{:S(2)}) collective-permute-start(f32[4,48,128]{2,1,0:T(8,128)} %get-tuple-element.22), channel_id=1, source_target_pairs={{0,116},{1,117},{2,118},{3,119},{4,120},{5,121},{6,122},{7,123},{8... | collective-permute-start | bytes 294920 | tf_op jit(solution)/shard_map/strides/ppermute | solution.py:39
  20.6 0.0 collective-permute-done.3.refs_4_
  20.6 2.3 %collective-permute-start.6 = (f32[4,48,128]{2,1,0:T(8,128)}, f32[4,48,128]{2,1,0:T(8,128)S(1)}, u32[]{:S(2)}, u32[]{:S(2)}) collective-permute-start(f32[4,48,128]{2,1,0:T(8,128)} %get-tuple-element.22), channel_id=1, source_target_pairs={{0,119},{1,120},{2,121},{3,122},{4,123},{5,124},{6,125},{7,126},{8... | collective-permute-start | bytes 294920 | tf_op jit(solution)/shard_map/strides/ppermute | solution.py:39
  22.8 0.0 collective-permute-done.2.refs_3_
  22.8 3.0 %collective-permute-start.5 = (f32[4,48,128]{2,1,0:T(8,128)}, f32[4,48,128]{2,1,0:T(8,128)S(1)}, u32[]{:S(2)}, u32[]{:S(2)}) collective-permute-start(f32[4,48,128]{2,1,0:T(8,128)} %get-tuple-element.22), channel_id=1, source_target_pairs={{0,122},{1,123},{2,124},{3,125},{4,126},{5,127},{6,0},{7,1},{8,2},... | collective-permute-start | bytes 294920 | tf_op jit(solution)/shard_map/strides/ppermute | solution.py:39
  25.9 0.0 collective-permute-done.1.refs_2_
  25.9 1.5 %collective-permute-start.4 = (f32[4,48,128]{2,1,0:T(8,128)}, f32[4,48,128]{2,1,0:T(8,128)S(1)}, u32[]{:S(2)}, u32[]{:S(2)}) collective-permute-start(f32[4,48,128]{2,1,0:T(8,128)} %get-tuple-element.22), channel_id=1, source_target_pairs={{0,125},{1,126},{2,127},{3,0},{4,1},{5,2},{6,3},{7,4},{8,5},{9,6},... | collective-permute-start | bytes 294920 | tf_op jit(solution)/shard_map/strides/ppermute | solution.py:39
  27.3 0.0 copy-done.1
  27.3 0.0 copy-done.3
  27.3 0.0 copy-done
  27.3 0.0 copy-done.2
  27.3 0.3 own_strips.1
  27.6 2.2 %plan.1.plan_hbm.plan_ref = s32[128]{0:T(128)} custom-call(s32[22]{0:T(128)} %len_ref.1), custom_call_target="tpu_custom_call" | custom-call | flops 4000000 | bytes 4000000 | tf_op jit(solution)/shard_map/plan/pallas_call | solution.py:439
  29.8 4.3 %collective-permute-done.refs_1_ = f32[4,48,128]{2,1,0:T(8,128)S(1)} collective-permute-done((f32[4,48,128]{2,1,0:T(8,128)}, f32[4,48,128]{2,1,0:T(8,128)S(1)}, u32[]{:S(2)}, u32[]{:S(2)}) %collective-permute-start) | collective-permute-done | bytes 98336 | tf_op jit(solution)/shard_map/strides/ppermute | solution.py:39
  34.1 0.0 collective-permute-done.7.refs_9_
  34.1 0.0 collective-permute-done.6.refs_8_
  34.1 0.0 collective-permute-done.5.refs_7_
  34.1 2.9 %collective-permute-done.4.refs_6_ = f32[4,48,128]{2,1,0:T(8,128)S(1)} collective-permute-done((f32[4,48,128]{2,1,0:T(8,128)}, f32[4,48,128]{2,1,0:T(8,128)S(1)}, u32[]{:S(2)}, u32[]{:S(2)}) %collective-permute-start.4) | collective-permute-done | bytes 98336 | tf_op jit(solution)/shard_map/strides/ppermute | solution.py:39
  37.0 0.0 copy-start.4
  37.0 0.7 %copy-done.4 = s32[128]{0:T(128)S(1)} copy-done((s32[128]{0:T(128)S(1)}, s32[128]{0:T(128)}, u32[]{:S(2)}) %copy-start.4) | copy-done | bytes 536
  37.7 2.7 %route.1 = (f32[608,128]{1,0:T(8,128)S(1)}, f32[480,128]{1,0:T(8,128)S(1)}, f32[608,128]{1,0:T(8,128)S(1)}) custom-call(s32[128]{0:T(128)S(1)} %copy-done.4, f32[4,48,128]{2,1,0:T(8,128)S(1)} %get-tuple-element.19.refs_0_, f32[4,48,128]{2,1,0:T(8,128)S(1)} %collective-permute-done.refs_1_, f32[4,48,128]{2,1,0:T(8,128)S(1)} %collective-permute-done.1.refs_2_, ...), custom_call_target="tpu_custom_call" | custom-call | tf_op jit(solution)/shard_map/route/pallas_call | solution.py:463
  40.4 0.9 %collective-permute-start.8 = (f32[608,128]{1,0:T(8,128)S(1)}, f32[608,128]{1,0:T(8,128)S(1)}, u32[]{:S(2)}, u32[]{:S(2)}) collective-permute-start(f32[608,128]{1,0:T(8,128)S(1)} %get-tuple-element.25), channel_id=1, source_target_pairs={{0,1},{1,2},{2,3},{3,4},{4,5},{5,6},{6,7},{7,8},{8,9},{9,10},{10,1... | collective-permute-start | bytes 933896 | tf_op jit(solution)/shard_map/last_step/ppermute | solution.py:39
  41.3 6.6 %collective-permute-start.9 = (f32[608,128]{1,0:T(8,128)S(1)}, f32[608,128]{1,0:T(8,128)S(1)}, u32[]{:S(2)}, u32[]{:S(2)}) collective-permute-start(f32[608,128]{1,0:T(8,128)S(1)} %get-tuple-element.27), channel_id=1, source_target_pairs={{0,127},{1,0},{2,1},{3,2},{4,3},{5,4},{6,5},{7,6},{8,7},{9,8},{10,... | collective-permute-start | bytes 933896 | tf_op jit(solution)/shard_map/last_step/ppermute | solution.py:39
  47.9 1.0 %own_fields.1 = (f32[5,160,128]{2,1,0:T(8,128)S(1)}, f32[5,160,128]{2,1,0:T(8,128)S(1)}, f32[5,160,128]{2,1,0:T(8,128)S(1)}, f32[5,160,128]{2,1,0:T(8,128)S(1)},...) custom-call(f32[4,128,128]{2,1,0:T(8,128)S(1)} %copy-done.2, f32[2,4,128,128]{3,2,1,0:T(8,128)S(1)} %copy-done, ...), custom_call_target="tpu_custom_call" | custom-call | flops 4000000 | bytes 4000000 | tf_op jit(solution)/shard_map/own_fields/pallas_call | solution.py:449
  48.9 4.5 %collective-permute-done.8.ahead_ref = f32[608,128]{1,0:T(8,128)S(1)} collective-permute-done((f32[608,128]{1,0:T(8,128)S(1)}, f32[608,128]{1,0:T(8,128)S(1)}, u32[]{:S(2)}, u32[]{:S(2)}) %collective-permute-start.8) | collective-permute-done | bytes 311328 | tf_op jit(solution)/shard_map/last_step/ppermute | solution.py:39
  53.4 0.0 collective-permute-done.9.back_ref
  53.4 9.8 %sweeps.1 = (f32[2,4,128,128]{3,2,1,0:T(8,128)}, f32[4,128,128]{2,1,0:T(8,128)}, f32[5,160,128]{2,1,0:T(8,128)S(1)}, f32[5,160,128]{2,1,0:T(8,128)S(1)}, f32[5,1...) custom-call(s32[128]{0:T(128)S(1)} %copy-done.4, ...), custom_call_target="tpu_custom_call", output_to_operand_aliasing={{2}: (4, {}), {3}: (5, {}), {4}: (6, {}), {5}: (7, {}), {6}... | custom-call | tf_op jit(solution)/shard_map/sweeps/pallas_call | solution.py:478
Async XLA Ops:
  0.6 26.7 %copy-start.1 = (f32[2,4,128,128]{3,2,1,0:T(8,128)S(1)}, f32[2,4,128,128]{3,2,1,0:T(8,128)}, u32[]{:S(2)}) copy-start(f32[2,4,128,128]{3,2,1,0:T(8,128)} %v_ref.5) | copy-start | bytes 1572868
  0.6 26.7 %copy-start.3 = (f32[4,128,128]{2,1,0:T(8,128)S(1)}, f32[4,128,128]{2,1,0:T(8,128)}, u32[]{:S(2)}) copy-start(f32[4,128,128]{2,1,0:T(8,128)} %f_ref.5) | copy-start | bytes 786436
  0.7 26.7 %copy-start = (f32[2,4,128,128]{3,2,1,0:T(8,128)S(1)}, f32[2,4,128,128]{3,2,1,0:T(8,128)}, u32[]{:S(2)}) copy-start(f32[2,4,128,128]{3,2,1,0:T(8,128)} %d_ref.5) | copy-start | bytes 1572868
  0.7 26.7 %copy-start.2 = (f32[4,128,128]{2,1,0:T(8,128)S(1)}, f32[4,128,128]{2,1,0:T(8,128)}, u32[]{:S(2)}) copy-start(f32[4,128,128]{2,1,0:T(8,128)} %h_ref.5) | copy-start | bytes 786436
  2.5 18.1 %collective-permute-start.3 = (f32[4,48,128]{2,1,0:T(8,128)}, f32[4,48,128]{2,1,0:T(8,128)S(1)}, u32[]{:S(2)}, u32[]{:S(2)}) collective-permute-start(f32[4,48,128]{2,1,0:T(8,128)} %get-tuple-element.20), channel_id=1, source_target_pairs={{0,12},{1,13},{2,14},{3,15},{4,16},{5,17},{6,18},{7,19},{8,20},{9,... | collective-permute-start | bytes 294920 | tf_op jit(solution)/shard_map/strides/ppermute | solution.py:39
  9.0 13.9 %collective-permute-start.2 = (f32[4,48,128]{2,1,0:T(8,128)}, f32[4,48,128]{2,1,0:T(8,128)S(1)}, u32[]{:S(2)}, u32[]{:S(2)}) collective-permute-start(f32[4,48,128]{2,1,0:T(8,128)} %get-tuple-element.20), channel_id=1, source_target_pairs={{0,9},{1,10},{2,11},{3,12},{4,13},{5,14},{6,15},{7,16},{8,17},{9,1... | collective-permute-start | bytes 294920 | tf_op jit(solution)/shard_map/strides/ppermute | solution.py:39
  10.9 14.9 %collective-permute-start.1 = (f32[4,48,128]{2,1,0:T(8,128)}, f32[4,48,128]{2,1,0:T(8,128)S(1)}, u32[]{:S(2)}, u32[]{:S(2)}) collective-permute-start(f32[4,48,128]{2,1,0:T(8,128)} %get-tuple-element.20), channel_id=1, source_target_pairs={{0,6},{1,7},{2,8},{3,9},{4,10},{5,11},{6,12},{7,13},{8,14},{9,15},... | collective-permute-start | bytes 294920 | tf_op jit(solution)/shard_map/strides/ppermute | solution.py:39
  12.1 22.0 %collective-permute-start = (f32[4,48,128]{2,1,0:T(8,128)}, f32[4,48,128]{2,1,0:T(8,128)S(1)}, u32[]{:S(2)}, u32[]{:S(2)}) collective-permute-start(f32[4,48,128]{2,1,0:T(8,128)} %get-tuple-element.20), channel_id=1, source_target_pairs={{0,3},{1,4},{2,5},{3,6},{4,7},{5,8},{6,9},{7,10},{8,11},{9,12},{10... | collective-permute-start | bytes 294920 | tf_op jit(solution)/shard_map/strides/ppermute | solution.py:39
  14.9 19.2 %collective-permute-start.7 = (f32[4,48,128]{2,1,0:T(8,128)}, f32[4,48,128]{2,1,0:T(8,128)S(1)}, u32[]{:S(2)}, u32[]{:S(2)}) collective-permute-start(f32[4,48,128]{2,1,0:T(8,128)} %get-tuple-element.22), channel_id=1, source_target_pairs={{0,116},{1,117},{2,118},{3,119},{4,120},{5,121},{6,122},{7,123},{8... | collective-permute-start | bytes 294920 | tf_op jit(solution)/shard_map/strides/ppermute | solution.py:39
  20.6 13.6 %collective-permute-start.6 = (f32[4,48,128]{2,1,0:T(8,128)}, f32[4,48,128]{2,1,0:T(8,128)S(1)}, u32[]{:S(2)}, u32[]{:S(2)}) collective-permute-start(f32[4,48,128]{2,1,0:T(8,128)} %get-tuple-element.22), channel_id=1, source_target_pairs={{0,119},{1,120},{2,121},{3,122},{4,123},{5,124},{6,125},{7,126},{8... | collective-permute-start | bytes 294920 | tf_op jit(solution)/shard_map/strides/ppermute | solution.py:39
  22.8 11.3 %collective-permute-start.5 = (f32[4,48,128]{2,1,0:T(8,128)}, f32[4,48,128]{2,1,0:T(8,128)S(1)}, u32[]{:S(2)}, u32[]{:S(2)}) collective-permute-start(f32[4,48,128]{2,1,0:T(8,128)} %get-tuple-element.22), channel_id=1, source_target_pairs={{0,122},{1,123},{2,124},{3,125},{4,126},{5,127},{6,0},{7,1},{8,2},... | collective-permute-start | bytes 294920 | tf_op jit(solution)/shard_map/strides/ppermute | solution.py:39
  25.9 11.1 %collective-permute-start.4 = (f32[4,48,128]{2,1,0:T(8,128)}, f32[4,48,128]{2,1,0:T(8,128)S(1)}, u32[]{:S(2)}, u32[]{:S(2)}) collective-permute-start(f32[4,48,128]{2,1,0:T(8,128)} %get-tuple-element.22), channel_id=1, source_target_pairs={{0,125},{1,126},{2,127},{3,0},{4,1},{5,2},{6,3},{7,4},{8,5},{9,6},... | collective-permute-start | bytes 294920 | tf_op jit(solution)/shard_map/strides/ppermute | solution.py:39
  37.0 0.7 %copy-start.4 = (s32[128]{0:T(128)S(1)}, s32[128]{0:T(128)}, u32[]{:S(2)}) copy-start(s32[128]{0:T(128)} %plan.1.plan_hbm.plan_ref) | copy-start | bytes 1540
  40.4 13.0 %collective-permute-start.8 = (f32[608,128]{1,0:T(8,128)S(1)}, f32[608,128]{1,0:T(8,128)S(1)}, u32[]{:S(2)}, u32[]{:S(2)}) collective-permute-start(f32[608,128]{1,0:T(8,128)S(1)} %get-tuple-element.25), channel_id=1, source_target_pairs={{0,1},{1,2},{2,3},{3,4},{4,5},{5,6},{6,7},{7,8},{8,9},{9,10},{10,1... | collective-permute-start | bytes 933896 | tf_op jit(solution)/shard_map/last_step/ppermute | solution.py:39
  41.3 12.0 %collective-permute-start.9 = (f32[608,128]{1,0:T(8,128)S(1)}, f32[608,128]{1,0:T(8,128)S(1)}, u32[]{:S(2)}, u32[]{:S(2)}) collective-permute-start(f32[608,128]{1,0:T(8,128)S(1)} %get-tuple-element.27), channel_id=1, source_target_pairs={{0,127},{1,0},{2,1},{3,2},{4,3},{5,4},{6,5},{7,6},{8,7},{9,8},{10,... | collective-permute-start | bytes 933896 | tf_op jit(solution)/shard_map/last_step/ppermute | solution.py:39

commit v3 on v2

--- a/solution.py
+++ b/solution.py
@@ -25,7 +25,9 @@
 HOPS = 5
 MAIN_BLOCKS = 2 * TPD
 PACK = (MAIN_BLOCKS + 2) * STRIP
-FULL_PACK = PACK + TS
+GROUP = 10
+HALF = TS // 2
+FULL_PACK = PACK + HALF
 VMEM_LIMIT = 40 * 1024 * 1024
 FIRST_VMEM_LIMIT = 60 * 1024 * 1024
 ROUTE = 3 * TPD * 2 * 3
@@ -125,13 +127,15 @@
 def own_strips_kernel(h_ref, d_ref, f_ref, v_ref, bottom_ref, top_ref, right_ref, left_ref):
     fields = field_refs(h_ref, d_ref, f_ref, v_ref)
     put_strips(lambda k, t, rows: fields[k][t, rows, :], bottom_ref, top_ref)
-    lane = lax.broadcasted_iota(jnp.int32, (TS, LANES), 1)
-    right = jnp.zeros((TS, LANES), jnp.float32)
-    left = jnp.zeros((TS, LANES), jnp.float32)
+    lane = lax.broadcasted_iota(jnp.int32, (HALF, LANES), 1)
+    right = left = jnp.zeros((HALF, LANES), jnp.float32)
     for k, field in enumerate(fields):
-        here = (lane >> 4) == k
-        right = jnp.where(here, pltpu.roll(field[TPD - 1], (MARGIN * k + MARGIN) % LANES, 1), right)
-        left = jnp.where(here, pltpu.roll(field[0], MARGIN * k, 1) if k else field[0], left)
+        for half in (0, 1):
+            start = half * HALF + k * GROUP
+            here = (lane >= start) & (lane < start + GROUP)
+            rows = slice(half * HALF, (half + 1) * HALF)
+            right = jnp.where(here, pltpu.roll(field[TPD - 1, rows, :], (start + GROUP) % LANES, 1), right)
+            left = jnp.where(here, pltpu.roll(field[0, rows, :], start, 1) if start else field[0, rows, :], left)
     right_ref[...] = right
     left_ref[...] = left
 
@@ -148,15 +152,15 @@
                     there, slot = tile.side(down, across)
                     a, shift = hop(device, slot, down)
                     entry = (((step + 1) * TPD + j) * 2 + down) * 3 + across + 1
-                    plan_ref[entry] = jnp.where(there & (shift == step), TPD * a + (slot & 3), -1)
+                    plan_ref[0, entry] = jnp.where(there & (shift == step), TPD * a + (slot & 3), -1)
                     if step == 0 and across == 0:
-                        plan_ref[WHICH + down * TPD + j] = jnp.where(there, shift + 1, -1)
+                        plan_ref[0, WHICH + down * TPD + j] = jnp.where(there, shift + 1, -1)
         if step == 0:
             for down in (0, 1):
-                plan_ref[BITS + down] = flag_bits([t.side(down, k)[0] for t in tiles for k in (-1, 1)])
-            plan_ref[BITS + 2] = flag_bits([flag for t in tiles for flag in (t.lower_x(), t.upper_x())])
+                plan_ref[0, BITS + down] = flag_bits([t.side(down, k)[0] for t in tiles for k in (-1, 1)])
+            plan_ref[0, BITS + 2] = flag_bits([flag for t in tiles for flag in (t.lower_x(), t.upper_x())])
     for unused in range(BITS + 3, PLAN):
-        plan_ref[unused] = 0
+        plan_ref[0, unused] = 0
     copy = pltpu.make_async_copy(plan_ref, out_ref, sem)
     copy.start()
     copy.wait()
@@ -182,12 +186,12 @@
         out[TPD, middle, :] = jnp.where((group & 1) == 0, lower, upper)
 
 
-def route_kernel(plan_hbm, *refs):
+def route_kernel(given_plan, *refs):
     given = refs[: 2 * HOPS]
     right_ref, left_ref = refs[2 * HOPS : 2 * HOPS + 2]
     outs = refs[2 * HOPS + 2 : 2 * HOPS + 5]
     plan_ref, sem = refs[2 * HOPS + 5 :]
-    copy = pltpu.make_async_copy(plan_hbm, plan_ref, sem)
+    copy = pltpu.make_async_copy(given_plan, plan_ref, sem)
     copy.start()
     outs[0][PACK:, :] = left_ref[...]
     outs[2][PACK:, :] = right_ref[...]
@@ -201,7 +205,7 @@
 
                 @pl.loop(0, TPD)
                 def _(j, step=step, out=out, down=down, across=across):
-                    source = plan_ref[((step * TPD + j) * 2 + down) * 3 + across + 1]
+                    source = plan_ref[0, ((step * TPD + j) * 2 + down) * 3 + across + 1]
 
                     @pl.when(source >= 0)
                     def _():
@@ -224,17 +228,12 @@
     return ((jnp.full(shape, bits) >> group) & 1) == 1
 
 
-def sweeps_kernel(plan_ref, ahead_ref, local_ref, back_ref, *refs):
+def sweeps_kernel(given_plan, ahead_ref, local_ref, back_ref, *refs):
     vel_ref, next_ref, u, v, h, d0, d1, f = refs[6:14]
-    u_other, v_other, w, ice, u_low, u_high, v_low, v_high, results, packs, sems, out_sems = refs[14:]
-    copies = [
-        (back_ref, packs.at[0]),
-        (local_ref, packs.at[1, pl.ds(0, PACK)]),
-        (ahead_ref, packs.at[2]),
-    ]
-    copies = [pltpu.make_async_copy(a, b, sems.at[i]) for i, (a, b) in enumerate(copies)]
-    for copy in copies:
-        copy.start()
+    u_other, v_other, w, ice, u_low, u_high, v_low, v_high, results, out_sems, plan_ref, sem = refs[14:]
+    plan_copy = pltpu.make_async_copy(given_plan, plan_ref, sem)
+    plan_copy.start()
+    packs = (back_ref, local_ref, ahead_ref)
     zero = jnp.zeros((SECTION, LANES), jnp.float32)
     one = jnp.ones((SECTION, LANES), jnp.float32)
     for block in range(TPD + 1):
@@ -243,8 +242,9 @@
             u[block, rows, :] = zero
             v[block, rows, :] = zero
             w[block, rows, :] = zero
-    for copy in copies:
-        copy.wait()
+    for j in range(TPD):
+        ice[j, TOP : TOP + TS, :] = jnp.ones((TS, LANES), jnp.float32)
+    plan_copy.wait()
 
     targets = (u, v, h, d0, d1, f)
     for down in (0, 1):
@@ -252,42 +252,52 @@
         rows = slice(start, start + SECTION)
         deep = SECTION - 1 if down else 0
         far = start + SECTION if down else start - 1
-        for j in range(TPD + 1):
-            if j < TPD:
-                which = plan_ref[WHICH + down * TPD + j]
-                there = which >= 0
-                which = jnp.maximum(which, 0)
-                base = (down * TPD + j) * STRIP
-                parts = [packs[which, base + k * SECTION : base + (k + 1) * SECTION, :] for k in range(6)]
-                mask = jnp.full((SECTION, LANES), jnp.where(there, 1, 0)) == 1
-            else:
-                base = (MAIN_BLOCKS + down) * STRIP
-                parts = [
-                    packs[0, base + k * SECTION : base + (k + 1) * SECTION, :]
-                    + packs[1, base + k * SECTION : base + (k + 1) * SECTION, :]
-                    + packs[2, base + k * SECTION : base + (k + 1) * SECTION, :]
-                    for k in range(6)
-                ]
-                mask = group_mask(plan_ref[BITS + down], (SECTION, LANES))
+
+        def put(j, parts, mask=None, rows=rows, deep=deep, far=far):
             for k, target in enumerate(targets):
-                target[j, rows, :] = jnp.where(mask, parts[k], one if k == 5 else zero)
+                target[j, rows, :] = parts[k] if mask is None else jnp.where(mask, parts[k], one if k == 5 else zero)
             for k in (0, 1):
-                line = jnp.where(mask, parts[3 + k], zero)
+                line = parts[3 + k] if mask is None else jnp.where(mask, parts[3 + k], zero)
                 targets[k][j, far : far + 1, :] = line[deep : deep + 1, :]
-            ice[j, rows, :] = jnp.where(mask, one, zero)
-
-    mask = group_mask(plan_ref[BITS + 2], (TS, LANES))
+
+        def sections(pack, block):
+            return [pack[block * STRIP + k * SECTION : block * STRIP + (k + 1) * SECTION, :] for k in range(6)]
+
+        for j in range(TPD):
+            which = plan_ref[0, WHICH + down * TPD + j]
+            for index, pack in enumerate(packs):
+
+                @pl.when(which == index)
+                def _(j=j, pack=pack, down=down, put=put, sections=sections, rows=rows):
+                    put(j, sections(pack, down * TPD + j))
+                    ice[j, rows, :] = one
+
+            @pl.when(which < 0)
+            def _(j=j, put=put, rows=rows):
+                put(j, [zero] * 5 + [one])
+                ice[j, rows, :] = zero
+
+        mask = group_mask(plan_ref[0, BITS + down], (SECTION, LANES))
+        parts = [sum(part) for part in zip(*[sections(pack, MAIN_BLOCKS + down) for pack in packs])]
+        put(TPD, parts, mask)
+        ice[TPD, rows, :] = jnp.where(mask, one, zero)
+
+    mask = group_mask(plan_ref[0, BITS + 2], (TS, LANES))
     group = lax.broadcasted_iota(jnp.int32, (TS, LANES), 1) >> 4
     middle = slice(TOP, TOP + TS)
     ice[TPD, middle, :] = jnp.where(mask, 1.0, 0.0)
+    group = group[:HALF]
     for k, target in enumerate(targets):
-        before = pltpu.roll(packs[2, PACK:, :], (LANES - MARGIN * k) % LANES, 1)
-        after = pltpu.roll(packs[0, PACK:, :], (LANES - MARGIN - MARGIN * k) % LANES, 1)
-        beside = jnp.where(group == 0, before, target[TPD, middle, :])
-        beside = jnp.where(group == 2 * TPD - 1, after, beside)
-        target[TPD, middle, :] = jnp.where(mask, beside, 1.0 if k == 5 else 0.0)
-
-    chunk = 72
+        for half in (0, 1):
+            start = half * HALF + k * GROUP
+            rows = slice(TOP + half * HALF, TOP + (half + 1) * HALF)
+            before = pltpu.roll(ahead_ref[PACK:, :], (MARGIN - GROUP - start) % LANES, 1)
+            after = pltpu.roll(back_ref[PACK:, :], (LANES - MARGIN - start) % LANES, 1)
+            beside = jnp.where(group == 0, before, target[TPD, rows, :])
+            beside = jnp.where(group == 2 * TPD - 1, after, beside)
+            target[TPD, rows, :] = jnp.where(mask[:HALF], beside, 1.0 if k == 5 else 0.0)
+
+    chunk = 48
     first_row, last_row = TOP - SECTION, TOP + TS + SECTION
 
     def in_tile(ref, j, rows):
@@ -346,9 +356,6 @@
             u_next[j, rows] = u_new
             v_next[j, rows] = v_new
 
-    for j in range(TPD):
-        ice[j, middle, :] = jnp.ones((TS, LANES), jnp.float32)
-
     def sweep(*state):
         @pl.loop(0, TPD)
         def _(j):
@@ -405,7 +412,7 @@
     anywhere = pl.BlockSpec(memory_space=pl.ANY)
     params = pltpu.CompilerParams(vmem_limit_bytes=VMEM_LIMIT)
     strips_shape = jax.ShapeDtypeStruct((TPD, STRIP, LANES), f32)
-    columns_shape = jax.ShapeDtypeStruct((TS, LANES), f32)
+    columns_shape = jax.ShapeDtypeStruct((HALF, LANES), f32)
     field_shape = jax.ShapeDtypeStruct((TPD + 1, ROWS, LANES), f32)
     pack_shape = jax.ShapeDtypeStruct((FULL_PACK, LANES), f32)
     rows = row_lengths.shape[0]
@@ -438,11 +445,12 @@
     with jax.named_scope("plan"):
         plan = pl.pallas_call(
             functools.partial(plan_kernel, slots),
-            out_shape=jax.ShapeDtypeStruct((PLAN,), jnp.int32),
+            out_shape=jax.ShapeDtypeStruct((1, PLAN), jnp.int32),
             in_specs=[smem],
-            out_specs=anywhere,
-            scratch_shapes=[pltpu.SMEM((PLAN,), jnp.int32), pltpu.SMEM((rows,), jnp.int32), pltpu.SemaphoreType.DMA],
+            out_specs=vmem,
+            scratch_shapes=[pltpu.SMEM((1, PLAN), jnp.int32), pltpu.SMEM((rows,), jnp.int32), pltpu.SemaphoreType.DMA],
             cost_estimate=cost,
+            compiler_params=params,
         )(row_lengths)
 
     with jax.named_scope("own_fields"):
@@ -463,9 +471,9 @@
         back, local, ahead = pl.pallas_call(
             route_kernel,
             out_shape=(pack_shape, jax.ShapeDtypeStruct((PACK, LANES), f32), pack_shape),
-            in_specs=[anywhere] + [vmem] * (2 * HOPS + 2),
+            in_specs=[vmem] * (2 * HOPS + 3),
             out_specs=(vmem,) * 3,
-            scratch_shapes=[pltpu.SMEM((PLAN,), jnp.int32), pltpu.SemaphoreType.DMA],
+            scratch_shapes=[pltpu.SMEM((1, PLAN), jnp.int32), pltpu.SemaphoreType.DMA],
             compiler_params=params,
         )(plan, *bottoms, *tops, right, left)
 
@@ -481,15 +489,15 @@
                 jax.ShapeDtypeStruct(velocity_start.shape, f32),
                 jax.ShapeDtypeStruct(thickness.shape, f32),
             ) + (field_shape,) * 6,
-            in_specs=[smem] + [anywhere] * 3 + [vmem] * 6,
+            in_specs=[vmem] * 10,
             out_specs=(anywhere, anywhere) + (vmem,) * 6,
             input_output_aliases={4 + k: 2 + k for k in range(6)},
             scratch_shapes=[
                 *[field] * 8,
                 pltpu.VMEM((3, TPD, TS, LANES), f32),
-                pltpu.VMEM((3, FULL_PACK, LANES), f32),
-                pltpu.SemaphoreType.DMA((3,)),
                 pltpu.SemaphoreType.DMA((3, TPD)),
+                pltpu.SMEM((1, PLAN), jnp.int32),
+                pltpu.SemaphoreType.DMA,
             ],
             compiler_params=params,
         )(plan, ahead, local, back, *fields)

time: 63.3 us -> 61.1 us (0.965)
  Pallas kernels: 17.8 us -> 16.4 us
  local copies, waits for them, and re-layouts: 0.69 us -> 0.02 us
    pallas_call x1, Pallas kernels: 2.68 us -> 1.74 us  [shards(): pl.pallas_call(route_kernel, out_shape=(pack_shape, jax.ShapeDtypeStruct(...]
    unnamed x10, local copies, waits for them, and re-layouts: 0.69 us -> 0.02 us
  transfers between devices with their start and end apart: 10 -> 10, of which waited for: 3 -> 3; matrix products, arithmetic and copies ran while one was open for 0% -> 0% of each run, Pallas kernels for 5% -> 6%
where the time goes in v3:
time: 61.1 us; the launch traced here: 60.8 us
  starting transfers between devices  32.4 us (53%)
  Pallas kernels  16.4 us (27%)
  waiting for transfers between devices  11.2 us (18%)
  between operations  0.74 us (1%)
    ppermute x10, starting transfers between devices, cyclic_shift(): lax.ppermute(value, 'ta', [(i, (i + steps) % count) for i in range(count)])  32.4 us
    ppermute x10, waiting for transfers between devices, cyclic_shift(): lax.ppermute(value, 'ta', [(i, (i + steps) % count) for i in range(count)])  11.2 us
    pallas_call x1, Pallas kernels, shards(): pl.pallas_call(sweeps_kernel, out_shape=(jax.ShapeDtypeStruct(velocity_st...  9.43 us
    pallas_call x1, Pallas kernels, shards(): pl.pallas_call(functools.partial(plan_kernel, slots), out_shape=jax.Shape...  2.13 us
    pallas_call x1, Pallas kernels, shards(): pl.pallas_call(sent_strips_kernel, out_shape=(strips_shape, strips_shape)...  1.84 us
    pallas_call x1, Pallas kernels, shards(): pl.pallas_call(route_kernel, out_shape=(pack_shape, jax.ShapeDtypeStruct(...  1.74 us
  transfers between devices with their start and end apart: 10, of which 3 were waited for; matrix products, arithmetic and copies ran while one was open for 0% of the time, Pallas kernels for 6%

profile of v3, /device:TPU:0, one launch (start us, length us, event | category | flops | bytes accessed | tf_op | source)
XLA Modules:
  0.0 60.8 jit_solution(17641549347638834895)
XLA Ops:
  0.6 0.0 copy-start.1
  0.6 0.0 copy-start.3
  0.7 0.0 copy-start
  0.7 0.0 copy-start.2
  0.7 1.8 %sent_strips.1 = (f32[4,48,128]{2,1,0:T(8,128)}, f32[4,48,128]{2,1,0:T(8,128)}) custom-call(f32[4,128,128]{2,1,0:T(8,128)} %h_ref.5, f32[2,4,128,128]{3,2,1,0:T(8,128)} %d_ref.5, f32[4,128,128]{2,1,0:T(8,128)} %f_ref.5, f32[2,4,128,128]{3,2,1,0:T(8,128)} %v_ref.5), custom_call_target="tpu_custom_call" | custom-call | tf_op jit(solution)/shard_map/sent_strips/pallas_call | solution.py:423
  2.5 6.5 %collective-permute-start.3 = (f32[4,48,128]{2,1,0:T(8,128)}, f32[4,48,128]{2,1,0:T(8,128)S(1)}, u32[]{:S(2)}, u32[]{:S(2)}) collective-permute-start(f32[4,48,128]{2,1,0:T(8,128)} %get-tuple-element.20), channel_id=1, source_target_pairs={{0,12},{1,13},{2,14},{3,15},{4,16},{5,17},{6,18},{7,19},{8,20},{9,... | collective-permute-start | bytes 294920 | tf_op jit(solution)/shard_map/strides/ppermute | solution.py:41
  9.0 1.9 %collective-permute-start.2 = (f32[4,48,128]{2,1,0:T(8,128)}, f32[4,48,128]{2,1,0:T(8,128)S(1)}, u32[]{:S(2)}, u32[]{:S(2)}) collective-permute-start(f32[4,48,128]{2,1,0:T(8,128)} %get-tuple-element.20), channel_id=1, source_target_pairs={{0,9},{1,10},{2,11},{3,12},{4,13},{5,14},{6,15},{7,16},{8,17},{9,1... | collective-permute-start | bytes 294920 | tf_op jit(solution)/shard_map/strides/ppermute | solution.py:41
  10.9 1.2 %collective-permute-start.1 = (f32[4,48,128]{2,1,0:T(8,128)}, f32[4,48,128]{2,1,0:T(8,128)S(1)}, u32[]{:S(2)}, u32[]{:S(2)}) collective-permute-start(f32[4,48,128]{2,1,0:T(8,128)} %get-tuple-element.20), channel_id=1, source_target_pairs={{0,6},{1,7},{2,8},{3,9},{4,10},{5,11},{6,12},{7,13},{8,14},{9,15},... | collective-permute-start | bytes 294920 | tf_op jit(solution)/shard_map/strides/ppermute | solution.py:41
  12.1 2.8 %collective-permute-start = (f32[4,48,128]{2,1,0:T(8,128)}, f32[4,48,128]{2,1,0:T(8,128)S(1)}, u32[]{:S(2)}, u32[]{:S(2)}) collective-permute-start(f32[4,48,128]{2,1,0:T(8,128)} %get-tuple-element.20), channel_id=1, source_target_pairs={{0,3},{1,4},{2,5},{3,6},{4,7},{5,8},{6,9},{7,10},{8,11},{9,12},{10... | collective-permute-start | bytes 294920 | tf_op jit(solution)/shard_map/strides/ppermute | solution.py:41
  14.9 0.0 copy-start.4
  14.9 5.6 %collective-permute-start.7 = (f32[4,48,128]{2,1,0:T(8,128)}, f32[4,48,128]{2,1,0:T(8,128)S(1)}, u32[]{:S(2)}, u32[]{:S(2)}) collective-permute-start(f32[4,48,128]{2,1,0:T(8,128)} %get-tuple-element.22), channel_id=1, source_target_pairs={{0,116},{1,117},{2,118},{3,119},{4,120},{5,121},{6,122},{7,123},{8... | collective-permute-start | bytes 294920 | tf_op jit(solution)/shard_map/strides/ppermute | solution.py:41
  20.6 0.0 collective-permute-done.3.refs_4_
  20.6 2.3 %collective-permute-start.6 = (f32[4,48,128]{2,1,0:T(8,128)}, f32[4,48,128]{2,1,0:T(8,128)S(1)}, u32[]{:S(2)}, u32[]{:S(2)}) collective-permute-start(f32[4,48,128]{2,1,0:T(8,128)} %get-tuple-element.22), channel_id=1, source_target_pairs={{0,119},{1,120},{2,121},{3,122},{4,123},{5,124},{6,125},{7,126},{8... | collective-permute-start | bytes 294920 | tf_op jit(solution)/shard_map/strides/ppermute | solution.py:41
  22.8 0.0 collective-permute-done.2.refs_3_
  22.8 3.0 %collective-permute-start.5 = (f32[4,48,128]{2,1,0:T(8,128)}, f32[4,48,128]{2,1,0:T(8,128)S(1)}, u32[]{:S(2)}, u32[]{:S(2)}) collective-permute-start(f32[4,48,128]{2,1,0:T(8,128)} %get-tuple-element.22), channel_id=1, source_target_pairs={{0,122},{1,123},{2,124},{3,125},{4,126},{5,127},{6,0},{7,1},{8,2},... | collective-permute-start | bytes 294920 | tf_op jit(solution)/shard_map/strides/ppermute | solution.py:41
  25.9 0.0 collective-permute-done.1.refs_2_
  25.9 1.5 %collective-permute-start.4 = (f32[4,48,128]{2,1,0:T(8,128)}, f32[4,48,128]{2,1,0:T(8,128)S(1)}, u32[]{:S(2)}, u32[]{:S(2)}) collective-permute-start(f32[4,48,128]{2,1,0:T(8,128)} %get-tuple-element.22), channel_id=1, source_target_pairs={{0,125},{1,126},{2,127},{3,0},{4,1},{5,2},{6,3},{7,4},{8,5},{9,6},... | collective-permute-start | bytes 294920 | tf_op jit(solution)/shard_map/strides/ppermute | solution.py:41
  27.3 0.0 copy-done.1
  27.3 0.0 copy-done.3
  27.3 0.0 copy-done
  27.3 0.0 copy-done.2
  27.3 0.3 own_strips.1
  27.6 0.0 copy-done.4
  27.6 2.1 %plan.1.given_plan = s32[1,128]{1,0:T(1,128)S(1)} custom-call(s32[22]{0:T(128)S(1)} %copy-done.4), custom_call_target="tpu_custom_call" | custom-call | flops 4000000 | bytes 4000000 | tf_op jit(solution)/shard_map/plan/pallas_call | solution.py:446
  29.8 4.4 %collective-permute-done.refs_1_ = f32[4,48,128]{2,1,0:T(8,128)S(1)} collective-permute-done((f32[4,48,128]{2,1,0:T(8,128)}, f32[4,48,128]{2,1,0:T(8,128)S(1)}, u32[]{:S(2)}, u32[]{:S(2)}) %collective-permute-start) | collective-permute-done | bytes 98336 | tf_op jit(solution)/shard_map/strides/ppermute | solution.py:41
  34.1 0.0 collective-permute-done.7.refs_9_
  34.1 0.0 collective-permute-done.6.refs_8_
  34.1 0.0 collective-permute-done.5.refs_7_
  34.1 2.9 %collective-permute-done.4.refs_6_ = f32[4,48,128]{2,1,0:T(8,128)S(1)} collective-permute-done((f32[4,48,128]{2,1,0:T(8,128)}, f32[4,48,128]{2,1,0:T(8,128)S(1)}, u32[]{:S(2)}, u32[]{:S(2)}) %collective-permute-start.4) | collective-permute-done | bytes 98336 | tf_op jit(solution)/shard_map/strides/ppermute | solution.py:41
  37.0 1.7 %route.1 = (f32[544,128]{1,0:T(8,128)S(1)}, f32[480,128]{1,0:T(8,128)S(1)}, f32[544,128]{1,0:T(8,128)S(1)}) custom-call(s32[1,128]{1,0:T(1,128)S(1)} %plan.1.given_plan, f32[4,48,128]{2,1,0:T(8,128)S(1)} %get-tuple-element.19.refs_0_, f32[4,48,128]{2,1,0:T(8,128)S(1)} %collective-permute-done.refs_1_, f32[4,48,128]{2,1,0:T(8,128)S(1)} %collective-permute-done.1.refs_2_, ...), custom_call_target="tpu_custom_call" | custom-call | tf_op jit(solution)/shard_map/route/pallas_call | solution.py:471
  38.8 0.1 collective-permute-start.8
  38.9 7.5 %collective-permute-start.9 = (f32[544,128]{1,0:T(8,128)S(1)}, f32[544,128]{1,0:T(8,128)S(1)}, u32[]{:S(2)}, u32[]{:S(2)}) collective-permute-start(f32[544,128]{1,0:T(8,128)S(1)} %get-tuple-element.27), channel_id=1, source_target_pairs={{0,127},{1,0},{2,1},{3,2},{4,3},{5,4},{6,5},{7,6},{8,7},{9,8},{10,... | collective-permute-start | bytes 835592 | tf_op jit(solution)/shard_map/last_step/ppermute | solution.py:41
  46.4 1.0 %own_fields.1 = (f32[5,160,128]{2,1,0:T(8,128)S(1)}, f32[5,160,128]{2,1,0:T(8,128)S(1)}, f32[5,160,128]{2,1,0:T(8,128)S(1)}, f32[5,160,128]{2,1,0:T(8,128)S(1)},...) custom-call(f32[4,128,128]{2,1,0:T(8,128)S(1)} %copy-done.2, f32[2,4,128,128]{3,2,1,0:T(8,128)S(1)} %copy-done, ...), custom_call_target="tpu_custom_call" | custom-call | flops 4000000 | bytes 4000000 | tf_op jit(solution)/shard_map/own_fields/pallas_call | solution.py:457
  47.4 4.0 %collective-permute-done.8.ahead_ref = f32[544,128]{1,0:T(8,128)S(1)} collective-permute-done((f32[544,128]{1,0:T(8,128)S(1)}, f32[544,128]{1,0:T(8,128)S(1)}, u32[]{:S(2)}, u32[]{:S(2)}) %collective-permute-start.8) | collective-permute-done | bytes 278560 | tf_op jit(solution)/shard_map/last_step/ppermute | solution.py:41
  51.4 0.0 collective-permute-done.9.back_ref
  51.4 9.4 %sweeps.1 = (f32[2,4,128,128]{3,2,1,0:T(8,128)}, f32[4,128,128]{2,1,0:T(8,128)}, f32[5,160,128]{2,1,0:T(8,128)S(1)}, f32[5,160,128]{2,1,0:T(8,128)S(1)}, f32[5,1...) custom-call(s32[1,128]{1,0:T(1,128)S(1)} %plan.1.given_plan, ...), custom_call_target="tpu_custom_call", output_to_operand_aliasing={{2}: (4, {}), {3}: (5, {}), {4}: (6, {}), {5}: (7, {}), {6}... | custom-call | tf_op jit(solution)/shard_map/sweeps/pallas_call | solution.py:486
Async XLA Ops:
  0.6 26.7 %copy-start.1 = (f32[2,4,128,128]{3,2,1,0:T(8,128)S(1)}, f32[2,4,128,128]{3,2,1,0:T(8,128)}, u32[]{:S(2)}) copy-start(f32[2,4,128,128]{3,2,1,0:T(8,128)} %v_ref.5) | copy-start | bytes 1572868
  0.6 26.7 %copy-start.3 = (f32[4,128,128]{2,1,0:T(8,128)S(1)}, f32[4,128,128]{2,1,0:T(8,128)}, u32[]{:S(2)}) copy-start(f32[4,128,128]{2,1,0:T(8,128)} %f_ref.5) | copy-start | bytes 786436
  0.7 26.7 %copy-start = (f32[2,4,128,128]{3,2,1,0:T(8,128)S(1)}, f32[2,4,128,128]{3,2,1,0:T(8,128)}, u32[]{:S(2)}) copy-start(f32[2,4,128,128]{3,2,1,0:T(8,128)} %d_ref.5) | copy-start | bytes 1572868
  0.7 26.7 %copy-start.2 = (f32[4,128,128]{2,1,0:T(8,128)S(1)}, f32[4,128,128]{2,1,0:T(8,128)}, u32[]{:S(2)}) copy-start(f32[4,128,128]{2,1,0:T(8,128)} %h_ref.5) | copy-start | bytes 786436
  2.5 18.1 %collective-permute-start.3 = (f32[4,48,128]{2,1,0:T(8,128)}, f32[4,48,128]{2,1,0:T(8,128)S(1)}, u32[]{:S(2)}, u32[]{:S(2)}) collective-permute-start(f32[4,48,128]{2,1,0:T(8,128)} %get-tuple-element.20), channel_id=1, source_target_pairs={{0,12},{1,13},{2,14},{3,15},{4,16},{5,17},{6,18},{7,19},{8,20},{9,... | collective-permute-start | bytes 294920 | tf_op jit(solution)/shard_map/strides/ppermute | solution.py:41
  9.0 13.9 %collective-permute-start.2 = (f32[4,48,128]{2,1,0:T(8,128)}, f32[4,48,128]{2,1,0:T(8,128)S(1)}, u32[]{:S(2)}, u32[]{:S(2)}) collective-permute-start(f32[4,48,128]{2,1,0:T(8,128)} %get-tuple-element.20), channel_id=1, source_target_pairs={{0,9},{1,10},{2,11},{3,12},{4,13},{5,14},{6,15},{7,16},{8,17},{9,1... | collective-permute-start | bytes 294920 | tf_op jit(solution)/shard_map/strides/ppermute | solution.py:41
  10.9 14.9 %collective-permute-start.1 = (f32[4,48,128]{2,1,0:T(8,128)}, f32[4,48,128]{2,1,0:T(8,128)S(1)}, u32[]{:S(2)}, u32[]{:S(2)}) collective-permute-start(f32[4,48,128]{2,1,0:T(8,128)} %get-tuple-element.20), channel_id=1, source_target_pairs={{0,6},{1,7},{2,8},{3,9},{4,10},{5,11},{6,12},{7,13},{8,14},{9,15},... | collective-permute-start | bytes 294920 | tf_op jit(solution)/shard_map/strides/ppermute | solution.py:41
  12.1 22.0 %collective-permute-start = (f32[4,48,128]{2,1,0:T(8,128)}, f32[4,48,128]{2,1,0:T(8,128)S(1)}, u32[]{:S(2)}, u32[]{:S(2)}) collective-permute-start(f32[4,48,128]{2,1,0:T(8,128)} %get-tuple-element.20), channel_id=1, source_target_pairs={{0,3},{1,4},{2,5},{3,6},{4,7},{5,8},{6,9},{7,10},{8,11},{9,12},{10... | collective-permute-start | bytes 294920 | tf_op jit(solution)/shard_map/strides/ppermute | solution.py:41
  14.9 12.7 %copy-start.4 = (s32[22]{0:T(128)S(1)}, s32[22]{0:T(128)}, u32[]{:S(2)}) copy-start(s32[22]{0:T(128)} %len_ref.1) | copy-start | bytes 268
  14.9 19.2 %collective-permute-start.7 = (f32[4,48,128]{2,1,0:T(8,128)}, f32[4,48,128]{2,1,0:T(8,128)S(1)}, u32[]{:S(2)}, u32[]{:S(2)}) collective-permute-start(f32[4,48,128]{2,1,0:T(8,128)} %get-tuple-element.22), channel_id=1, source_target_pairs={{0,116},{1,117},{2,118},{3,119},{4,120},{5,121},{6,122},{7,123},{8... | collective-permute-start | bytes 294920 | tf_op jit(solution)/shard_map/strides/ppermute | solution.py:41
  20.6 13.6 %collective-permute-start.6 = (f32[4,48,128]{2,1,0:T(8,128)}, f32[4,48,128]{2,1,0:T(8,128)S(1)}, u32[]{:S(2)}, u32[]{:S(2)}) collective-permute-start(f32[4,48,128]{2,1,0:T(8,128)} %get-tuple-element.22), channel_id=1, source_target_pairs={{0,119},{1,120},{2,121},{3,122},{4,123},{5,124},{6,125},{7,126},{8... | collective-permute-start | bytes 294920 | tf_op jit(solution)/shard_map/strides/ppermute | solution.py:41
  22.8 11.3 %collective-permute-start.5 = (f32[4,48,128]{2,1,0:T(8,128)}, f32[4,48,128]{2,1,0:T(8,128)S(1)}, u32[]{:S(2)}, u32[]{:S(2)}) collective-permute-start(f32[4,48,128]{2,1,0:T(8,128)} %get-tuple-element.22), channel_id=1, source_target_pairs={{0,122},{1,123},{2,124},{3,125},{4,126},{5,127},{6,0},{7,1},{8,2},... | collective-permute-start | bytes 294920 | tf_op jit(solution)/shard_map/strides/ppermute | solution.py:41
  25.9 11.2 %collective-permute-start.4 = (f32[4,48,128]{2,1,0:T(8,128)}, f32[4,48,128]{2,1,0:T(8,128)S(1)}, u32[]{:S(2)}, u32[]{:S(2)}) collective-permute-start(f32[4,48,128]{2,1,0:T(8,128)} %get-tuple-element.22), channel_id=1, source_target_pairs={{0,125},{1,126},{2,127},{3,0},{4,1},{5,2},{6,3},{7,4},{8,5},{9,6},... | collective-permute-start | bytes 294920 | tf_op jit(solution)/shard_map/strides/ppermute | solution.py:41
  38.8 12.6 %collective-permute-start.8 = (f32[544,128]{1,0:T(8,128)S(1)}, f32[544,128]{1,0:T(8,128)S(1)}, u32[]{:S(2)}, u32[]{:S(2)}) collective-permute-start(f32[544,128]{1,0:T(8,128)S(1)} %get-tuple-element.25), channel_id=1, source_target_pairs={{0,1},{1,2},{2,3},{3,4},{4,5},{5,6},{6,7},{7,8},{8,9},{9,10},{10,1... | collective-permute-start | bytes 835592 | tf_op jit(solution)/shard_map/last_step/ppermute | solution.py:41
  38.9 12.5 %collective-permute-start.9 = (f32[544,128]{1,0:T(8,128)S(1)}, f32[544,128]{1,0:T(8,128)S(1)}, u32[]{:S(2)}, u32[]{:S(2)}) collective-permute-start(f32[544,128]{1,0:T(8,128)S(1)} %get-tuple-element.27), channel_id=1, source_target_pairs={{0,127},{1,0},{2,1},{3,2},{4,3},{5,4},{6,5},{7,6},{8,7},{9,8},{10,... | collective-permute-start | bytes 835592 | tf_op jit(solution)/shard_map/last_step/ppermute | solution.py:41

commit v4 on v3

--- a/solution.py
+++ b/solution.py
@@ -24,7 +24,8 @@
 STRIDE = 3
 HOPS = 5
 MAIN_BLOCKS = 2 * TPD
-PACK = (MAIN_BLOCKS + 2) * STRIP
+PACK = (MAIN_BLOCKS + 1) * STRIP
+CORNER = 8
 GROUP = 10
 HALF = TS // 2
 FULL_PACK = PACK + HALF
@@ -196,7 +197,7 @@
     outs[0][PACK:, :] = left_ref[...]
     outs[2][PACK:, :] = right_ref[...]
     for out in outs:
-        out[MAIN_BLOCKS * STRIP : PACK, :] = jnp.zeros((2 * STRIP, LANES), jnp.float32)
+        out[MAIN_BLOCKS * STRIP : PACK, :] = jnp.zeros((STRIP, LANES), jnp.float32)
     lane = lax.broadcasted_iota(jnp.int32, (STRIP, LANES), 1)
     copy.wait()
     for step, out in enumerate(outs):
@@ -214,12 +215,13 @@
                             @pl.when((source >> 2) == a)
                             def _():
                                 strip = given[down * HOPS + a][source & 3]
-                                moved = pltpu.roll(strip, 2 * MARGIN * j + MARGIN, 1)
+                                turn = 2 * MARGIN * j + MARGIN + (MARGIN * down if across else 0)
+                                moved = pltpu.roll(strip, turn & (LANES - 1), 1)
                                 if across == 0:
                                     out[pl.ds(pl.multiple_of((down * TPD + j) * STRIP, 8), STRIP), :] = moved
                                 else:
-                                    rows = slice((MAIN_BLOCKS + down) * STRIP, (MAIN_BLOCKS + down + 1) * STRIP)
-                                    here = (lane >> 4) == 2 * j + (across + 1) // 2
+                                    rows = slice(MAIN_BLOCKS * STRIP, PACK)
+                                    here = (lane >> 3) == ((4 * j + 1 + (across + 1) // 2 + 2 * down) & 15)
                                     out[rows, :] = jnp.where(here, moved, out[rows, :])
 
 
@@ -277,8 +279,11 @@
                 put(j, [zero] * 5 + [one])
                 ice[j, rows, :] = zero
 
-        mask = group_mask(plan_ref[0, BITS + down], (SECTION, LANES))
-        parts = [sum(part) for part in zip(*[sections(pack, MAIN_BLOCKS + down) for pack in packs])]
+        within = lax.broadcasted_iota(jnp.int32, (SECTION, LANES), 1) & (2 * MARGIN - 1)
+        near = (within >= MARGIN - CORNER) & (within < MARGIN + CORNER)
+        mask = group_mask(plan_ref[0, BITS + down], (SECTION, LANES)) & near
+        parts = [sum(part) for part in zip(*[sections(pack, MAIN_BLOCKS) for pack in packs])]
+        parts = [pltpu.roll(part, LANES - MARGIN, 1) for part in parts] if down else parts
         put(TPD, parts, mask)
         ice[TPD, rows, :] = jnp.where(mask, one, zero)
 

time: 61.1 us -> 60.7 us (level)
    ppermute x10, waiting for transfers between devices: 11.2 us -> 10.6 us  [cyclic_shift(): lax.ppermute(value, 'ta', [(i, (i + steps) % count) for i in range(count)])]
where the time goes in v4:
time: 60.7 us; the launch traced here: 60.6 us
  starting transfers between devices  32.3 us (53%)
  Pallas kernels  16.9 us (28%)
  waiting for transfers between devices  10.6 us (17%)
  between operations  0.74 us (1%)
    ppermute x10, starting transfers between devices, cyclic_shift(): lax.ppermute(value, 'ta', [(i, (i + steps) % count) for i in range(count)])  32.3 us
    ppermute x10, waiting for transfers between devices, cyclic_shift(): lax.ppermute(value, 'ta', [(i, (i + steps) % count) for i in range(count)])  10.6 us
    pallas_call x1, Pallas kernels, shards(): pl.pallas_call(sweeps_kernel, out_shape=(jax.ShapeDtypeStruct(velocity_st...  9.45 us
    pallas_call x1, Pallas kernels, shards(): pl.pallas_call(route_kernel, out_shape=(pack_shape, jax.ShapeDtypeStruct(...  2.27 us
    pallas_call x1, Pallas kernels, shards(): pl.pallas_call(functools.partial(plan_kernel, slots), out_shape=jax.Shape...  2.13 us
    pallas_call x1, Pallas kernels, shards(): pl.pallas_call(sent_strips_kernel, out_shape=(strips_shape, strips_shape)...  1.84 us
  transfers between devices with their start and end apart: 10, of which 3 were waited for; matrix products, arithmetic and copies ran while one was open for 0% of the time, Pallas kernels for 6%

profile of v4, /device:TPU:0, one launch (start us, length us, event | category | flops | bytes accessed | tf_op | source)
XLA Modules:
  0.0 60.6 jit_solution(542511981376815722)
XLA Ops:
  0.6 0.0 copy-start.1
  0.6 0.0 copy-start.3
  0.7 0.0 copy-start
  0.7 0.0 copy-start.2
  0.7 1.8 %sent_strips.1 = (f32[4,48,128]{2,1,0:T(8,128)}, f32[4,48,128]{2,1,0:T(8,128)}) custom-call(f32[4,128,128]{2,1,0:T(8,128)} %h_ref.5, f32[2,4,128,128]{3,2,1,0:T(8,128)} %d_ref.5, f32[4,128,128]{2,1,0:T(8,128)} %f_ref.5, f32[2,4,128,128]{3,2,1,0:T(8,128)} %v_ref.5), custom_call_target="tpu_custom_call" | custom-call | tf_op jit(solution)/shard_map/sent_strips/pallas_call | solution.py:428
  2.5 6.5 %collective-permute-start.3 = (f32[4,48,128]{2,1,0:T(8,128)}, f32[4,48,128]{2,1,0:T(8,128)S(1)}, u32[]{:S(2)}, u32[]{:S(2)}) collective-permute-start(f32[4,48,128]{2,1,0:T(8,128)} %get-tuple-element.20), channel_id=1, source_target_pairs={{0,12},{1,13},{2,14},{3,15},{4,16},{5,17},{6,18},{7,19},{8,20},{9,... | collective-permute-start | bytes 294920 | tf_op jit(solution)/shard_map/strides/ppermute | solution.py:42
  9.0 1.9 %collective-permute-start.2 = (f32[4,48,128]{2,1,0:T(8,128)}, f32[4,48,128]{2,1,0:T(8,128)S(1)}, u32[]{:S(2)}, u32[]{:S(2)}) collective-permute-start(f32[4,48,128]{2,1,0:T(8,128)} %get-tuple-element.20), channel_id=1, source_target_pairs={{0,9},{1,10},{2,11},{3,12},{4,13},{5,14},{6,15},{7,16},{8,17},{9,1... | collective-permute-start | bytes 294920 | tf_op jit(solution)/shard_map/strides/ppermute | solution.py:42
  10.9 1.2 %collective-permute-start.1 = (f32[4,48,128]{2,1,0:T(8,128)}, f32[4,48,128]{2,1,0:T(8,128)S(1)}, u32[]{:S(2)}, u32[]{:S(2)}) collective-permute-start(f32[4,48,128]{2,1,0:T(8,128)} %get-tuple-element.20), channel_id=1, source_target_pairs={{0,6},{1,7},{2,8},{3,9},{4,10},{5,11},{6,12},{7,13},{8,14},{9,15},... | collective-permute-start | bytes 294920 | tf_op jit(solution)/shard_map/strides/ppermute | solution.py:42
  12.1 2.8 %collective-permute-start = (f32[4,48,128]{2,1,0:T(8,128)}, f32[4,48,128]{2,1,0:T(8,128)S(1)}, u32[]{:S(2)}, u32[]{:S(2)}) collective-permute-start(f32[4,48,128]{2,1,0:T(8,128)} %get-tuple-element.20), channel_id=1, source_target_pairs={{0,3},{1,4},{2,5},{3,6},{4,7},{5,8},{6,9},{7,10},{8,11},{9,12},{10... | collective-permute-start | bytes 294920 | tf_op jit(solution)/shard_map/strides/ppermute | solution.py:42
  14.9 0.0 copy-start.4
  14.9 5.6 %collective-permute-start.7 = (f32[4,48,128]{2,1,0:T(8,128)}, f32[4,48,128]{2,1,0:T(8,128)S(1)}, u32[]{:S(2)}, u32[]{:S(2)}) collective-permute-start(f32[4,48,128]{2,1,0:T(8,128)} %get-tuple-element.22), channel_id=1, source_target_pairs={{0,116},{1,117},{2,118},{3,119},{4,120},{5,121},{6,122},{7,123},{8... | collective-permute-start | bytes 294920 | tf_op jit(solution)/shard_map/strides/ppermute | solution.py:42
  20.6 0.0 collective-permute-done.3.refs_4_
  20.6 2.3 %collective-permute-start.6 = (f32[4,48,128]{2,1,0:T(8,128)}, f32[4,48,128]{2,1,0:T(8,128)S(1)}, u32[]{:S(2)}, u32[]{:S(2)}) collective-permute-start(f32[4,48,128]{2,1,0:T(8,128)} %get-tuple-element.22), channel_id=1, source_target_pairs={{0,119},{1,120},{2,121},{3,122},{4,123},{5,124},{6,125},{7,126},{8... | collective-permute-start | bytes 294920 | tf_op jit(solution)/shard_map/strides/ppermute | solution.py:42
  22.8 0.0 collective-permute-done.2.refs_3_
  22.8 3.0 %collective-permute-start.5 = (f32[4,48,128]{2,1,0:T(8,128)}, f32[4,48,128]{2,1,0:T(8,128)S(1)}, u32[]{:S(2)}, u32[]{:S(2)}) collective-permute-start(f32[4,48,128]{2,1,0:T(8,128)} %get-tuple-element.22), channel_id=1, source_target_pairs={{0,122},{1,123},{2,124},{3,125},{4,126},{5,127},{6,0},{7,1},{8,2},... | collective-permute-start | bytes 294920 | tf_op jit(solution)/shard_map/strides/ppermute | solution.py:42
  25.9 0.0 collective-permute-done.1.refs_2_
  25.9 1.5 %collective-permute-start.4 = (f32[4,48,128]{2,1,0:T(8,128)}, f32[4,48,128]{2,1,0:T(8,128)S(1)}, u32[]{:S(2)}, u32[]{:S(2)}) collective-permute-start(f32[4,48,128]{2,1,0:T(8,128)} %get-tuple-element.22), channel_id=1, source_target_pairs={{0,125},{1,126},{2,127},{3,0},{4,1},{5,2},{6,3},{7,4},{8,5},{9,6},... | collective-permute-start | bytes 294920 | tf_op jit(solution)/shard_map/strides/ppermute | solution.py:42
  27.3 0.0 copy-done.1
  27.3 0.0 copy-done.3
  27.3 0.0 copy-done
  27.3 0.0 copy-done.2
  27.3 0.3 own_strips.1
  27.6 0.0 copy-done.4
  27.6 2.1 %plan.1.given_plan = s32[1,128]{1,0:T(1,128)S(1)} custom-call(s32[22]{0:T(128)S(1)} %copy-done.4), custom_call_target="tpu_custom_call" | custom-call | flops 4000000 | bytes 4000000 | tf_op jit(solution)/shard_map/plan/pallas_call | solution.py:451
  29.8 4.4 %collective-permute-done.refs_1_ = f32[4,48,128]{2,1,0:T(8,128)S(1)} collective-permute-done((f32[4,48,128]{2,1,0:T(8,128)}, f32[4,48,128]{2,1,0:T(8,128)S(1)}, u32[]{:S(2)}, u32[]{:S(2)}) %collective-permute-start) | collective-permute-done | bytes 98336 | tf_op jit(solution)/shard_map/strides/ppermute | solution.py:42
  34.1 0.0 collective-permute-done.7.refs_9_
  34.1 0.0 collective-permute-done.6.refs_8_
  34.1 0.0 collective-permute-done.5.refs_7_
  34.1 2.9 %collective-permute-done.4.refs_6_ = f32[4,48,128]{2,1,0:T(8,128)S(1)} collective-permute-done((f32[4,48,128]{2,1,0:T(8,128)}, f32[4,48,128]{2,1,0:T(8,128)S(1)}, u32[]{:S(2)}, u32[]{:S(2)}) %collective-permute-start.4) | collective-permute-done | bytes 98336 | tf_op jit(solution)/shard_map/strides/ppermute | solution.py:42
  37.0 2.3 %route.1 = (f32[496,128]{1,0:T(8,128)S(1)}, f32[432,128]{1,0:T(8,128)S(1)}, f32[496,128]{1,0:T(8,128)S(1)}) custom-call(s32[1,128]{1,0:T(1,128)S(1)} %plan.1.given_plan, f32[4,48,128]{2,1,0:T(8,128)S(1)} %get-tuple-element.19.refs_0_, f32[4,48,128]{2,1,0:T(8,128)S(1)} %collective-permute-done.refs_1_, f32[4,48,128]{2,1,0:T(8,128)S(1)} %collective-permute-done.1.refs_2_, ...), custom_call_target="tpu_custom_call" | custom-call | tf_op jit(solution)/shard_map/route/pallas_call | solution.py:476
  39.3 0.1 collective-permute-start.8
  39.4 7.4 %collective-permute-start.9 = (f32[496,128]{1,0:T(8,128)S(1)}, f32[496,128]{1,0:T(8,128)S(1)}, u32[]{:S(2)}, u32[]{:S(2)}) collective-permute-start(f32[496,128]{1,0:T(8,128)S(1)} %get-tuple-element.27), channel_id=1, source_target_pairs={{0,127},{1,0},{2,1},{3,2},{4,3},{5,4},{6,5},{7,6},{8,7},{9,8},{10,... | collective-permute-start | bytes 761864 | tf_op jit(solution)/shard_map/last_step/ppermute | solution.py:42
  46.9 1.0 %own_fields.1 = (f32[5,160,128]{2,1,0:T(8,128)S(1)}, f32[5,160,128]{2,1,0:T(8,128)S(1)}, f32[5,160,128]{2,1,0:T(8,128)S(1)}, f32[5,160,128]{2,1,0:T(8,128)S(1)},...) custom-call(f32[4,128,128]{2,1,0:T(8,128)S(1)} %copy-done.2, f32[2,4,128,128]{3,2,1,0:T(8,128)S(1)} %copy-done, ...), custom_call_target="tpu_custom_call" | custom-call | flops 4000000 | bytes 4000000 | tf_op jit(solution)/shard_map/own_fields/pallas_call | solution.py:462
  47.8 3.3 %collective-permute-done.8.ahead_ref = f32[496,128]{1,0:T(8,128)S(1)} collective-permute-done((f32[496,128]{1,0:T(8,128)S(1)}, f32[496,128]{1,0:T(8,128)S(1)}, u32[]{:S(2)}, u32[]{:S(2)}) %collective-permute-start.8) | collective-permute-done | bytes 253984 | tf_op jit(solution)/shard_map/last_step/ppermute | solution.py:42
  51.1 0.0 collective-permute-done.9.back_ref
  51.1 9.4 %sweeps.1 = (f32[2,4,128,128]{3,2,1,0:T(8,128)}, f32[4,128,128]{2,1,0:T(8,128)}, f32[5,160,128]{2,1,0:T(8,128)S(1)}, f32[5,160,128]{2,1,0:T(8,128)S(1)}, f32[5,1...) custom-call(s32[1,128]{1,0:T(1,128)S(1)} %plan.1.given_plan, ...), custom_call_target="tpu_custom_call", output_to_operand_aliasing={{2}: (4, {}), {3}: (5, {}), {4}: (6, {}), {5}: (7, {}), {6}... | custom-call | tf_op jit(solution)/shard_map/sweeps/pallas_call | solution.py:491
Async XLA Ops:
  0.6 26.7 %copy-start.1 = (f32[2,4,128,128]{3,2,1,0:T(8,128)S(1)}, f32[2,4,128,128]{3,2,1,0:T(8,128)}, u32[]{:S(2)}) copy-start(f32[2,4,128,128]{3,2,1,0:T(8,128)} %v_ref.5) | copy-start | bytes 1572868
  0.6 26.7 %copy-start.3 = (f32[4,128,128]{2,1,0:T(8,128)S(1)}, f32[4,128,128]{2,1,0:T(8,128)}, u32[]{:S(2)}) copy-start(f32[4,128,128]{2,1,0:T(8,128)} %f_ref.5) | copy-start | bytes 786436
  0.7 26.7 %copy-start = (f32[2,4,128,128]{3,2,1,0:T(8,128)S(1)}, f32[2,4,128,128]{3,2,1,0:T(8,128)}, u32[]{:S(2)}) copy-start(f32[2,4,128,128]{3,2,1,0:T(8,128)} %d_ref.5) | copy-start | bytes 1572868
  0.7 26.7 %copy-start.2 = (f32[4,128,128]{2,1,0:T(8,128)S(1)}, f32[4,128,128]{2,1,0:T(8,128)}, u32[]{:S(2)}) copy-start(f32[4,128,128]{2,1,0:T(8,128)} %h_ref.5) | copy-start | bytes 786436
  2.5 18.1 %collective-permute-start.3 = (f32[4,48,128]{2,1,0:T(8,128)}, f32[4,48,128]{2,1,0:T(8,128)S(1)}, u32[]{:S(2)}, u32[]{:S(2)}) collective-permute-start(f32[4,48,128]{2,1,0:T(8,128)} %get-tuple-element.20), channel_id=1, source_target_pairs={{0,12},{1,13},{2,14},{3,15},{4,16},{5,17},{6,18},{7,19},{8,20},{9,... | collective-permute-start | bytes 294920 | tf_op jit(solution)/shard_map/strides/ppermute | solution.py:42
  9.0 13.9 %collective-permute-start.2 = (f32[4,48,128]{2,1,0:T(8,128)}, f32[4,48,128]{2,1,0:T(8,128)S(1)}, u32[]{:S(2)}, u32[]{:S(2)}) collective-permute-start(f32[4,48,128]{2,1,0:T(8,128)} %get-tuple-element.20), channel_id=1, source_target_pairs={{0,9},{1,10},{2,11},{3,12},{4,13},{5,14},{6,15},{7,16},{8,17},{9,1... | collective-permute-start | bytes 294920 | tf_op jit(solution)/shard_map/strides/ppermute | solution.py:42
  10.9 14.9 %collective-permute-start.1 = (f32[4,48,128]{2,1,0:T(8,128)}, f32[4,48,128]{2,1,0:T(8,128)S(1)}, u32[]{:S(2)}, u32[]{:S(2)}) collective-permute-start(f32[4,48,128]{2,1,0:T(8,128)} %get-tuple-element.20), channel_id=1, source_target_pairs={{0,6},{1,7},{2,8},{3,9},{4,10},{5,11},{6,12},{7,13},{8,14},{9,15},... | collective-permute-start | bytes 294920 | tf_op jit(solution)/shard_map/strides/ppermute | solution.py:42
  12.1 22.0 %collective-permute-start = (f32[4,48,128]{2,1,0:T(8,128)}, f32[4,48,128]{2,1,0:T(8,128)S(1)}, u32[]{:S(2)}, u32[]{:S(2)}) collective-permute-start(f32[4,48,128]{2,1,0:T(8,128)} %get-tuple-element.20), channel_id=1, source_target_pairs={{0,3},{1,4},{2,5},{3,6},{4,7},{5,8},{6,9},{7,10},{8,11},{9,12},{10... | collective-permute-start | bytes 294920 | tf_op jit(solution)/shard_map/strides/ppermute | solution.py:42
  14.9 12.7 %copy-start.4 = (s32[22]{0:T(128)S(1)}, s32[22]{0:T(128)}, u32[]{:S(2)}) copy-start(s32[22]{0:T(128)} %len_ref.1) | copy-start | bytes 268
  14.9 19.2 %collective-permute-start.7 = (f32[4,48,128]{2,1,0:T(8,128)}, f32[4,48,128]{2,1,0:T(8,128)S(1)}, u32[]{:S(2)}, u32[]{:S(2)}) collective-permute-start(f32[4,48,128]{2,1,0:T(8,128)} %get-tuple-element.22), channel_id=1, source_target_pairs={{0,116},{1,117},{2,118},{3,119},{4,120},{5,121},{6,122},{7,123},{8... | collective-permute-start | bytes 294920 | tf_op jit(solution)/shard_map/strides/ppermute | solution.py:42
  20.6 13.6 %collective-permute-start.6 = (f32[4,48,128]{2,1,0:T(8,128)}, f32[4,48,128]{2,1,0:T(8,128)S(1)}, u32[]{:S(2)}, u32[]{:S(2)}) collective-permute-start(f32[4,48,128]{2,1,0:T(8,128)} %get-tuple-element.22), channel_id=1, source_target_pairs={{0,119},{1,120},{2,121},{3,122},{4,123},{5,124},{6,125},{7,126},{8... | collective-permute-start | bytes 294920 | tf_op jit(solution)/shard_map/strides/ppermute | solution.py:42
  22.8 11.3 %collective-permute-start.5 = (f32[4,48,128]{2,1,0:T(8,128)}, f32[4,48,128]{2,1,0:T(8,128)S(1)}, u32[]{:S(2)}, u32[]{:S(2)}) collective-permute-start(f32[4,48,128]{2,1,0:T(8,128)} %get-tuple-element.22), channel_id=1, source_target_pairs={{0,122},{1,123},{2,124},{3,125},{4,126},{5,127},{6,0},{7,1},{8,2},... | collective-permute-start | bytes 294920 | tf_op jit(solution)/shard_map/strides/ppermute | solution.py:42
  25.9 11.2 %collective-permute-start.4 = (f32[4,48,128]{2,1,0:T(8,128)}, f32[4,48,128]{2,1,0:T(8,128)S(1)}, u32[]{:S(2)}, u32[]{:S(2)}) collective-permute-start(f32[4,48,128]{2,1,0:T(8,128)} %get-tuple-element.22), channel_id=1, source_target_pairs={{0,125},{1,126},{2,127},{3,0},{4,1},{5,2},{6,3},{7,4},{8,5},{9,6},... | collective-permute-start | bytes 294920 | tf_op jit(solution)/shard_map/strides/ppermute | solution.py:42
  39.3 11.8 %collective-permute-start.8 = (f32[496,128]{1,0:T(8,128)S(1)}, f32[496,128]{1,0:T(8,128)S(1)}, u32[]{:S(2)}, u32[]{:S(2)}) collective-permute-start(f32[496,128]{1,0:T(8,128)S(1)} %get-tuple-element.25), channel_id=1, source_target_pairs={{0,1},{1,2},{2,3},{3,4},{4,5},{5,6},{6,7},{7,8},{8,9},{9,10},{10,1... | collective-permute-start | bytes 761864 | tf_op jit(solution)/shard_map/last_step/ppermute | solution.py:42
  39.4 11.7 %collective-permute-start.9 = (f32[496,128]{1,0:T(8,128)S(1)}, f32[496,128]{1,0:T(8,128)S(1)}, u32[]{:S(2)}, u32[]{:S(2)}) collective-permute-start(f32[496,128]{1,0:T(8,128)S(1)} %get-tuple-element.27), channel_id=1, source_target_pairs={{0,127},{1,0},{2,1},{3,2},{4,3},{5,4},{6,5},{7,6},{8,7},{9,8},{10,... | collective-permute-start | bytes 761864 | tf_op jit(solution)/shard_map/last_step/ppermute | solution.py:42

commit v5 on v4

--- a/solution.py
+++ b/solution.py
@@ -105,24 +105,35 @@
             top_ref[t, k * SECTION : (k + 1) * SECTION, :] = first
 
 
-def sent_strips_kernel(h_ref, d_ref, f_ref, v_ref, bottom_ref, top_ref, held, sems):
-    copies = []
-    for k, ref in enumerate(field_refs(h_ref, d_ref, f_ref, v_ref)):
-        copies += [
-            pltpu.make_async_copy(ref.at[:, pl.ds(0, 2 * SECTION)], held.at[0, k], sems.at[0, k]),
-            pltpu.make_async_copy(ref.at[:, pl.ds(TS - 2 * SECTION, 2 * SECTION)], held.at[1, k], sems.at[1, k]),
+def sent_strips_kernel(h_ref, d_ref, f_ref, v_ref, bottom_ref, top_ref, held, made, sems, out_sems):
+    starts = (TS - 2 * SECTION, 0)
+    fields = field_refs(h_ref, d_ref, f_ref, v_ref)
+    copies = [
+        [
+            pltpu.make_async_copy(ref.at[:, pl.ds(start, 2 * SECTION)], held.at[side, k], sems.at[side, k])
+            for k, ref in enumerate(fields)
         ]
-    for copy in copies:
+        for side, start in enumerate(starts)
+    ]
+    for copy in copies[0] + copies[1]:
         copy.start()
-    for copy in copies:
+    row = lax.broadcasted_iota(jnp.int32, (SECTION, LANES), 0)
+    results = [pltpu.make_async_copy(made.at[s], ref, out_sems.at[s]) for s, ref in enumerate((bottom_ref, top_ref))]
+    for side in (0, 1):
+        for copy in copies[side]:
+            copy.wait()
+        own = slice(0, SECTION) if side else slice(SECTION, 2 * SECTION)
+        ninth = SECTION if side else SECTION - 1
+        for t in range(TPD):
+            for k in range(6):
+                part = held[side, k, t, own, :]
+                if k in (3, 4):
+                    deepest = row == (SECTION - 1 if side else 0)
+                    part = jnp.where(deepest, held[side, k - 3, t, ninth : ninth + 1, :], part)
+                made[side, t, k * SECTION : (k + 1) * SECTION, :] = part
+        results[side].start()
+    for copy in results:
         copy.wait()
-
-    def ends(k, t, rows):
-        if rows.start < 2 * SECTION:
-            return held[0, k, t, rows, :]
-        return held[1, k, t, rows.start - TS + 2 * SECTION : rows.stop - TS + 2 * SECTION, :]
-
-    put_strips(ends, bottom_ref, top_ref)
 
 
 def own_strips_kernel(h_ref, d_ref, f_ref, v_ref, bottom_ref, top_ref, right_ref, left_ref):
@@ -302,7 +313,7 @@
             beside = jnp.where(group == 2 * TPD - 1, after, beside)
             target[TPD, rows, :] = jnp.where(mask[:HALF], beside, 1.0 if k == 5 else 0.0)
 
-    chunk = 48
+    chunk = 24
     first_row, last_row = TOP - SECTION, TOP + TS + SECTION
 
     def in_tile(ref, j, rows):
@@ -429,10 +440,12 @@
             sent_strips_kernel,
             out_shape=(strips_shape, strips_shape),
             in_specs=[anywhere] * 4,
-            out_specs=(vmem,) * 2,
+            out_specs=(anywhere,) * 2,
             scratch_shapes=[
                 pltpu.VMEM((2, 6, TPD, 2 * SECTION, LANES), f32),
+                pltpu.VMEM((2, TPD, STRIP, LANES), f32),
                 pltpu.SemaphoreType.DMA((2, 6)),
+                pltpu.SemaphoreType.DMA((2,)),
             ],
             compiler_params=pltpu.CompilerParams(vmem_limit_bytes=FIRST_VMEM_LIMIT),
         )(*given)

time: 60.7 us -> 60.7 us (level)
  no operation moved by 1% of the time
where the time goes in v5:
time: 60.7 us; the launch traced here: 60.1 us
  starting transfers between devices  32.3 us (53%)
  Pallas kernels  16.5 us (27%)
  waiting for transfers between devices  10.6 us (17%)
  between operations  0.74 us (1%)
    ppermute x10, starting transfers between devices, cyclic_shift(): lax.ppermute(value, 'ta', [(i, (i + steps) % count) for i in range(count)])  32.3 us
    ppermute x10, waiting for transfers between devices, cyclic_shift(): lax.ppermute(value, 'ta', [(i, (i + steps) % count) for i in range(count)])  10.6 us
    pallas_call x1, Pallas kernels, shards(): pl.pallas_call(sweeps_kernel, out_shape=(jax.ShapeDtypeStruct(velocity_st...  9.34 us
    pallas_call x1, Pallas kernels, shards(): pl.pallas_call(functools.partial(plan_kernel, slots), out_shape=jax.Shape...  2.13 us
    pallas_call x1, Pallas kernels, shards(): pl.pallas_call(route_kernel, out_shape=(pack_shape, jax.ShapeDtypeStruct(...  1.97 us
    pallas_call x1, Pallas kernels, shards(): pl.pallas_call(sent_strips_kernel, out_shape=(strips_shape, strips_shape)...  1.82 us
  transfers between devices with their start and end apart: 10, of which 3 were waited for; matrix products, arithmetic and copies ran while one was open for 0% of the time, Pallas kernels for 6%

profile of v5, /device:TPU:0, one launch (start us, length us, event | category | flops | bytes accessed | tf_op | source)
XLA Modules:
  0.0 60.1 jit_solution(6044504655207211963)
XLA Ops:
  0.6 0.0 copy-start.1
  0.6 0.0 copy-start.3
  0.7 0.0 copy-start
  0.7 0.0 copy-start.2
  0.7 1.8 %sent_strips.1 = (f32[4,48,128]{2,1,0:T(8,128)}, f32[4,48,128]{2,1,0:T(8,128)}) custom-call(f32[4,128,128]{2,1,0:T(8,128)} %h_ref.5, f32[2,4,128,128]{3,2,1,0:T(8,128)} %d_ref.5, f32[4,128,128]{2,1,0:T(8,128)} %f_ref.5, f32[2,4,128,128]{3,2,1,0:T(8,128)} %v_ref.5), custom_call_target="tpu_custom_call" | custom-call | tf_op jit(solution)/shard_map/sent_strips/pallas_call | solution.py:439
  2.5 6.5 %collective-permute-start.3 = (f32[4,48,128]{2,1,0:T(8,128)}, f32[4,48,128]{2,1,0:T(8,128)S(1)}, u32[]{:S(2)}, u32[]{:S(2)}) collective-permute-start(f32[4,48,128]{2,1,0:T(8,128)} %get-tuple-element.20), channel_id=1, source_target_pairs={{0,12},{1,13},{2,14},{3,15},{4,16},{5,17},{6,18},{7,19},{8,20},{9,... | collective-permute-start | bytes 294920 | tf_op jit(solution)/shard_map/strides/ppermute | solution.py:42
  9.0 1.9 %collective-permute-start.2 = (f32[4,48,128]{2,1,0:T(8,128)}, f32[4,48,128]{2,1,0:T(8,128)S(1)}, u32[]{:S(2)}, u32[]{:S(2)}) collective-permute-start(f32[4,48,128]{2,1,0:T(8,128)} %get-tuple-element.20), channel_id=1, source_target_pairs={{0,9},{1,10},{2,11},{3,12},{4,13},{5,14},{6,15},{7,16},{8,17},{9,1... | collective-permute-start | bytes 294920 | tf_op jit(solution)/shard_map/strides/ppermute | solution.py:42
  10.9 1.2 %collective-permute-start.1 = (f32[4,48,128]{2,1,0:T(8,128)}, f32[4,48,128]{2,1,0:T(8,128)S(1)}, u32[]{:S(2)}, u32[]{:S(2)}) collective-permute-start(f32[4,48,128]{2,1,0:T(8,128)} %get-tuple-element.20), channel_id=1, source_target_pairs={{0,6},{1,7},{2,8},{3,9},{4,10},{5,11},{6,12},{7,13},{8,14},{9,15},... | collective-permute-start | bytes 294920 | tf_op jit(solution)/shard_map/strides/ppermute | solution.py:42
  12.1 2.8 %collective-permute-start = (f32[4,48,128]{2,1,0:T(8,128)}, f32[4,48,128]{2,1,0:T(8,128)S(1)}, u32[]{:S(2)}, u32[]{:S(2)}) collective-permute-start(f32[4,48,128]{2,1,0:T(8,128)} %get-tuple-element.20), channel_id=1, source_target_pairs={{0,3},{1,4},{2,5},{3,6},{4,7},{5,8},{6,9},{7,10},{8,11},{9,12},{10... | collective-permute-start | bytes 294920 | tf_op jit(solution)/shard_map/strides/ppermute | solution.py:42
  14.9 0.0 copy-start.4
  14.9 5.6 %collective-permute-start.7 = (f32[4,48,128]{2,1,0:T(8,128)}, f32[4,48,128]{2,1,0:T(8,128)S(1)}, u32[]{:S(2)}, u32[]{:S(2)}) collective-permute-start(f32[4,48,128]{2,1,0:T(8,128)} %get-tuple-element.22), channel_id=1, source_target_pairs={{0,116},{1,117},{2,118},{3,119},{4,120},{5,121},{6,122},{7,123},{8... | collective-permute-start | bytes 294920 | tf_op jit(solution)/shard_map/strides/ppermute | solution.py:42
  20.5 0.0 collective-permute-done.3.refs_4_
  20.6 2.3 %collective-permute-start.6 = (f32[4,48,128]{2,1,0:T(8,128)}, f32[4,48,128]{2,1,0:T(8,128)S(1)}, u32[]{:S(2)}, u32[]{:S(2)}) collective-permute-start(f32[4,48,128]{2,1,0:T(8,128)} %get-tuple-element.22), channel_id=1, source_target_pairs={{0,119},{1,120},{2,121},{3,122},{4,123},{5,124},{6,125},{7,126},{8... | collective-permute-start | bytes 294920 | tf_op jit(solution)/shard_map/strides/ppermute | solution.py:42
  22.8 0.0 collective-permute-done.2.refs_3_
  22.8 3.0 %collective-permute-start.5 = (f32[4,48,128]{2,1,0:T(8,128)}, f32[4,48,128]{2,1,0:T(8,128)S(1)}, u32[]{:S(2)}, u32[]{:S(2)}) collective-permute-start(f32[4,48,128]{2,1,0:T(8,128)} %get-tuple-element.22), channel_id=1, source_target_pairs={{0,122},{1,123},{2,124},{3,125},{4,126},{5,127},{6,0},{7,1},{8,2},... | collective-permute-start | bytes 294920 | tf_op jit(solution)/shard_map/strides/ppermute | solution.py:42
  25.8 0.0 collective-permute-done.1.refs_2_
  25.8 1.5 %collective-permute-start.4 = (f32[4,48,128]{2,1,0:T(8,128)}, f32[4,48,128]{2,1,0:T(8,128)S(1)}, u32[]{:S(2)}, u32[]{:S(2)}) collective-permute-start(f32[4,48,128]{2,1,0:T(8,128)} %get-tuple-element.22), channel_id=1, source_target_pairs={{0,125},{1,126},{2,127},{3,0},{4,1},{5,2},{6,3},{7,4},{8,5},{9,6},... | collective-permute-start | bytes 294920 | tf_op jit(solution)/shard_map/strides/ppermute | solution.py:42
  27.3 0.0 copy-done.1
  27.3 0.0 copy-done.3
  27.3 0.0 copy-done
  27.3 0.0 copy-done.2
  27.3 0.3 own_strips.1
  27.6 0.0 copy-done.4
  27.6 2.1 %plan.1.given_plan = s32[1,128]{1,0:T(1,128)S(1)} custom-call(s32[22]{0:T(128)S(1)} %copy-done.4), custom_call_target="tpu_custom_call" | custom-call | flops 4000000 | bytes 4000000 | tf_op jit(solution)/shard_map/plan/pallas_call | solution.py:464
  29.7 4.4 %collective-permute-done.refs_1_ = f32[4,48,128]{2,1,0:T(8,128)S(1)} collective-permute-done((f32[4,48,128]{2,1,0:T(8,128)}, f32[4,48,128]{2,1,0:T(8,128)S(1)}, u32[]{:S(2)}, u32[]{:S(2)}) %collective-permute-start) | collective-permute-done | bytes 98336 | tf_op jit(solution)/shard_map/strides/ppermute | solution.py:42
  34.1 0.0 collective-permute-done.7.refs_9_
  34.1 0.0 collective-permute-done.6.refs_8_
  34.1 0.0 collective-permute-done.5.refs_7_
  34.1 2.9 %collective-permute-done.4.refs_6_ = f32[4,48,128]{2,1,0:T(8,128)S(1)} collective-permute-done((f32[4,48,128]{2,1,0:T(8,128)}, f32[4,48,128]{2,1,0:T(8,128)S(1)}, u32[]{:S(2)}, u32[]{:S(2)}) %collective-permute-start.4) | collective-permute-done | bytes 98336 | tf_op jit(solution)/shard_map/strides/ppermute | solution.py:42
  37.0 2.0 %route.1 = (f32[496,128]{1,0:T(8,128)S(1)}, f32[432,128]{1,0:T(8,128)S(1)}, f32[496,128]{1,0:T(8,128)S(1)}) custom-call(s32[1,128]{1,0:T(1,128)S(1)} %plan.1.given_plan, f32[4,48,128]{2,1,0:T(8,128)S(1)} %get-tuple-element.19.refs_0_, f32[4,48,128]{2,1,0:T(8,128)S(1)} %collective-permute-done.refs_1_, f32[4,48,128]{2,1,0:T(8,128)S(1)} %collective-permute-done.1.refs_2_, ...), custom_call_target="tpu_custom_call" | custom-call | tf_op jit(solution)/shard_map/route/pallas_call | solution.py:489
  39.0 0.1 collective-permute-start.8
  39.1 7.4 %collective-permute-start.9 = (f32[496,128]{1,0:T(8,128)S(1)}, f32[496,128]{1,0:T(8,128)S(1)}, u32[]{:S(2)}, u32[]{:S(2)}) collective-permute-start(f32[496,128]{1,0:T(8,128)S(1)} %get-tuple-element.27), channel_id=1, source_target_pairs={{0,127},{1,0},{2,1},{3,2},{4,3},{5,4},{6,5},{7,6},{8,7},{9,8},{10,... | collective-permute-start | bytes 761864 | tf_op jit(solution)/shard_map/last_step/ppermute | solution.py:42
  46.5 1.0 %own_fields.1 = (f32[5,160,128]{2,1,0:T(8,128)S(1)}, f32[5,160,128]{2,1,0:T(8,128)S(1)}, f32[5,160,128]{2,1,0:T(8,128)S(1)}, f32[5,160,128]{2,1,0:T(8,128)S(1)},...) custom-call(f32[4,128,128]{2,1,0:T(8,128)S(1)} %copy-done.2, f32[2,4,128,128]{3,2,1,0:T(8,128)S(1)} %copy-done, ...), custom_call_target="tpu_custom_call" | custom-call | flops 4000000 | bytes 4000000 | tf_op jit(solution)/shard_map/own_fields/pallas_call | solution.py:475
  47.5 3.3 %collective-permute-done.8.ahead_ref = f32[496,128]{1,0:T(8,128)S(1)} collective-permute-done((f32[496,128]{1,0:T(8,128)S(1)}, f32[496,128]{1,0:T(8,128)S(1)}, u32[]{:S(2)}, u32[]{:S(2)}) %collective-permute-start.8) | collective-permute-done | bytes 253984 | tf_op jit(solution)/shard_map/last_step/ppermute | solution.py:42
  50.8 0.0 collective-permute-done.9.back_ref
  50.8 9.3 %sweeps.1 = (f32[2,4,128,128]{3,2,1,0:T(8,128)}, f32[4,128,128]{2,1,0:T(8,128)}, f32[5,160,128]{2,1,0:T(8,128)S(1)}, f32[5,160,128]{2,1,0:T(8,128)S(1)}, f32[5,1...) custom-call(s32[1,128]{1,0:T(1,128)S(1)} %plan.1.given_plan, ...), custom_call_target="tpu_custom_call", output_to_operand_aliasing={{2}: (4, {}), {3}: (5, {}), {4}: (6, {}), {5}: (7, {}), {6}... | custom-call | tf_op jit(solution)/shard_map/sweeps/pallas_call | solution.py:504
Async XLA Ops:
  0.6 26.7 %copy-start.1 = (f32[2,4,128,128]{3,2,1,0:T(8,128)S(1)}, f32[2,4,128,128]{3,2,1,0:T(8,128)}, u32[]{:S(2)}) copy-start(f32[2,4,128,128]{3,2,1,0:T(8,128)} %v_ref.5) | copy-start | bytes 1572868
  0.6 26.7 %copy-start.3 = (f32[4,128,128]{2,1,0:T(8,128)S(1)}, f32[4,128,128]{2,1,0:T(8,128)}, u32[]{:S(2)}) copy-start(f32[4,128,128]{2,1,0:T(8,128)} %f_ref.5) | copy-start | bytes 786436
  0.7 26.7 %copy-start = (f32[2,4,128,128]{3,2,1,0:T(8,128)S(1)}, f32[2,4,128,128]{3,2,1,0:T(8,128)}, u32[]{:S(2)}) copy-start(f32[2,4,128,128]{3,2,1,0:T(8,128)} %d_ref.5) | copy-start | bytes 1572868
  0.7 26.7 %copy-start.2 = (f32[4,128,128]{2,1,0:T(8,128)S(1)}, f32[4,128,128]{2,1,0:T(8,128)}, u32[]{:S(2)}) copy-start(f32[4,128,128]{2,1,0:T(8,128)} %h_ref.5) | copy-start | bytes 786436
  2.5 18.1 %collective-permute-start.3 = (f32[4,48,128]{2,1,0:T(8,128)}, f32[4,48,128]{2,1,0:T(8,128)S(1)}, u32[]{:S(2)}, u32[]{:S(2)}) collective-permute-start(f32[4,48,128]{2,1,0:T(8,128)} %get-tuple-element.20), channel_id=1, source_target_pairs={{0,12},{1,13},{2,14},{3,15},{4,16},{5,17},{6,18},{7,19},{8,20},{9,... | collective-permute-start | bytes 294920 | tf_op jit(solution)/shard_map/strides/ppermute | solution.py:42
  9.0 13.9 %collective-permute-start.2 = (f32[4,48,128]{2,1,0:T(8,128)}, f32[4,48,128]{2,1,0:T(8,128)S(1)}, u32[]{:S(2)}, u32[]{:S(2)}) collective-permute-start(f32[4,48,128]{2,1,0:T(8,128)} %get-tuple-element.20), channel_id=1, source_target_pairs={{0,9},{1,10},{2,11},{3,12},{4,13},{5,14},{6,15},{7,16},{8,17},{9,1... | collective-permute-start | bytes 294920 | tf_op jit(solution)/shard_map/strides/ppermute | solution.py:42
  10.9 14.9 %collective-permute-start.1 = (f32[4,48,128]{2,1,0:T(8,128)}, f32[4,48,128]{2,1,0:T(8,128)S(1)}, u32[]{:S(2)}, u32[]{:S(2)}) collective-permute-start(f32[4,48,128]{2,1,0:T(8,128)} %get-tuple-element.20), channel_id=1, source_target_pairs={{0,6},{1,7},{2,8},{3,9},{4,10},{5,11},{6,12},{7,13},{8,14},{9,15},... | collective-permute-start | bytes 294920 | tf_op jit(solution)/shard_map/strides/ppermute | solution.py:42
  12.1 22.0 %collective-permute-start = (f32[4,48,128]{2,1,0:T(8,128)}, f32[4,48,128]{2,1,0:T(8,128)S(1)}, u32[]{:S(2)}, u32[]{:S(2)}) collective-permute-start(f32[4,48,128]{2,1,0:T(8,128)} %get-tuple-element.20), channel_id=1, source_target_pairs={{0,3},{1,4},{2,5},{3,6},{4,7},{5,8},{6,9},{7,10},{8,11},{9,12},{10... | collective-permute-start | bytes 294920 | tf_op jit(solution)/shard_map/strides/ppermute | solution.py:42
  14.9 12.7 %copy-start.4 = (s32[22]{0:T(128)S(1)}, s32[22]{0:T(128)}, u32[]{:S(2)}) copy-start(s32[22]{0:T(128)} %len_ref.1) | copy-start | bytes 268
  14.9 19.2 %collective-permute-start.7 = (f32[4,48,128]{2,1,0:T(8,128)}, f32[4,48,128]{2,1,0:T(8,128)S(1)}, u32[]{:S(2)}, u32[]{:S(2)}) collective-permute-start(f32[4,48,128]{2,1,0:T(8,128)} %get-tuple-element.22), channel_id=1, source_target_pairs={{0,116},{1,117},{2,118},{3,119},{4,120},{5,121},{6,122},{7,123},{8... | collective-permute-start | bytes 294920 | tf_op jit(solution)/shard_map/strides/ppermute | solution.py:42
  20.6 13.6 %collective-permute-start.6 = (f32[4,48,128]{2,1,0:T(8,128)}, f32[4,48,128]{2,1,0:T(8,128)S(1)}, u32[]{:S(2)}, u32[]{:S(2)}) collective-permute-start(f32[4,48,128]{2,1,0:T(8,128)} %get-tuple-element.22), channel_id=1, source_target_pairs={{0,119},{1,120},{2,121},{3,122},{4,123},{5,124},{6,125},{7,126},{8... | collective-permute-start | bytes 294920 | tf_op jit(solution)/shard_map/strides/ppermute | solution.py:42
  22.8 11.3 %collective-permute-start.5 = (f32[4,48,128]{2,1,0:T(8,128)}, f32[4,48,128]{2,1,0:T(8,128)S(1)}, u32[]{:S(2)}, u32[]{:S(2)}) collective-permute-start(f32[4,48,128]{2,1,0:T(8,128)} %get-tuple-element.22), channel_id=1, source_target_pairs={{0,122},{1,123},{2,124},{3,125},{4,126},{5,127},{6,0},{7,1},{8,2},... | collective-permute-start | bytes 294920 | tf_op jit(solution)/shard_map/strides/ppermute | solution.py:42
  25.8 11.2 %collective-permute-start.4 = (f32[4,48,128]{2,1,0:T(8,128)}, f32[4,48,128]{2,1,0:T(8,128)S(1)}, u32[]{:S(2)}, u32[]{:S(2)}) collective-permute-start(f32[4,48,128]{2,1,0:T(8,128)} %get-tuple-element.22), channel_id=1, source_target_pairs={{0,125},{1,126},{2,127},{3,0},{4,1},{5,2},{6,3},{7,4},{8,5},{9,6},... | collective-permute-start | bytes 294920 | tf_op jit(solution)/shard_map/strides/ppermute | solution.py:42
  39.0 11.8 %collective-permute-start.8 = (f32[496,128]{1,0:T(8,128)S(1)}, f32[496,128]{1,0:T(8,128)S(1)}, u32[]{:S(2)}, u32[]{:S(2)}) collective-permute-start(f32[496,128]{1,0:T(8,128)S(1)} %get-tuple-element.25), channel_id=1, source_target_pairs={{0,1},{1,2},{2,3},{3,4},{4,5},{5,6},{6,7},{7,8},{8,9},{9,10},{10,1... | collective-permute-start | bytes 761864 | tf_op jit(solution)/shard_map/last_step/ppermute | solution.py:42
  39.1 11.7 %collective-permute-start.9 = (f32[496,128]{1,0:T(8,128)S(1)}, f32[496,128]{1,0:T(8,128)S(1)}, u32[]{:S(2)}, u32[]{:S(2)}) collective-permute-start(f32[496,128]{1,0:T(8,128)S(1)} %get-tuple-element.27), channel_id=1, source_target_pairs={{0,127},{1,0},{2,1},{3,2},{4,3},{5,4},{6,5},{7,6},{8,7},{9,8},{10,... | collective-permute-start | bytes 761864 | tf_op jit(solution)/shard_map/last_step/ppermute | solution.py:42
